TPU v7x, 256 devices: a whole 4x4x8 slice. The times are simulated.
256 devices in a mesh: dp: 16 (over z, x_hi), mp: 16 (over x_lo, y, core).
Axes of the slice: x: 4 (x_hi: 2, x_lo: 2; x = x_hi * 2 + x_lo), y: 4, z: 8, core: 2. Of those that a mesh axis runs over, the one named last changes fastest.
Arguments:
- image_embed: bfloat16 [32768, 1152], P(('dp', 'mp')), may hold values from -0.176776695 to 0.176776695
- text_embed: bfloat16 [32768, 1152], P(('dp', 'mp')), may hold values from -0.176776695 to 0.176776695
- log_scale: float32 [1], replicated, may hold values from 1.1 to 2.3
- logit_bias: float32 [1], replicated, may hold values from -3 to -1
Outputs:
- loss: float32 [1], replicated
- image_grad: float32 [32768, 1152], P(('dp', 'mp'))
- text_grad: float32 [32768, 1152], P(('dp', 'mp'))
All inputs are finite; a program needn't handle non-finite values.
Results may differ from a plain program's by a relative error of at most 0.0015.
Values may be sent and summed in bfloat16 or wider, within the bound.
No kernel may reach another device: no remote copies, remote signals or barrier semaphores. Data moves between devices by JAX's collectives and lax.ppermute only.
A program may use at most 128 MiB of HBM per device.

v0:
```python
import jax
import jax.numpy as jnp
from jax import lax
from jax.sharding import PartitionSpec as P

STEPS = 2


def shifted(block, axis, distance):
    devices = range(lax.axis_size(axis))
    route = [((i - distance) % len(devices), i) for i in devices]
    return lax.ppermute(block, axis, route)


def unit_rows(raw):
    values = raw.astype(jnp.float32)
    norm = jnp.sqrt(jnp.sum(values * values, axis=1, keepdims=True) + 1e-06)
    unit = values / norm
    return (unit, unit.astype(jnp.bfloat16), norm)


def back_norm(hat, unit, norm):
    return (hat - unit * jnp.sum(unit * hat, axis=1, keepdims=True)) / norm


def pair_terms(logits, positive):
    label = jnp.where(positive, 1.0, -1.0).astype(jnp.float32)
    total = jnp.sum(jax.nn.softplus(-label * logits))
    coef = (-label * jax.nn.sigmoid(-label * logits)).astype(jnp.bfloat16)
    return (total, coef)


def body(image_embed, text_embed, log_scale, logit_bias):
    image_unit, image_low, image_norm = unit_rows(image_embed)
    text_unit, text_low, text_norm = unit_rows(text_embed)
    scale = jnp.exp(log_scale[0])
    bias = logit_bias[0]
    rows = image_low.shape[0]
    width = image_low.shape[1]
    group_size = lax.axis_size("mp")
    group_rows = rows * group_size
    offset = lax.axis_index("mp") * rows
    own_index = offset + lax.iota(jnp.int32, rows)
    total = jnp.zeros((), jnp.float32)
    carried = jnp.zeros((rows, width), jnp.float32)
    text_now = text_low
    image_hat = jnp.zeros((rows, width), jnp.float32)
    for step in range(STEPS):
        if step < STEPS - 1:
            text_next = shifted(text_now, "dp", 1)
        piece = lax.all_gather(text_now, "mp", axis=0, tiled=True)
        sum_now = total
        hat_now = image_hat
        logits = (
            scale
            * lax.dot_general(
                image_low, piece, (((1,), (1,)), ((), ())), preferred_element_type=jnp.float32
            )
            + bias
        )
        columns = lax.iota(jnp.int32, piece.shape[0])
        positive = (own_index[:, None] == columns[None, :]) & (step == 0)
        piece_total, coef = pair_terms(logits, positive)
        hat_now = hat_now + jnp.dot(coef, piece, preferred_element_type=jnp.float32)
        update = lax.dot_general(
            coef, image_low, (((0,), (0,)), ((), ())), preferred_element_type=jnp.float32
        )
        total = sum_now + piece_total
        image_hat = hat_now
        carried = carried + lax.psum_scatter(update, "mp", scatter_dimension=0, tiled=True)
        if step < STEPS - 1:
            carried = shifted(carried, "dp", 1)
            text_now = text_next
    carried = shifted(carried, "dp", 1 - STEPS)
    whole_total = lax.psum(total, ("dp", "mp"))
    pair_count = rows * lax.axis_size("dp") * group_size * STEPS * group_rows
    loss = jnp.reshape(whole_total / pair_count, (1,))
    image_grad = back_norm(scale * image_hat, image_unit, image_norm)
    text_grad = back_norm(scale * carried, text_unit, text_norm)
    return (loss, image_grad, text_grad)


def solution(mesh):
    placed = (P(("dp", "mp"), None), P(("dp", "mp"), None), P(), P())
    return jax.shard_map(
        body,
        mesh=mesh,
        in_specs=placed,
        out_specs=(P(), P(("dp", "mp"), None), P(("dp", "mp"), None)),
        check_vma=False,
    )
```

profile of v0, /device:TPU:1, one launch (start us, length us, event | category | flops | bytes accessed | tf_op | source)
XLA Modules:
  0.0 356.3 jit_solution(7241331829350591480)
XLA Ops:
  7.2 0.0 all-gather.3.cloned.1.call-start
  7.2 1.1 fusion.7
  8.3 1.8 fusion.9
  10.1 0.0 all-gather.3.cloned.1.call-update
  10.2 0.0 all-gather.5.cloned.1.call-start
  10.2 3.7 %collective-permute-start = (bf16[128,1152]{1,0:T(8,128)(2,1)}, bf16[128,1152]{1,0:T(8,128)(2,1)S(1)}, u32[]{:S(2)}, u32[]{:S(2)}) collective-permute-start(bf16[128,1152]{1,0:T(8,128)(2,1)} %fusion.9), channel_id=1, source_target_pairs={{240,0},{0,16},{16,32},{32,48},{48,64},{64,80},{80,96},{96,112},{1... | collective-permute-start | bytes 884744 | tf_op jit(solution)/shard_map/ppermute | solution.py:12
  13.9 12.2 %collective-permute-done = bf16[128,1152]{1,0:T(8,128)(2,1)S(1)} collective-permute-done((bf16[128,1152]{1,0:T(8,128)(2,1)}, bf16[128,1152]{1,0:T(8,128)(2,1)S(1)}, u32[]{:S(2)}, u32[]{:S(2)}) %collective-permute-start) | collective-permute-done | bytes 294944 | tf_op jit(solution)/shard_map/ppermute | solution.py:12
  26.1 0.0 copy-start.2
  26.1 0.7 copy-done.2
  26.8 0.0 all-gather.5.cloned.1.call-update
  26.8 0.0 reduce-scatter.3.cloned.1.call-start
  28.2 1.1 fusion.6
  29.3 26.3 %all-gather.3.cloned.1.call-done = bf16[2048,1152]{1,0:T(8,128)(2,1)} async-done(((bf16[128,1152]{1,0:T(8,128)(2,1)}), bf16[2048,1152]{1,0:T(8,128)(2,1)}) %all-gather.3.cloned.1.call-update) | async-done | bytes 4718608 | tf_op jit(solution)/shard_map/all_gather | solution.py:51
  55.7 0.0 copy-start.1
  55.7 5.1 %fusion.4 = (f32[]{:T(128)}, f32[128,2048]{1,0:T(8,128)S(1)}) fusion(f32[]{:T(128)} %bitcast.7, bf16[2048,1152]{1,0:T(8,128)(2,1)} %all-gather.3.cloned.1.call-done, f32[128]{0:T(128)S(1)} %add_sqrt_fusion.1, bf16[128,1152]{1,0:T(8,128)(2,1)} %param.4, f32[]{:T(128)} %bitcast, s32[128]{0:T(128)S(1)} %iota_add_fusion), kind=kOutput, calls=%fused_computation.9 | convolution fusion | flops 607830016 | bytes 6063116 | tf_op jit(solution)/shard_map/dot_general | solution.py:56
  60.8 0.0 copy-done.1
  60.8 5.3 %fusion.11 = f32[2048,1152]{1,0:T(8,128)} fusion(f32[128,2048]{1,0:T(8,128)S(1)} %get-tuple-element.4, s32[128]{0:T(128)S(1)} %iota_add_fusion, f32[128]{0:T(128)S(1)} %add_sqrt_fusion.1, bf16[128,1152]{1,0:T(8,128)(2,1)S(1)} %copy-done.1), kind=kOutput, calls=%fused_computation.31 | convolution fusion | flops 606519296 | bytes 10781696 | tf_op jit(solution)/shard_map/dot_general | solution.py:65
  66.1 0.0 reduce-scatter.3.cloned.1.call-update
  66.1 0.0 reduce-scatter.5.cloned.1.call-start
  66.1 33.3 %all-gather.5.cloned.1.call-done = bf16[2048,1152]{1,0:T(8,128)(2,1)} async-done(((bf16[128,1152]{1,0:T(8,128)(2,1)}), bf16[2048,1152]{1,0:T(8,128)(2,1)}) %all-gather.5.cloned.1.call-update) | async-done | bytes 4718608 | tf_op jit(solution)/shard_map/all_gather | solution.py:51
  99.5 4.9 %fusion.5 = (f32[]{:T(128)}, f32[128,2048]{1,0:T(8,128)S(1)}) fusion(f32[]{:T(128)} %bitcast.8, bf16[2048,1152]{1,0:T(8,128)(2,1)} %all-gather.5.cloned.1.call-done, f32[128]{0:T(128)S(1)} %add_sqrt_fusion.1, bf16[128,1152]{1,0:T(8,128)(2,1)S(1)} %copy-done.1, f32[]{:T(128)} %bitcast), kind=kOutput, calls=%fused_computation.10 | convolution fusion | flops 606781440 | bytes 6062604 | tf_op jit(solution)/shard_map/dot_general | solution.py:56
  104.3 5.1 %fusion.10 = f32[2048,1152]{1,0:T(8,128)} fusion(f32[128,2048]{1,0:T(8,128)S(1)} %get-tuple-element.6, f32[128]{0:T(128)S(1)} %add_sqrt_fusion.1, bf16[128,1152]{1,0:T(8,128)(2,1)S(1)} %copy-done.1), kind=kOutput, calls=%fused_computation.30 | convolution fusion | flops 605470720 | bytes 10781184 | tf_op jit(solution)/shard_map/dot_general | solution.py:65
  109.4 0.0 reduce-scatter.5.cloned.1.call-update
  109.5 67.9 %reduce-scatter.3.cloned.1.call-done = f32[128,1152]{1,0:T(8,128)} async-done(((f32[2048,1152]{1,0:T(8,128)}), f32[128,1152]{1,0:T(8,128)}) %reduce-scatter.3.cloned.1.call-update) | async-done | bytes 589840 | tf_op jit(solution)/shard_map/reduce_scatter | solution.py:70
  177.4 2.7 collective-permute-start.1
  180.0 4.1 %fusion.12 = f32[128,1152]{1,0:T(8,128)} fusion(bf16[2048,1152]{1,0:T(8,128)(2,1)} %all-gather.3.cloned.1.call-done, f32[128,2048]{1,0:T(8,128)S(1)} %get-tuple-element.4, s32[128]{0:T(128)S(1)} %iota_add_fusion), kind=kOutput, calls=%fused_computation.32 | convolution fusion | flops 606076928 | bytes 6357504 | tf_op jit(solution)/shard_map/dot_general | solution.py:64
  185.5 72.4 %reduce-scatter.5.cloned.1.call-done = f32[128,1152]{1,0:T(8,128)} async-done(((f32[2048,1152]{1,0:T(8,128)}), f32[128,1152]{1,0:T(8,128)}) %reduce-scatter.5.cloned.1.call-update) | async-done | bytes 589840 | tf_op jit(solution)/shard_map/reduce_scatter | solution.py:70
  257.8 0.0 collective-permute-done.1
  257.8 1.1 add.77
  258.9 0.0 copy-start
  258.9 5.2 %collective-permute-start.2 = (f32[128,1152]{1,0:T(8,128)S(1)}, f32[128,1152]{1,0:T(8,128)S(1)}, u32[]{:S(2)}, u32[]{:S(2)}) collective-permute-start(f32[128,1152]{1,0:T(8,128)S(1)} %add.77), channel_id=1, source_target_pairs={{16,0},{32,16},{48,32},{64,48},{80,64},{96,80},{112,96},{128,112},... | collective-permute-start | bytes 1769480 | tf_op jit(solution)/shard_map/ppermute | solution.py:12
  264.1 3.5 multiply_reduce_fusion.1
  267.6 78.1 %psum.7 = f32[]{:T(128)} all-reduce(f32[]{:T(128)S(6)} %add.73), channel_id=1, replica_groups=mesh['dp'=16,'mp'=16] {'dp','mp'}, use_global_device_ids=true, to_apply=%region_4.5 | all-reduce | flops 1 | bytes 8 | tf_op jit(solution)/shard_map/psum | solution.py:75
  346.4 1.0 subtract_divide_fusion.1
  347.4 0.0 collective-permute-done.2
  347.4 0.0 copy-done
  347.4 0.2 multiply_reduce_fusion
  347.6 1.0 subtract_divide_fusion
  (3 shorter events, 0.0 us)
Async XLA Ops:
  7.2 48.5 %all-gather.3.cloned.1.call-start = ((), (), s32[]{:S(2)}) async-start(), calls=%async_computation.2 | async-start | bytes 5013504 | tf_op jit(solution)/shard_map/all_gather | solution.py:51
  10.2 89.3 %all-gather.5.cloned.1.call-start = ((), (), s32[]{:S(2)}) async-start(), calls=%async_computation.3 | async-start | bytes 5013504 | tf_op jit(solution)/shard_map/all_gather | solution.py:51
  10.2 15.9 %collective-permute-start = (bf16[128,1152]{1,0:T(8,128)(2,1)}, bf16[128,1152]{1,0:T(8,128)(2,1)S(1)}, u32[]{:S(2)}, u32[]{:S(2)}) collective-permute-start(bf16[128,1152]{1,0:T(8,128)(2,1)} %fusion.9), channel_id=1, source_target_pairs={{240,0},{0,16},{16,32},{32,48},{48,64},{64,80},{80,96},{96,112},{1... | collective-permute-start | bytes 884744 | tf_op jit(solution)/shard_map/ppermute | solution.py:12
  26.1 0.7 copy-start.2
  26.8 150.5 %reduce-scatter.3.cloned.1.call-start = ((), (), s32[]{:S(2)}) async-start(), calls=%async_computation.4 | async-start | bytes 10027008 | tf_op jit(solution)/shard_map/reduce_scatter | solution.py:70
  55.7 5.1 %copy-start.1 = (bf16[128,1152]{1,0:T(8,128)(2,1)S(1)}, bf16[128,1152]{1,0:T(8,128)(2,1)}, u32[]{:S(2)}) copy-start(bf16[128,1152]{1,0:T(8,128)(2,1)} %param.4) | copy-start | bytes 884740
  66.1 191.7 %reduce-scatter.5.cloned.1.call-start = ((), (), s32[]{:S(2)}) async-start(), calls=%async_computation.5 | async-start | bytes 10027008 | tf_op jit(solution)/shard_map/reduce_scatter | solution.py:70
  177.4 80.4 %collective-permute-start.1 = (f32[128,1152]{1,0:T(8,128)}, f32[128,1152]{1,0:T(8,128)S(1)}, u32[]{:S(2)}, u32[]{:S(2)}) collective-permute-start(f32[128,1152]{1,0:T(8,128)} %reduce-scatter.3.cloned.1.call-done), channel_id=1, source_target_pairs={{240,0},{0,16},{16,32},{32,48},{48,64},{64,80},{80,96},{96,112},{1... | collective-permute-start | bytes 1769480 | tf_op jit(solution)/shard_map/ppermute | solution.py:12
  258.9 88.5 %copy-start = (bf16[128,1152]{1,0:T(8,128)(2,1)S(1)}, bf16[128,1152]{1,0:T(8,128)(2,1)}, u32[]{:S(2)}) copy-start(bf16[128,1152]{1,0:T(8,128)(2,1)} %param.5) | copy-start | bytes 884740
  258.9 88.5 %collective-permute-start.2 = (f32[128,1152]{1,0:T(8,128)S(1)}, f32[128,1152]{1,0:T(8,128)S(1)}, u32[]{:S(2)}, u32[]{:S(2)}) collective-permute-start(f32[128,1152]{1,0:T(8,128)S(1)} %add.77), channel_id=1, source_target_pairs={{16,0},{32,16},{48,32},{64,48},{80,64},{96,80},{112,96},{128,112},... | collective-permute-start | bytes 1769480 | tf_op jit(solution)/shard_map/ppermute | solution.py:12
Sparse Core Ops, SparseCore 0:
  10.4 45.1 all-gather.2
  58.1 41.3 all-gather.4
  102.0 75.2 reduce-scatter.2
  179.8 77.9 reduce-scatter.4
where the time goes:
time: 357 us; the launch traced here: 356 us
  waiting for transfers between devices  212 us (59%)
  blocking collectives  78.1 us (22%)
  matrix products  28 us (8%)
  between operations  18.2 us (5%)
  starting transfers between devices  11.7 us (3%)
  other arithmetic  7.41 us (2%)
    reduce_scatter x2, waiting for transfers between devices, body(): lax.psum_scatter(update, 'mp', scatter_dimension=0, tiled=True)  140 us
    psum x1, blocking collectives, body(): whole_total = lax.psum(total, ('dp', 'mp'))  78.1 us
    all_gather x2, waiting for transfers between devices, body(): piece = lax.all_gather(text_now, 'mp', axis=0, tiled=True)  59.6 us
    ppermute x3, waiting for transfers between devices, shifted(): return lax.ppermute(block, axis, route)  12.2 us
    ppermute x3, starting transfers between devices, shifted(): return lax.ppermute(block, axis, route)  11.5 us
    dot_general x2, matrix products, body(): lax.dot_general(coef, image_low, (((0,), (0,)), ((), ())), preferred_elem...  10.4 us
    dot_general x2, matrix products, body(): lax.dot_general(image_low, piece, (((1,), (1,)), ((), ())), preferred_ele...  10 us
    dot_general x2, matrix products, body(): hat_now = hat_now + jnp.dot(coef, piece, preferred_element_type=jnp.float32)  7.65 us
  transfers between devices with their start and end apart: 7, of which 5 were waited for; matrix products, arithmetic and copies ran while one was open for 8% of the time, Pallas kernels for 0%

commit v1 on v0

v1 whole, which is shorter than its diff:
```python
import jax
import jax.numpy as jnp
from jax import lax
from jax.experimental import pallas as pl
from jax.experimental.pallas import tpu as pltpu
from jax.sharding import Mesh, PartitionSpec as P

STEPS = 2
ROWS = 128
TILE = 256
AXES = ("z", "xh", "xl", "y", "c")
SHAPE = (8, 2, 2, 4, 2)
VMEM_LIMIT = 48 * 1024 * 1024


def low_rows_kernel(image_ref, text_ref, image_low_ref, text_low_ref):
    for raw_ref, low_ref in ((image_ref, image_low_ref), (text_ref, text_low_ref)):
        values = raw_ref[...].astype(jnp.float32)
        norm = jnp.sqrt(jnp.sum(values * values, axis=1, keepdims=True) + 1e-06)
        low_ref[...] = (values / norm).astype(jnp.bfloat16)


def low_rows(image, text):
    shape = jax.ShapeDtypeStruct(image.shape, jnp.bfloat16)
    return pl.pallas_call(low_rows_kernel, out_shape=(shape, shape), name="low_rows")(image, text)


def pair_kernel(scalar_ref, i0, i1, i2, i3, t0, t1, t2, t3, s0, s1, s2, s3,
                ih0, ih1, ih2, ih3, th0, th1, thx, sh0, sh1, shx, loss_ref,
                images, texts, coefs):
    scale = scalar_ref[0]
    bias = scalar_ref[1]
    for n, ref in enumerate((i0, i1, i2, i3)):
        images[pl.ds(n * ROWS, ROWS), :] = ref[...]
    for n, ref in enumerate((s0, s1, s2, s3, t0, t1, t2, t3)):
        texts[pl.ds(n * ROWS, ROWS), :] = ref[...]
    total = jnp.zeros((8, TILE), jnp.float32)
    for tile in range(8 * ROWS // TILE):
        columns = pl.ds(tile * TILE, TILE)
        z = scale * lax.dot_general(
            images[...], texts[columns, :], (((1,), (1,)), ((), ())),
            preferred_element_type=jnp.float32) + bias
        if tile == 4 * ROWS // TILE:
            row = lax.broadcasted_iota(jnp.int32, z.shape, 0)
            column = lax.broadcasted_iota(jnp.int32, z.shape, 1)
            positive = row == column
            positive = positive & (row < ROWS)
            z = jnp.where(positive, -z, z)
        small = jnp.exp(-jnp.abs(z))
        term = jnp.maximum(z, 0.0) + jnp.log1p(small)
        coef = jnp.where(z >= 0.0, 1.0, small) / (1.0 + small)
        if tile == 4 * ROWS // TILE:
            coef = jnp.where(positive, -coef, coef)
        total = total + jnp.sum(term.reshape(-1, 8, TILE), axis=0)
        low = coef.astype(jnp.bfloat16)
        coefs[:, columns] = low
        update = lax.dot_general(
            low, images[...], (((0,), (0,)), ((), ())), preferred_element_type=jnp.float32)
        if tile == 0:
            sh0[...] = update[:ROWS]
            sh1[...] = update[ROWS:]
        elif tile == 1:
            shx[...] = update
        elif tile == 2:
            th0[...] = update[:ROWS]
            th1[...] = update[ROWS:]
        else:
            thx[...] = update
    hat = jnp.dot(coefs[...], texts[...], preferred_element_type=jnp.float32)
    for n, ref in enumerate((ih0, ih1, ih2, ih3)):
        ref[...] = hat[n * ROWS:(n + 1) * ROWS]
    loss_ref[...] = jnp.sum(total.reshape(8, TILE // 128, 128), axis=1)


def pairs(scalars, images, texts, shifted):
    width = images[0].shape[1]
    block = jax.ShapeDtypeStruct((ROWS, width), jnp.float32)
    double = jax.ShapeDtypeStruct((2 * ROWS, width), jnp.float32)
    vmem = pl.BlockSpec(memory_space=pltpu.VMEM)
    return pl.pallas_call(
        pair_kernel,
        out_shape=(block,) * 4 + (block, block, double) * 2 + (jax.ShapeDtypeStruct((8, 128), jnp.float32),),
        in_specs=[pl.BlockSpec(memory_space=pltpu.SMEM)] + [vmem] * 12,
        out_specs=(vmem,) * 11,
        scratch_shapes=[
            pltpu.VMEM((4 * ROWS, width), jnp.bfloat16),
            pltpu.VMEM((8 * ROWS, width), jnp.bfloat16),
            pltpu.VMEM((4 * ROWS, 8 * ROWS), jnp.bfloat16),
        ],
        compiler_params=pltpu.CompilerParams(vmem_limit_bytes=VMEM_LIMIT),
        name="pairs",
    )(scalars, *images, *texts, *shifted)


def flip(block, axis, bit=1):
    size = SHAPE[AXES.index(axis)]
    return lax.ppermute(block, axis, [(i, i ^ bit) for i in range(size)])


def turn(block, distance):
    return lax.ppermute(block, "y", [(i, (i + distance) % 4) for i in range(4)])


def next_group():
    route = []
    for group in range(16):
        for side in range(2):
            route.append((group * 2 + side, ((group + 1) % 16) * 2 + 1 - side))
    return route


def forward(block):
    return lax.ppermute(block, ("z", "xh", "xl"), next_group())


def backward(block):
    return lax.ppermute(block, ("z", "xh", "xl"), [(j, i) for i, j in next_group()])


def narrow(block):
    return (block * 32.0).astype(jnp.float16)


def widen(block):
    return block.astype(jnp.float32) * (1.0 / 32.0)


def back_norm(hat, raw):
    values = raw.astype(jnp.float32)
    norm = jnp.sqrt(jnp.sum(values * values, axis=1, keepdims=True) + 1e-06)
    unit = values / norm
    return (hat - unit * jnp.sum(unit * hat, axis=1, keepdims=True)) / norm


def body(image_embed, text_embed, log_scale, logit_bias):
    scale = jnp.exp(log_scale[0])
    scalars = jnp.stack([scale, logit_bias[0]])
    image_low, text_low = low_rows(image_embed, text_embed)
    s0 = forward(text_low)
    t1 = flip(text_low, "xl")
    images = [image_low] + [turn(image_low, k) for k in (1, 2, 3)]
    t23 = flip(jnp.concatenate([text_low, t1]), "c")
    s1 = flip(s0, "xl")
    s23 = flip(jnp.concatenate([s0, s1]), "c")
    texts = [text_low, t1, t23[:ROWS], t23[ROWS:]]
    shifted = [s0, s1, s23[:ROWS], s23[ROWS:]]
    ih0, ih1, ih2, ih3, th0, th1, thx, sh0, sh1, shx, loss = pairs(scalars, images, texts, shifted)
    own = [turn(narrow(part), -k) for k, part in ((1, ih1), (2, ih2), (3, ih3))]
    sc = flip(shx, "c")
    tc = flip(thx, "c")
    sx = flip(narrow(sh1 + sc[ROWS:]), "xl")
    tx = flip(narrow(th1 + tc[ROWS:]), "xl")
    back = backward(narrow(sh0 + sc[:ROWS] + widen(sx)))
    for axis, bit in (("c", 1), ("xl", 1), ("y", 1), ("y", 2), ("xh", 1), ("z", 1), ("z", 2), ("z", 4)):
        loss = loss + flip(loss, axis, bit)
    count = ROWS * 256 * STEPS * ROWS * 16
    loss = jnp.reshape(jnp.sum(loss) / count, (1,))
    image_hat = ih0 + widen(own[0]) + widen(own[1]) + widen(own[2])
    text_hat = th0 + tc[:ROWS] + widen(tx) + widen(back)
    return loss, back_norm(scale * image_hat, image_embed), back_norm(scale * text_hat, text_embed)


def solution(mesh):
    grid = Mesh(mesh.devices.reshape(SHAPE), AXES)
    rows = P(AXES, None)
    return jax.shard_map(
        body, mesh=grid, in_specs=(rows, rows, P(), P()), out_specs=(P(), rows, rows), check_vma=False)
```

time: 357 us -> 106 us (0.30)
  the two profiles are of different devices: /device:TPU:1 before, /device:TPU:2 now
where the time goes in v1:
time: 106 us
  waiting for transfers between devices  52.7 us (50%)
  starting transfers between devices  29.8 us (28%)
  Pallas kernels  9.46 us (9%)
  other arithmetic  8.87 us (8%)
  between operations  3.94 us (4%)
    ppermute x16, waiting for transfers between devices, flip(): return lax.ppermute(block, axis, [(i, i ^ bit) for i in range(size)])  24.3 us
    ppermute x6, waiting for transfers between devices, turn(): return lax.ppermute(block, 'y', [(i, (i + distance) % 4) for i in range(4)])  14.5 us
    ppermute x16, starting transfers between devices, flip(): return lax.ppermute(block, axis, [(i, i ^ bit) for i in range(size)])  14 us
    ppermute x6, starting transfers between devices, turn(): return lax.ppermute(block, 'y', [(i, (i + distance) % 4) for i in range(4)])  11.6 us
    ppermute x1, waiting for transfers between devices, forward(): return lax.ppermute(block, ('z', 'xh', 'xl'), next_group())  10.7 us
    pallas_call x1, Pallas kernels, pairs(): pl.pallas_call(pair_kernel, out_shape=(block,) * 4 + (block, block, doubl...  7.43 us
    ppermute x1, waiting for transfers between devices, backward(): lax.ppermute(block, ('z', 'xh', 'xl'), [(j, i) for i, j in next_group()])  3.11 us
    convert_element_type x6, other arithmetic, narrow(): return (block * 32.0).astype(jnp.float16)  2.94 us
  transfers between devices with their start and end apart: 24, of which 15 were waited for; matrix products, arithmetic and copies ran while one was open for 6% of the time, Pallas kernels for 0%

profile of v1, /device:TPU:2, one launch (start us, length us, event | category | flops | bytes accessed | tf_op | source)
XLA Modules:
  0.0 105.5 jit_solution(18205527848501322530)
XLA Ops:
  0.6 2.0 %low_rows.1 = (bf16[128,1152]{1,0:T(8,128)(2,1)}, bf16[128,1152]{1,0:T(8,128)(2,1)}) custom-call(bf16[128,1152]{1,0:T(8,128)(2,1)} %image_ref.1, bf16[128,1152]{1,0:T(8,128)(2,1)} %text_ref.1), custom_call_target="tpu_custom_call" | custom-call | tf_op jit(solution)/shard_map/low_rows/pallas_call | solution.py:25
  2.7 1.5 %collective-permute-start.5 = (bf16[128,1152]{1,0:T(8,128)(2,1)}, bf16[128,1152]{1,0:T(8,128)(2,1)S(1)}, u32[]{:S(2)}, u32[]{:S(2)}) collective-permute-start(bf16[128,1152]{1,0:T(8,128)(2,1)} %get-tuple-element.17.t0), channel_id=1, source_target_pairs={{0,24},{8,16},{16,40},{24,32},{32,56},{40,48},{48,72},{56,64},{64,... | collective-permute-start | bytes 884744 | tf_op jit(solution)/shard_map/ppermute | solution.py:113
  4.2 1.8 %collective-permute-start.3 = (bf16[128,1152]{1,0:T(8,128)(2,1)}, bf16[128,1152]{1,0:T(8,128)(2,1)S(1)}, u32[]{:S(2)}, u32[]{:S(2)}) collective-permute-start(bf16[128,1152]{1,0:T(8,128)(2,1)} %get-tuple-element.17.t0), channel_id=1, source_target_pairs={{0,8},{8,0},{1,9},{9,1},{2,10},{10,2},{3,11},{11,3},{4,12},{12,4},... | collective-permute-start | bytes 884744 | tf_op jit(solution)/shard_map/ppermute | solution.py:97
  6.0 10.7 %collective-permute-done.5.s0 = bf16[128,1152]{1,0:T(8,128)(2,1)S(1)} collective-permute-done((bf16[128,1152]{1,0:T(8,128)(2,1)}, bf16[128,1152]{1,0:T(8,128)(2,1)S(1)}, u32[]{:S(2)}, u32[]{:S(2)}) %collective-permute-start.5) | collective-permute-done | bytes 294944 | tf_op jit(solution)/shard_map/ppermute | solution.py:113
  16.7 1.8 %collective-permute-start.6 = (bf16[128,1152]{1,0:T(8,128)(2,1)S(1)}, bf16[128,1152]{1,0:T(8,128)(2,1)S(1)}, u32[]{:S(2)}, u32[]{:S(2)}) collective-permute-start(bf16[128,1152]{1,0:T(8,128)(2,1)S(1)} %collective-permute-done.5.s0), channel_id=1, source_target_pairs={{0,8},{8,0},{1,9},{9,1},{2,10},{10,2},{3,11},{11,3},{4,12},{12,4},... | collective-permute-start | bytes 884744 | tf_op jit(solution)/shard_map/ppermute | solution.py:97
  18.5 1.0 pad_maximum_fusion
  19.5 0.1 collective-permute-start.4
  19.6 1.7 %collective-permute-start = (bf16[128,1152]{1,0:T(8,128)(2,1)S(1)}, bf16[128,1152]{1,0:T(8,128)(2,1)S(1)}, u32[]{:S(2)}, u32[]{:S(2)}) collective-permute-start(bf16[128,1152]{1,0:T(8,128)(2,1)S(1)} %copy-done.1), channel_id=1, source_target_pairs={{0,2},{2,4},{4,6},{6,0},{1,3},{3,5},{5,7},{7,1},{8,10},{10,12},{12... | collective-permute-start | bytes 884744 | tf_op jit(solution)/shard_map/ppermute | solution.py:101
  21.2 2.9 %collective-permute-start.1 = (bf16[128,1152]{1,0:T(8,128)(2,1)S(1)}, bf16[128,1152]{1,0:T(8,128)(2,1)S(1)}, u32[]{:S(2)}, u32[]{:S(2)}) collective-permute-start(bf16[128,1152]{1,0:T(8,128)(2,1)S(1)} %copy-done.1), channel_id=1, source_target_pairs={{0,4},{2,6},{4,0},{6,2},{1,5},{3,7},{5,1},{7,3},{8,12},{10,14},{12... | collective-permute-start | bytes 884744 | tf_op jit(solution)/shard_map/ppermute | solution.py:101
  24.1 1.3 %collective-permute-start.2 = (bf16[128,1152]{1,0:T(8,128)(2,1)S(1)}, bf16[128,1152]{1,0:T(8,128)(2,1)S(1)}, u32[]{:S(2)}, u32[]{:S(2)}) collective-permute-start(bf16[128,1152]{1,0:T(8,128)(2,1)S(1)} %copy-done.1), channel_id=1, source_target_pairs={{0,6},{2,0},{4,2},{6,4},{1,7},{3,1},{5,3},{7,5},{8,14},{10,8},{12,... | collective-permute-start | bytes 884744 | tf_op jit(solution)/shard_map/ppermute | solution.py:101
  27.1 1.9 %collective-permute-done.7 = bf16[256,1152]{1,0:T(8,128)(2,1)S(1)} collective-permute-done((bf16[256,1152]{1,0:T(8,128)(2,1)S(1)}, bf16[256,1152]{1,0:T(8,128)(2,1)S(1)}, u32[]{:S(2)}, u32[]{:S(2)}) %collective-permute-start.7) | collective-permute-done | bytes 589856 | tf_op jit(solution)/shard_map/ppermute | solution.py:97
  29.0 1.2 %collective-permute-done.i1 = bf16[128,1152]{1,0:T(8,128)(2,1)S(1)} collective-permute-done((bf16[128,1152]{1,0:T(8,128)(2,1)S(1)}, bf16[128,1152]{1,0:T(8,128)(2,1)S(1)}, u32[]{:S(2)}, u32[]{:S(2)}) %collective-permute-start) | collective-permute-done | bytes 294944 | tf_op jit(solution)/shard_map/ppermute | solution.py:101
  30.3 7.5 %collective-permute-done.1.i2 = bf16[128,1152]{1,0:T(8,128)(2,1)S(1)} collective-permute-done((bf16[128,1152]{1,0:T(8,128)(2,1)S(1)}, bf16[128,1152]{1,0:T(8,128)(2,1)S(1)}, u32[]{:S(2)}, u32[]{:S(2)}) %collective-permute-start.1) | collective-permute-done | bytes 294944 | tf_op jit(solution)/shard_map/ppermute | solution.py:101
  37.8 7.4 %pairs.1 = (f32[128,1152]{1,0:T(8,128)S(1)}, f32[128,1152]{1,0:T(8,128)S(1)}, f32[128,1152]{1,0:T(8,128)S(1)}, f32[128,1152]{1,0:T(8,128)S(1)}, f32[128,1152]{1,...) custom-call(f32[2]{0:T(128)S(1)} %pad_maximum_fusion.2.scalar_ref, ...), custom_call_target="tpu_custom_call" | custom-call | tf_op jit(solution)/shard_map/pairs/pallas_call | solution.py:80
  45.2 1.2 %collective-permute-done.8 = f32[8,128]{1,0:T(8,128)S(1)} collective-permute-done((f32[8,128]{1,0:T(8,128)S(1)}, f32[8,128]{1,0:T(8,128)S(1)}, u32[]{:S(2)}, u32[]{:S(2)}) %collective-permute-start.8) | collective-permute-done | bytes 4128 | tf_op jit(solution)/shard_map/ppermute | solution.py:97
  46.4 0.2 collective-permute-start.9
  46.6 3.4 %collective-permute-done.9 = f32[8,128]{1,0:T(8,128)S(1)} collective-permute-done((f32[8,128]{1,0:T(8,128)S(1)}, f32[8,128]{1,0:T(8,128)S(1)}, u32[]{:S(2)}, u32[]{:S(2)}) %collective-permute-start.9) | collective-permute-done | bytes 4128 | tf_op jit(solution)/shard_map/ppermute | solution.py:97
  50.0 1.1 %collective-permute-start.10 = (f32[8,128]{1,0:T(8,128)S(1)}, f32[8,128]{1,0:T(8,128)S(1)}, u32[]{:S(2)}, u32[]{:S(2)}) collective-permute-start(f32[8,128]{1,0:T(8,128)S(1)} %add.71), channel_id=1, source_target_pairs={{0,2},{2,0},{4,6},{6,4},{1,3},{3,1},{5,7},{7,5},{8,10},{10,8},{12,... | collective-permute-start | bytes 12296 | tf_op jit(solution)/shard_map/ppermute | solution.py:97
  51.1 0.1 fusion.1
  51.3 2.4 %collective-permute-done.10 = f32[8,128]{1,0:T(8,128)S(1)} collective-permute-done((f32[8,128]{1,0:T(8,128)S(1)}, f32[8,128]{1,0:T(8,128)S(1)}, u32[]{:S(2)}, u32[]{:S(2)}) %collective-permute-start.10) | collective-permute-done | bytes 4128 | tf_op jit(solution)/shard_map/ppermute | solution.py:97
  53.6 2.5 %collective-permute-start.11 = (f32[8,128]{1,0:T(8,128)S(1)}, f32[8,128]{1,0:T(8,128)S(1)}, u32[]{:S(2)}, u32[]{:S(2)}) collective-permute-start(f32[8,128]{1,0:T(8,128)S(1)} %add.72), channel_id=1, source_target_pairs={{0,4},{2,6},{4,0},{6,2},{1,5},{3,7},{5,1},{7,3},{8,12},{10,14},{12... | collective-permute-start | bytes 12296 | tf_op jit(solution)/shard_map/ppermute | solution.py:97
  56.2 2.6 %collective-permute-done.11 = f32[8,128]{1,0:T(8,128)S(1)} collective-permute-done((f32[8,128]{1,0:T(8,128)S(1)}, f32[8,128]{1,0:T(8,128)S(1)}, u32[]{:S(2)}, u32[]{:S(2)}) %collective-permute-start.11) | collective-permute-done | bytes 4128 | tf_op jit(solution)/shard_map/ppermute | solution.py:97
  58.8 0.1 fusion
  59.0 0.5 collective-permute-start.21
  59.5 4.4 %collective-permute-done.12 = f32[8,128]{1,0:T(8,128)S(1)} collective-permute-done((f32[8,128]{1,0:T(8,128)S(1)}, f32[8,128]{1,0:T(8,128)S(1)}, u32[]{:S(2)}, u32[]{:S(2)}) %collective-permute-start.12) | collective-permute-done | bytes 4128 | tf_op jit(solution)/shard_map/ppermute | solution.py:97
  63.9 2.1 %collective-permute-start.16 = (f16[128,1152]{1,0:T(8,128)(2,1)S(1)}, f16[128,1152]{1,0:T(8,128)(2,1)S(1)}, u32[]{:S(2)}, u32[]{:S(2)}) collective-permute-start(f16[128,1152]{1,0:T(8,128)(2,1)S(1)} %multiply_convert_fusion.2), channel_id=1, source_target_pairs={{0,6},{2,0},{4,2},{6,4},{1,7},{3,1},{5,3},{7,5},{8,14},{10,8},{12,... | collective-permute-start | bytes 884744 | tf_op jit(solution)/shard_map/ppermute | solution.py:101
  66.0 1.4 %collective-permute-done.13 = f32[8,128]{1,0:T(8,128)S(1)} collective-permute-done((f32[8,128]{1,0:T(8,128)S(1)}, f32[8,128]{1,0:T(8,128)S(1)}, u32[]{:S(2)}, u32[]{:S(2)}) %collective-permute-start.13) | collective-permute-done | bytes 4128 | tf_op jit(solution)/shard_map/ppermute | solution.py:97
  67.5 0.8 multiply_convert_fusion.1
  68.3 2.5 %collective-permute-start.17 = (f16[128,1152]{1,0:T(8,128)(2,1)}, f16[128,1152]{1,0:T(8,128)(2,1)S(1)}, u32[]{:S(2)}, u32[]{:S(2)}) collective-permute-start(f16[128,1152]{1,0:T(8,128)(2,1)} %multiply_convert_fusion.1), channel_id=1, source_target_pairs={{0,4},{2,6},{4,0},{6,2},{1,5},{3,7},{5,1},{7,3},{8,12},{10,14},{12... | collective-permute-start | bytes 884744 | tf_op jit(solution)/shard_map/ppermute | solution.py:101
  70.8 1.2 %collective-permute-done.14 = f32[8,128]{1,0:T(8,128)S(1)} collective-permute-done((f32[8,128]{1,0:T(8,128)S(1)}, f32[8,128]{1,0:T(8,128)S(1)}, u32[]{:S(2)}, u32[]{:S(2)}) %collective-permute-start.14) | collective-permute-done | bytes 4128 | tf_op jit(solution)/shard_map/ppermute | solution.py:97
  72.0 4.2 %collective-permute-start.15 = (f32[8,128]{1,0:T(8,128)S(1)}, f32[8,128]{1,0:T(8,128)S(1)}, u32[]{:S(2)}, u32[]{:S(2)}) collective-permute-start(f32[8,128]{1,0:T(8,128)S(1)} %add.76), channel_id=1, source_target_pairs={{0,128},{32,160},{64,192},{96,224},{128,0},{160,32},{192,64},{224,... | collective-permute-start | bytes 12296 | tf_op jit(solution)/shard_map/ppermute | solution.py:97
  76.2 0.8 multiply_convert_fusion
  77.0 2.5 %collective-permute-done.15 = f32[8,128]{1,0:T(8,128)S(1)} collective-permute-done((f32[8,128]{1,0:T(8,128)S(1)}, f32[8,128]{1,0:T(8,128)S(1)}, u32[]{:S(2)}, u32[]{:S(2)}) %collective-permute-start.15) | collective-permute-done | bytes 4128 | tf_op jit(solution)/shard_map/ppermute | solution.py:97
  79.5 1.1 %collective-permute-start.18 = (f16[128,1152]{1,0:T(8,128)(2,1)}, f16[128,1152]{1,0:T(8,128)(2,1)S(1)}, u32[]{:S(2)}, u32[]{:S(2)}) collective-permute-start(f16[128,1152]{1,0:T(8,128)(2,1)} %multiply_convert_fusion), channel_id=1, source_target_pairs={{0,2},{2,4},{4,6},{6,0},{1,3},{3,5},{5,7},{7,1},{8,10},{10,12},{12... | collective-permute-start | bytes 884744 | tf_op jit(solution)/shard_map/ppermute | solution.py:101
  80.6 0.6 add_reduce_fusion
  81.9 5.8 %collective-permute-done.18 = f16[128,1152]{1,0:T(8,128)(2,1)S(1)} collective-permute-done((f16[128,1152]{1,0:T(8,128)(2,1)}, f16[128,1152]{1,0:T(8,128)(2,1)S(1)}, u32[]{:S(2)}, u32[]{:S(2)}) %collective-permute-start.18) | collective-permute-done | bytes 294944 | tf_op jit(solution)/shard_map/ppermute | solution.py:101
  87.7 0.4 multiply_reduce_fusion.1
  88.1 0.3 collective-permute-start.22
  88.4 0.6 copy-done.6
  89.1 1.1 %fusion.8 = f16[128,1152]{1,0:T(8,128)(2,1)S(1)} fusion(f32[128,1152]{1,0:T(8,128)S(1)} %copy-done.6, f32[256,1152]{1,0:T(8,128)} %collective-permute-done.19), kind=kLoop, calls=%fused_computation.15 | loop fusion | flops 442368 | bytes 1474560 | tf_op jit(solution)/shard_map/convert_element_type | solution.py:121
  90.2 1.3 %collective-permute-start.20 = (f16[128,1152]{1,0:T(8,128)(2,1)S(1)}, f16[128,1152]{1,0:T(8,128)(2,1)S(1)}, u32[]{:S(2)}, u32[]{:S(2)}) collective-permute-start(f16[128,1152]{1,0:T(8,128)(2,1)S(1)} %fusion.8), channel_id=1, source_target_pairs={{0,8},{8,0},{1,9},{9,1},{2,10},{10,2},{3,11},{11,3},{4,12},{12,4},... | collective-permute-start | bytes 884744 | tf_op jit(solution)/shard_map/ppermute | solution.py:97
  91.5 3.5 %collective-permute-done.22 = f16[128,1152]{1,0:T(8,128)(2,1)S(1)} collective-permute-done((f16[128,1152]{1,0:T(8,128)(2,1)S(1)}, f16[128,1152]{1,0:T(8,128)(2,1)S(1)}, u32[]{:S(2)}, u32[]{:S(2)}) %collective-permute-start.22) | collective-permute-done | bytes 294944 | tf_op jit(solution)/shard_map/ppermute | solution.py:97
  94.9 0.1 fusion.6
  95.1 2.7 %collective-permute-start.23 = (f16[128,1152]{1,0:T(8,128)(2,1)S(1)}, f16[128,1152]{1,0:T(8,128)(2,1)S(1)}, u32[]{:S(2)}, u32[]{:S(2)}) collective-permute-start(f16[128,1152]{1,0:T(8,128)(2,1)S(1)} %fusion.6), channel_id=1, source_target_pairs={{24,0},{16,8},{40,16},{32,24},{56,32},{48,40},{72,48},{64,56},{88,... | collective-permute-start | bytes 884744 | tf_op jit(solution)/shard_map/ppermute | solution.py:117
  97.8 1.1 %subtract_divide_fusion.1 = f32[128,1152]{1,0:T(8,128)} fusion(bf16[128,1152]{1,0:T(8,128)(2,1)S(1)} %copy-done.2, f32[128]{0:T(128)S(1)} %multiply_reduce_fusion.1, f32[128]{0:T(128)S(1)} %add_sqrt_fusion.1, f16[128,1152]{1,0:T(8,128)(2,1)S(1)} %collective-permute-done.18, f16[128,1152]{1,0:T(8,128)(2,1)S(1)} %collective-permute-done.17, ...), kind=kLoop, calls=%fused_computation.24 | loop fusion | flops 2211840 | bytes 2360324 | tf_op jit(solution)/shard_map/div | solution.py:132
  98.9 3.1 %collective-permute-done.23 = f16[128,1152]{1,0:T(8,128)(2,1)S(1)} collective-permute-done((f16[128,1152]{1,0:T(8,128)(2,1)S(1)}, f16[128,1152]{1,0:T(8,128)(2,1)S(1)}, u32[]{:S(2)}, u32[]{:S(2)}) %collective-permute-start.23) | collective-permute-done | bytes 294944 | tf_op jit(solution)/shard_map/ppermute | solution.py:117
  102.0 1.4 %multiply_reduce_fusion = (f32[128]{0:T(128)S(1)}, f32[128,1152]{1,0:T(8,128)S(1)}) fusion(bf16[128,1152]{1,0:T(8,128)(2,1)S(1)} %copy-done.3, f32[128]{0:T(128)S(1)} %add_sqrt_fusion, f16[128,1152]{1,0:T(8,128)(2,1)S(1)} %collective-permute-done.23, f16[128,1152]{1,0:T(8,128)(2,1)S(1)} %collective-permute-done.20, f32[128,1152]{1,0:T(8,128)S(1)} %copy-done.5, ...), kind=kLoop, calls=%fused_computation.23 | loop fusion | flops 1769344 | bytes 2655236 | tf_op jit(solution)/shard_map/reduce_sum | solution.py:132
  103.4 1.0 subtract_divide_fusion
  (45 shorter events, 0.6 us)
Async XLA Ops:
  2.7 16.9 %copy-start.1 = (bf16[128,1152]{1,0:T(8,128)(2,1)S(1)}, bf16[128,1152]{1,0:T(8,128)(2,1)}, u32[]{:S(2)}) copy-start(bf16[128,1152]{1,0:T(8,128)(2,1)} %get-tuple-element.16.i0) | copy-start | bytes 884740
  2.7 14.0 %collective-permute-start.5 = (bf16[128,1152]{1,0:T(8,128)(2,1)}, bf16[128,1152]{1,0:T(8,128)(2,1)S(1)}, u32[]{:S(2)}, u32[]{:S(2)}) collective-permute-start(bf16[128,1152]{1,0:T(8,128)(2,1)} %get-tuple-element.17.t0), channel_id=1, source_target_pairs={{0,24},{8,16},{16,40},{24,32},{32,56},{40,48},{48,72},{56,64},{64,... | collective-permute-start | bytes 884744 | tf_op jit(solution)/shard_map/ppermute | solution.py:113
  4.2 14.3 %collective-permute-start.3 = (bf16[128,1152]{1,0:T(8,128)(2,1)}, bf16[128,1152]{1,0:T(8,128)(2,1)S(1)}, u32[]{:S(2)}, u32[]{:S(2)}) collective-permute-start(bf16[128,1152]{1,0:T(8,128)(2,1)} %get-tuple-element.17.t0), channel_id=1, source_target_pairs={{0,8},{8,0},{1,9},{9,1},{2,10},{10,2},{3,11},{11,3},{4,12},{12,4},... | collective-permute-start | bytes 884744 | tf_op jit(solution)/shard_map/ppermute | solution.py:97
  16.7 10.2 %collective-permute-start.6 = (bf16[128,1152]{1,0:T(8,128)(2,1)S(1)}, bf16[128,1152]{1,0:T(8,128)(2,1)S(1)}, u32[]{:S(2)}, u32[]{:S(2)}) collective-permute-start(bf16[128,1152]{1,0:T(8,128)(2,1)S(1)} %collective-permute-done.5.s0), channel_id=1, source_target_pairs={{0,8},{8,0},{1,9},{9,1},{2,10},{10,2},{3,11},{11,3},{4,12},{12,4},... | collective-permute-start | bytes 884744 | tf_op jit(solution)/shard_map/ppermute | solution.py:97
  19.5 7.6 %collective-permute-start.4 = (bf16[256,1152]{1,0:T(8,128)(2,1)S(1)}, bf16[256,1152]{1,0:T(8,128)(2,1)S(1)}, u32[]{:S(2)}, u32[]{:S(2)}) collective-permute-start(bf16[256,1152]{1,0:T(8,128)(2,1)S(1)} %pad_maximum_fusion), channel_id=1, source_target_pairs={{0,1},{1,0},{2,3},{3,2},{4,5},{5,4},{6,7},{7,6},{8,9},{9,8},{10,11... | collective-permute-start | bytes 1769480 | tf_op jit(solution)/shard_map/ppermute | solution.py:97
  19.6 10.7 %collective-permute-start = (bf16[128,1152]{1,0:T(8,128)(2,1)S(1)}, bf16[128,1152]{1,0:T(8,128)(2,1)S(1)}, u32[]{:S(2)}, u32[]{:S(2)}) collective-permute-start(bf16[128,1152]{1,0:T(8,128)(2,1)S(1)} %copy-done.1), channel_id=1, source_target_pairs={{0,2},{2,4},{4,6},{6,0},{1,3},{3,5},{5,7},{7,1},{8,10},{10,12},{12... | collective-permute-start | bytes 884744 | tf_op jit(solution)/shard_map/ppermute | solution.py:101
  21.2 16.5 %collective-permute-start.1 = (bf16[128,1152]{1,0:T(8,128)(2,1)S(1)}, bf16[128,1152]{1,0:T(8,128)(2,1)S(1)}, u32[]{:S(2)}, u32[]{:S(2)}) collective-permute-start(bf16[128,1152]{1,0:T(8,128)(2,1)S(1)} %copy-done.1), channel_id=1, source_target_pairs={{0,4},{2,6},{4,0},{6,2},{1,5},{3,7},{5,1},{7,3},{8,12},{10,14},{12... | collective-permute-start | bytes 884744 | tf_op jit(solution)/shard_map/ppermute | solution.py:101
  24.1 13.6 %collective-permute-start.2 = (bf16[128,1152]{1,0:T(8,128)(2,1)S(1)}, bf16[128,1152]{1,0:T(8,128)(2,1)S(1)}, u32[]{:S(2)}, u32[]{:S(2)}) collective-permute-start(bf16[128,1152]{1,0:T(8,128)(2,1)S(1)} %copy-done.1), channel_id=1, source_target_pairs={{0,6},{2,0},{4,2},{6,4},{1,7},{3,1},{5,3},{7,5},{8,14},{10,8},{12,... | collective-permute-start | bytes 884744 | tf_op jit(solution)/shard_map/ppermute | solution.py:101
  26.9 2.1 %collective-permute-start.7 = (bf16[256,1152]{1,0:T(8,128)(2,1)S(1)}, bf16[256,1152]{1,0:T(8,128)(2,1)S(1)}, u32[]{:S(2)}, u32[]{:S(2)}) collective-permute-start(bf16[256,1152]{1,0:T(8,128)(2,1)S(1)} %pad_maximum_fusion.1), channel_id=1, source_target_pairs={{0,1},{1,0},{2,3},{3,2},{4,5},{5,4},{6,7},{7,6},{8,9},{9,8},{10,11... | collective-permute-start | bytes 1769480 | tf_op jit(solution)/shard_map/ppermute | solution.py:97
  27.1 10.7 %copy-start = (bf16[128,1152]{1,0:T(8,128)(2,1)S(1)}, bf16[128,1152]{1,0:T(8,128)(2,1)}, u32[]{:S(2)}) copy-start(bf16[128,1152]{1,0:T(8,128)(2,1)} %get-tuple-element.17.t0) | copy-start | bytes 884740
  37.8 13.3 %copy-start.3 = (bf16[128,1152]{1,0:T(8,128)(2,1)S(1)}, bf16[128,1152]{1,0:T(8,128)(2,1)}, u32[]{:S(2)}) copy-start(bf16[128,1152]{1,0:T(8,128)(2,1)} %text_ref.1) | copy-start | bytes 884740
  37.8 21.0 %copy-start.2 = (bf16[128,1152]{1,0:T(8,128)(2,1)S(1)}, bf16[128,1152]{1,0:T(8,128)(2,1)}, u32[]{:S(2)}) copy-start(bf16[128,1152]{1,0:T(8,128)(2,1)} %image_ref.1) | copy-start | bytes 884740
  45.2 1.2 %collective-permute-start.8 = (f32[8,128]{1,0:T(8,128)S(1)}, f32[8,128]{1,0:T(8,128)S(1)}, u32[]{:S(2)}, u32[]{:S(2)}) collective-permute-start(f32[8,128]{1,0:T(8,128)S(1)} %get-tuple-element.18), channel_id=1, source_target_pairs={{0,1},{1,0},{2,3},{3,2},{4,5},{5,4},{6,7},{7,6},{8,9},{9,8},{10,11... | collective-permute-start | bytes 12296 | tf_op jit(solution)/shard_map/ppermute | solution.py:97
  46.4 3.6 %collective-permute-start.9 = (f32[8,128]{1,0:T(8,128)S(1)}, f32[8,128]{1,0:T(8,128)S(1)}, u32[]{:S(2)}, u32[]{:S(2)}) collective-permute-start(f32[8,128]{1,0:T(8,128)S(1)} %add.70), channel_id=1, source_target_pairs={{0,8},{8,0},{1,9},{9,1},{2,10},{10,2},{3,11},{11,3},{4,12},{12,4},... | collective-permute-start | bytes 12296 | tf_op jit(solution)/shard_map/ppermute | solution.py:97
  50.0 3.6 %collective-permute-start.10 = (f32[8,128]{1,0:T(8,128)S(1)}, f32[8,128]{1,0:T(8,128)S(1)}, u32[]{:S(2)}, u32[]{:S(2)}) collective-permute-start(f32[8,128]{1,0:T(8,128)S(1)} %add.71), channel_id=1, source_target_pairs={{0,2},{2,0},{4,6},{6,4},{1,3},{3,1},{5,7},{7,5},{8,10},{10,8},{12,... | collective-permute-start | bytes 12296 | tf_op jit(solution)/shard_map/ppermute | solution.py:97
  53.6 5.1 %collective-permute-start.11 = (f32[8,128]{1,0:T(8,128)S(1)}, f32[8,128]{1,0:T(8,128)S(1)}, u32[]{:S(2)}, u32[]{:S(2)}) collective-permute-start(f32[8,128]{1,0:T(8,128)S(1)} %add.72), channel_id=1, source_target_pairs={{0,4},{2,6},{4,0},{6,2},{1,5},{3,7},{5,1},{7,3},{8,12},{10,14},{12... | collective-permute-start | bytes 12296 | tf_op jit(solution)/shard_map/ppermute | solution.py:97
  58.7 5.1 %collective-permute-start.12 = (f32[8,128]{1,0:T(8,128)S(1)}, f32[8,128]{1,0:T(8,128)S(1)}, u32[]{:S(2)}, u32[]{:S(2)}) collective-permute-start(f32[8,128]{1,0:T(8,128)S(1)} %add.73), channel_id=1, source_target_pairs={{0,16},{16,0},{1,17},{17,1},{2,18},{18,2},{3,19},{19,3},{4,20},{20... | collective-permute-start | bytes 12296 | tf_op jit(solution)/shard_map/ppermute | solution.py:97
  58.9 29.6 %collective-permute-start.19 = (f32[256,1152]{1,0:T(8,128)}, f32[256,1152]{1,0:T(8,128)}, u32[]{:S(2)}, u32[]{:S(2)}) collective-permute-start(f32[256,1152]{1,0:T(8,128)} %get-tuple-element.24), channel_id=1, source_target_pairs={{0,1},{1,0},{2,3},{3,2},{4,5},{5,4},{6,7},{7,6},{8,9},{9,8},{10,11... | collective-permute-start | bytes 3538952 | tf_op jit(solution)/shard_map/ppermute | solution.py:97
  59.0 29.0 %collective-permute-start.21 = (f32[256,1152]{1,0:T(8,128)}, f32[256,1152]{1,0:T(8,128)S(1)}, u32[]{:S(2)}, u32[]{:S(2)}) collective-permute-start(f32[256,1152]{1,0:T(8,128)} %get-tuple-element.27), channel_id=1, source_target_pairs={{0,1},{1,0},{2,3},{3,2},{4,5},{5,4},{6,7},{7,6},{8,9},{9,8},{10,11... | collective-permute-start | bytes 3538952 | tf_op jit(solution)/shard_map/ppermute | solution.py:97
  63.9 3.6 %collective-permute-start.13 = (f32[8,128]{1,0:T(8,128)S(1)}, f32[8,128]{1,0:T(8,128)S(1)}, u32[]{:S(2)}, u32[]{:S(2)}) collective-permute-start(f32[8,128]{1,0:T(8,128)S(1)} %add.74), channel_id=1, source_target_pairs={{0,32},{32,0},{64,96},{96,64},{128,160},{160,128},{192,224},{224,1... | collective-permute-start | bytes 12296 | tf_op jit(solution)/shard_map/ppermute | solution.py:97
  63.9 17.9 %collective-permute-start.16 = (f16[128,1152]{1,0:T(8,128)(2,1)S(1)}, f16[128,1152]{1,0:T(8,128)(2,1)S(1)}, u32[]{:S(2)}, u32[]{:S(2)}) collective-permute-start(f16[128,1152]{1,0:T(8,128)(2,1)S(1)} %multiply_convert_fusion.2), channel_id=1, source_target_pairs={{0,6},{2,0},{4,2},{6,4},{1,7},{3,1},{5,3},{7,5},{8,14},{10,8},{12,... | collective-permute-start | bytes 884744 | tf_op jit(solution)/shard_map/ppermute | solution.py:101
  67.5 4.5 %collective-permute-start.14 = (f32[8,128]{1,0:T(8,128)S(1)}, f32[8,128]{1,0:T(8,128)S(1)}, u32[]{:S(2)}, u32[]{:S(2)}) collective-permute-start(f32[8,128]{1,0:T(8,128)S(1)} %add.75), channel_id=1, source_target_pairs={{0,64},{32,96},{64,0},{96,32},{128,192},{160,224},{192,128},{224,1... | collective-permute-start | bytes 12296 | tf_op jit(solution)/shard_map/ppermute | solution.py:97
  68.3 13.6 %collective-permute-start.17 = (f16[128,1152]{1,0:T(8,128)(2,1)}, f16[128,1152]{1,0:T(8,128)(2,1)S(1)}, u32[]{:S(2)}, u32[]{:S(2)}) collective-permute-start(f16[128,1152]{1,0:T(8,128)(2,1)} %multiply_convert_fusion.1), channel_id=1, source_target_pairs={{0,4},{2,6},{4,0},{6,2},{1,5},{3,7},{5,1},{7,3},{8,12},{10,14},{12... | collective-permute-start | bytes 884744 | tf_op jit(solution)/shard_map/ppermute | solution.py:101
  72.0 7.5 %collective-permute-start.15 = (f32[8,128]{1,0:T(8,128)S(1)}, f32[8,128]{1,0:T(8,128)S(1)}, u32[]{:S(2)}, u32[]{:S(2)}) collective-permute-start(f32[8,128]{1,0:T(8,128)S(1)} %add.76), channel_id=1, source_target_pairs={{0,128},{32,160},{64,192},{96,224},{128,0},{160,32},{192,64},{224,... | collective-permute-start | bytes 12296 | tf_op jit(solution)/shard_map/ppermute | solution.py:97
  79.5 8.1 %collective-permute-start.18 = (f16[128,1152]{1,0:T(8,128)(2,1)}, f16[128,1152]{1,0:T(8,128)(2,1)S(1)}, u32[]{:S(2)}, u32[]{:S(2)}) collective-permute-start(f16[128,1152]{1,0:T(8,128)(2,1)} %multiply_convert_fusion), channel_id=1, source_target_pairs={{0,2},{2,4},{4,6},{6,0},{1,3},{3,5},{5,7},{7,1},{8,10},{10,12},{12... | collective-permute-start | bytes 884744 | tf_op jit(solution)/shard_map/ppermute | solution.py:101
  81.9 6.2 %copy-start.7 = (f32[128,1152]{1,0:T(8,128)S(1)}, f32[128,1152]{1,0:T(8,128)}, u32[]{:S(2)}) copy-start(f32[128,1152]{1,0:T(8,128)} %get-tuple-element.28) | copy-start | bytes 1769476
  88.0 1.1 %copy-start.6 = (f32[128,1152]{1,0:T(8,128)S(1)}, f32[128,1152]{1,0:T(8,128)}, u32[]{:S(2)}) copy-start(f32[128,1152]{1,0:T(8,128)} %get-tuple-element.25) | copy-start | bytes 1769476
  88.0 6.9 %copy-start.4 = (f32[128,1152]{1,0:T(8,128)S(1)}, f32[128,1152]{1,0:T(8,128)}, u32[]{:S(2)}) copy-start(f32[128,1152]{1,0:T(8,128)} %get-tuple-element.26) | copy-start | bytes 1769476
  88.1 6.8 %collective-permute-start.22 = (f16[128,1152]{1,0:T(8,128)(2,1)S(1)}, f16[128,1152]{1,0:T(8,128)(2,1)S(1)}, u32[]{:S(2)}, u32[]{:S(2)}) collective-permute-start(f16[128,1152]{1,0:T(8,128)(2,1)S(1)} %fusion.3), channel_id=1, source_target_pairs={{0,8},{8,0},{1,9},{9,1},{2,10},{10,2},{3,11},{11,3},{4,12},{12,4},... | collective-permute-start | bytes 884744 | tf_op jit(solution)/shard_map/ppermute | solution.py:97
  90.2 8.7 %collective-permute-start.20 = (f16[128,1152]{1,0:T(8,128)(2,1)S(1)}, f16[128,1152]{1,0:T(8,128)(2,1)S(1)}, u32[]{:S(2)}, u32[]{:S(2)}) collective-permute-start(f16[128,1152]{1,0:T(8,128)(2,1)S(1)} %fusion.8), channel_id=1, source_target_pairs={{0,8},{8,0},{1,9},{9,1},{2,10},{10,2},{3,11},{11,3},{4,12},{12,4},... | collective-permute-start | bytes 884744 | tf_op jit(solution)/shard_map/ppermute | solution.py:97
  95.1 6.9 %copy-start.5 = (f32[128,1152]{1,0:T(8,128)S(1)}, f32[128,1152]{1,0:T(8,128)}, u32[]{:S(2)}) copy-start(f32[128,1152]{1,0:T(8,128)} %get-tuple-element.23) | copy-start | bytes 1769476
  95.1 6.9 %collective-permute-start.23 = (f16[128,1152]{1,0:T(8,128)(2,1)S(1)}, f16[128,1152]{1,0:T(8,128)(2,1)S(1)}, u32[]{:S(2)}, u32[]{:S(2)}) collective-permute-start(f16[128,1152]{1,0:T(8,128)(2,1)S(1)} %fusion.6), channel_id=1, source_target_pairs={{24,0},{16,8},{40,16},{32,24},{56,32},{48,40},{72,48},{64,56},{88,... | collective-permute-start | bytes 884744 | tf_op jit(solution)/shard_map/ppermute | solution.py:117

commit v2 on v1

v2 whole, which is shorter than its diff:
```python
import jax
import jax.numpy as jnp
from jax import lax
from jax.experimental import pallas as pl
from jax.experimental.pallas import tpu as pltpu
from jax.sharding import Mesh, PartitionSpec as P

STEPS = 2
ROWS = 128
TILE = 256
AXES = ("z", "xh", "xl", "y", "c")
SHAPE = (8, 2, 2, 4, 2)
VMEM_LIMIT = 28 * 1024 * 1024
VMEM = pl.BlockSpec(memory_space=pltpu.VMEM)
PARAMS = pltpu.CompilerParams(vmem_limit_bytes=VMEM_LIMIT)


def low_rows_kernel(image_ref, text_ref, image_low_ref, text_low_ref):
    for raw_ref, low_ref in ((text_ref, text_low_ref), (image_ref, image_low_ref)):
        values = raw_ref[...].astype(jnp.float32)
        norm = jnp.sqrt(jnp.sum(values * values, axis=1, keepdims=True) + 1e-06)
        low_ref[...] = (values / norm).astype(jnp.bfloat16)


def low_rows(image, text):
    shape = jax.ShapeDtypeStruct(image.shape, jnp.bfloat16)
    return pl.pallas_call(low_rows_kernel, out_shape=(shape, shape), name="low_rows")(image, text)


def score_kernel(scalar_ref, i0, i1, i2, i3, t0, t1, s0, s1, tx, sx, images, texts, coefs, loss_ref):
    scale = scalar_ref[0]
    bias = scalar_ref[1]
    for n, ref in enumerate((i0, i1, i2, i3)):
        images[pl.ds(n * ROWS, ROWS), :] = ref[...]
    for n, ref in enumerate((t0, t1, s0, s1)):
        texts[pl.ds(n * ROWS, ROWS), :] = ref[...]
    texts[pl.ds(4 * ROWS, 3 * ROWS), :] = tx[...]
    texts[pl.ds(7 * ROWS, ROWS), :] = sx[...]
    total = jnp.zeros((8, TILE), jnp.float32)
    for tile in range(8 * ROWS // TILE):
        columns = pl.ds(tile * TILE, TILE)
        z = scale * lax.dot_general(
            images[...], texts[columns, :], (((1,), (1,)), ((), ())),
            preferred_element_type=jnp.float32) + bias
        if tile == 0:
            row = lax.broadcasted_iota(jnp.int32, z.shape, 0)
            column = lax.broadcasted_iota(jnp.int32, z.shape, 1)
            positive = (row == column) & (row < ROWS)
            z = jnp.where(positive, -z, z)
        small = jnp.exp(-jnp.abs(z))
        term = jnp.maximum(z, 0.0) + jnp.log1p(small)
        coef = jnp.where(z >= 0.0, 1.0, small) / (1.0 + small)
        if tile == 0:
            coef = jnp.where(positive, -coef, coef)
        total = total + jnp.sum(term.reshape(-1, 8, TILE), axis=0)
        coefs[:, columns] = coef.astype(jnp.bfloat16)
    loss_ref[...] = total[:, :128] + total[:, 128:]


def score(scalars, *blocks):
    width = blocks[0].shape[1]
    return pl.pallas_call(
        score_kernel,
        out_shape=(
            jax.ShapeDtypeStruct((4 * ROWS, width), jnp.bfloat16),
            jax.ShapeDtypeStruct((8 * ROWS, width), jnp.bfloat16),
            jax.ShapeDtypeStruct((4 * ROWS, 8 * ROWS), jnp.bfloat16),
            jax.ShapeDtypeStruct((8, 128), jnp.float32),
        ),
        in_specs=[pl.BlockSpec(memory_space=pltpu.SMEM)] + [VMEM] * len(blocks),
        out_specs=(VMEM,) * 4,
        compiler_params=PARAMS,
        name="score",
    )(scalars, *blocks)


def text_sums_kernel(coefs, images, t0, t1, s0, s1, others):
    for tile, refs in enumerate(((t0, t1), (s0, s1))):
        update = lax.dot_general(
            coefs[:, tile * TILE:(tile + 1) * TILE], images[...], (((0,), (0,)), ((), ())),
            preferred_element_type=jnp.float32)
        refs[0][...] = update[:ROWS]
        refs[1][...] = update[ROWS:]
    for tile in range(2):
        others[pl.ds(tile * TILE, TILE), :] = lax.dot_general(
            coefs[:, (tile + 2) * TILE:(tile + 3) * TILE], images[...], (((0,), (0,)), ((), ())),
            preferred_element_type=jnp.float32)


def text_sums(coefs, images):
    width = images.shape[1]
    block = jax.ShapeDtypeStruct((ROWS, width), jnp.float32)
    return pl.pallas_call(
        text_sums_kernel,
        out_shape=(block,) * 4 + (jax.ShapeDtypeStruct((4 * ROWS, width), jnp.float32),),
        in_specs=[VMEM] * 2, out_specs=(VMEM,) * 5, compiler_params=PARAMS, name="text_sums",
    )(coefs, images)


def image_sums_kernel(coefs, texts, *outs):
    for half in range(2):
        hat = jnp.dot(coefs[pl.ds(half * TILE, TILE), :], texts[...], preferred_element_type=jnp.float32)
        outs[2 * half][...] = hat[:ROWS]
        outs[2 * half + 1][...] = hat[ROWS:]


def image_sums(coefs, texts):
    block = jax.ShapeDtypeStruct((ROWS, texts.shape[1]), jnp.float32)
    return pl.pallas_call(
        image_sums_kernel, out_shape=(block,) * 4,
        in_specs=[VMEM] * 2, out_specs=(VMEM,) * 4, compiler_params=PARAMS, name="image_sums",
    )(coefs, texts)


def flip(block, axis, bit=1):
    size = SHAPE[AXES.index(axis)]
    return lax.ppermute(block, axis, [(i, i ^ bit) for i in range(size)])


def turn(block, distance):
    return lax.ppermute(block, "y", [(i, (i + distance) % 4) for i in range(4)])


def swap(route):
    return [(j, i) for i, j in route]


def next_group():
    return [
        (group * 2 + side, ((group + 1) % 16) * 2 + 1 - side) for group in range(16) for side in range(2)]


def forward(block):
    return lax.ppermute(block, ("z", "xh", "xl"), next_group())


def backward(block):
    return lax.ppermute(block, ("z", "xh", "xl"), swap(next_group()))


def far_text():
    route = [((a * 4 + y) * 2, (b * 4 + y) * 2) for a, b in next_group() for y in range(4)]
    route += [((a * 4 + y) * 2 + 1, ((a ^ 1) * 4 + y) * 2 + 1) for a in range(32) for y in range(4)]
    return route


def far_image():
    return [(y * 2, (y + 1) % 4 * 2) for y in range(4)] + [(y * 2 + 1, (y + 3) % 4 * 2 + 1) for y in range(4)]


def narrow(block):
    return (block * 32.0).astype(jnp.float16)


def widen(block):
    return block.astype(jnp.float32) * (1.0 / 32.0)


def back_norm(hat, raw):
    values = raw.astype(jnp.float32)
    norm = jnp.sqrt(jnp.sum(values * values, axis=1, keepdims=True) + 1e-06)
    unit = values / norm
    return (hat - unit * jnp.sum(unit * hat, axis=1, keepdims=True)) / norm


def together(*arrays):
    return lax.optimization_barrier(arrays)


def spread(loss, axes, routes):
    return loss + sum(lax.ppermute(loss, axes, route) for route in routes)


def body(image_embed, text_embed, log_scale, logit_bias):
    scale = jnp.exp(log_scale[0])
    scalars = jnp.stack([scale, logit_bias[0]])
    first = lax.axis_index("c") == 0
    i0, t0 = low_rows(image_embed, text_embed)

    s0, t1, ia, ib = together(forward(t0), flip(t0, "xl"), turn(i0, 1), turn(i0, -1))

    s1 = lax.ppermute(jnp.where(first, t1, s0), ("z", "xh", "xl", "y", "c"), far_text())
    i2 = lax.ppermute(jnp.where(first, ia, ib), ("y", "c"), far_image())
    tx = flip(jnp.concatenate([t0, t1, s0]), "c")
    s1, i2, tx = together(s1, i2, tx)
    sx = flip(s1, "c")

    images, texts, coefs, loss = score(scalars, i0, ia, ib, i2, t0, t1, s0, s1, tx, sx)

    ht0, ht1, hs0, hs1, others = text_sums(coefs, images)
    loss = loss + flip(loss, "c")
    others, loss = together(narrow(others), loss)
    other = flip(others, "c")
    hi0, hia, hib, hi2 = image_sums(coefs, texts)
    loss = loss + flip(loss, "xl")
    other, loss, hi2 = together(other, loss, hi2)
    ht0, ht1, hs0, hs1 = [
        own + widen(other[n * ROWS:(n + 1) * ROWS]) for n, own in enumerate((ht0, ht1, hs0, hs1))]

    r2 = lax.ppermute(narrow(hi2), ("y", "c"), swap(far_image()))
    rs = lax.ppermute(narrow(hs1), ("z", "xh", "xl", "y", "c"), swap(far_text()))
    loss = spread(loss, "y", [[(i, (i + k) % 4) for i in range(4)] for k in (1, 2, 3)])
    r2, rs, loss = together(r2, rs, loss)
    r2, rs = widen(r2), widen(rs)
    hia = hia + jnp.where(first, r2, 0.0)
    hib = hib + jnp.where(first, 0.0, r2)
    ht1 = ht1 + jnp.where(first, rs, 0.0)
    hs0 = hs0 + jnp.where(first, 0.0, rs)

    loss = spread(loss, ("z", "xh"), [[(i, i ^ k) for i in range(16)] for k in (1, 2, 3)])
    back = (backward(narrow(hs0)), flip(narrow(ht1), "xl"), turn(narrow(hia), -1), turn(narrow(hib), 1))
    back, loss = together(back, loss)
    text_hat = ht0 + widen(back[0]) + widen(back[1])
    image_hat = hi0 + widen(back[2]) + widen(back[3])
    loss = spread(loss, "z", [[(i, i ^ k) for i in range(8)] for k in (2, 4, 6)])
    count = ROWS * 256 * STEPS * ROWS * 16
    loss = jnp.reshape(jnp.sum(loss) / count, (1,))
    return loss, back_norm(scale * image_hat, image_embed), back_norm(scale * text_hat, text_embed)


def solution(mesh):
    grid = Mesh(mesh.devices.reshape(SHAPE), AXES)
    rows = P(AXES, None)
    return jax.shard_map(
        body, mesh=grid, in_specs=(rows, rows, P(), P()), out_specs=(P(), rows, rows), check_vma=False)
```

time: 106 us -> 86.3 us (0.81)
  the two profiles are of different devices: /device:TPU:2 before, /device:TPU:64 now
where the time goes in v2:
time: 86.3 us; the launch traced here: 86.1 us
  starting transfers between devices  36.7 us (43%)
  waiting for transfers between devices  31.2 us (36%)
  Pallas kernels  8.57 us (10%)
  other arithmetic  5.23 us (6%)
  between operations  3.89 us (5%)
    ppermute x9, starting transfers between devices, spread(): return loss + sum((lax.ppermute(loss, axes, route) for route in routes))  18.9 us
    ppermute x1, waiting for transfers between devices, body(): lax.ppermute(narrow(hs1), ('z', 'xh', 'xl', 'y', 'c'), swap(far_text()))  5.65 us
    ppermute x9, waiting for transfers between devices, spread(): return loss + sum((lax.ppermute(loss, axes, route) for route in routes))  5.38 us
    ppermute x4, starting transfers between devices, turn(): return lax.ppermute(block, 'y', [(i, (i + distance) % 4) for i in range(4)])  5.34 us
    ppermute x1, waiting for transfers between devices, forward(): return lax.ppermute(block, ('z', 'xh', 'xl'), next_group())  4.84 us
    ppermute x1, waiting for transfers between devices, body(): lax.ppermute(jnp.where(first, t1, s0), ('z', 'xh', 'xl', 'y', 'c'), far_t...  4.7 us
    ppermute x4, waiting for transfers between devices, turn(): return lax.ppermute(block, 'y', [(i, (i + distance) % 4) for i in range(4)])  3.6 us
    pallas_call x1, Pallas kernels, score(): pl.pallas_call(score_kernel, out_shape=(jax.ShapeDtypeStruct((4 * ROWS, w...  3.44 us
  transfers between devices with their start and end apart: 26, of which 16 were waited for; matrix products, arithmetic and copies ran while one was open for 4% of the time, Pallas kernels for 4%

profile of v2, /device:TPU:64, one launch (start us, length us, event | category | flops | bytes accessed | tf_op | source)
XLA Modules:
  0.0 86.1 jit_solution(3631857686489025094)
XLA Ops:
  0.6 2.0 %low_rows.1 = (bf16[128,1152]{1,0:T(8,128)(2,1)}, bf16[128,1152]{1,0:T(8,128)(2,1)}) custom-call(bf16[128,1152]{1,0:T(8,128)(2,1)} %image_ref.1, bf16[128,1152]{1,0:T(8,128)(2,1)} %text_ref.1), custom_call_target="tpu_custom_call" | custom-call | tf_op jit(solution)/shard_map/low_rows/pallas_call | solution.py:27
  2.7 2.8 %collective-permute-start = (bf16[128,1152]{1,0:T(8,128)(2,1)}, bf16[128,1152]{1,0:T(8,128)(2,1)S(1)}, u32[]{:S(2)}, u32[]{:S(2)}) collective-permute-start(bf16[128,1152]{1,0:T(8,128)(2,1)} %get-tuple-element.39.t0), channel_id=1, source_target_pairs={{0,24},{8,16},{16,40},{24,32},{32,56},{40,48},{48,72},{56,64},{64,... | collective-permute-start | bytes 884744 | tf_op jit(solution)/shard_map/ppermute | solution.py:134
  5.4 0.2 collective-permute-start.1
  5.7 1.6 %collective-permute-start.2 = (bf16[128,1152]{1,0:T(8,128)(2,1)}, bf16[128,1152]{1,0:T(8,128)(2,1)S(1)}, u32[]{:S(2)}, u32[]{:S(2)}) collective-permute-start(bf16[128,1152]{1,0:T(8,128)(2,1)} %get-tuple-element.38.i0), channel_id=1, source_target_pairs={{0,2},{2,4},{4,6},{6,0},{1,3},{3,5},{5,7},{7,1},{8,10},{10,12},{12... | collective-permute-start | bytes 884744 | tf_op jit(solution)/shard_map/ppermute | solution.py:121
  7.2 1.7 %collective-permute-start.3 = (bf16[128,1152]{1,0:T(8,128)(2,1)}, bf16[128,1152]{1,0:T(8,128)(2,1)S(1)}, u32[]{:S(2)}, u32[]{:S(2)}) collective-permute-start(bf16[128,1152]{1,0:T(8,128)(2,1)} %get-tuple-element.38.i0), channel_id=1, source_target_pairs={{0,6},{2,0},{4,2},{6,4},{1,7},{3,1},{5,3},{7,5},{8,14},{10,8},{12,... | collective-permute-start | bytes 884744 | tf_op jit(solution)/shard_map/ppermute | solution.py:121
  8.9 4.8 %collective-permute-done.s0 = bf16[128,1152]{1,0:T(8,128)(2,1)S(1)} collective-permute-done((bf16[128,1152]{1,0:T(8,128)(2,1)}, bf16[128,1152]{1,0:T(8,128)(2,1)S(1)}, u32[]{:S(2)}, u32[]{:S(2)}) %collective-permute-start) | collective-permute-done | bytes 294944 | tf_op jit(solution)/shard_map/ppermute | solution.py:134
  13.7 0.4 collective-permute-done.1.t1
  14.1 1.3 %collective-permute-done.2.i1 = bf16[128,1152]{1,0:T(8,128)(2,1)S(1)} collective-permute-done((bf16[128,1152]{1,0:T(8,128)(2,1)}, bf16[128,1152]{1,0:T(8,128)(2,1)S(1)}, u32[]{:S(2)}, u32[]{:S(2)}) %collective-permute-start.2) | collective-permute-done | bytes 294944 | tf_op jit(solution)/shard_map/ppermute | solution.py:121
  15.4 1.0 %pad_maximum_fusion = bf16[384,1152]{1,0:T(8,128)(2,1)S(1)} fusion(bf16[128,1152]{1,0:T(8,128)(2,1)S(1)} %collective-permute-done.s0, bf16[128,1152]{1,0:T(8,128)(2,1)S(1)} %collective-permute-done.1.t1, bf16[128,1152]{1,0:T(8,128)(2,1)} %get-tuple-element.39.t0), kind=kLoop, calls=%fused_computation.1 | loop fusion | flops 2654208 | bytes 1769472 | tf_op jit(solution)/shard_map/concatenate | solution.py:184
  16.6 2.5 %collective-permute-start.4 = (bf16[128,1152]{1,0:T(8,128)(2,1)S(1)}, bf16[128,1152]{1,0:T(8,128)(2,1)S(1)}, u32[]{:S(2)}, u32[]{:S(2)}) collective-permute-start(bf16[128,1152]{1,0:T(8,128)(2,1)S(1)} %broadcast_select_fusion.1), channel_id=1, source_target_pairs={{0,24},{2,26},{4,28},{6,30},{8,16},{10,18},{12,20},{14,22},{16,40}... | collective-permute-start | bytes 884744 | tf_op jit(solution)/shard_map/ppermute | solution.py:182
  19.1 1.7 %collective-permute-start.5 = (bf16[128,1152]{1,0:T(8,128)(2,1)S(1)}, bf16[128,1152]{1,0:T(8,128)(2,1)S(1)}, u32[]{:S(2)}, u32[]{:S(2)}) collective-permute-start(bf16[128,1152]{1,0:T(8,128)(2,1)S(1)} %broadcast_select_fusion), channel_id=1, source_target_pairs={{0,2},{2,4},{4,6},{6,0},{1,7},{3,1},{5,3},{7,5},{8,10},{10,12},{12... | collective-permute-start | bytes 884744 | tf_op jit(solution)/shard_map/ppermute | solution.py:183
  20.8 4.7 %collective-permute-done.4.s1 = bf16[128,1152]{1,0:T(8,128)(2,1)S(1)} collective-permute-done((bf16[128,1152]{1,0:T(8,128)(2,1)S(1)}, bf16[128,1152]{1,0:T(8,128)(2,1)S(1)}, u32[]{:S(2)}, u32[]{:S(2)}) %collective-permute-start.4) | collective-permute-done | bytes 294944 | tf_op jit(solution)/shard_map/ppermute | solution.py:182
  25.5 1.7 %collective-permute-done.5.i3 = bf16[128,1152]{1,0:T(8,128)(2,1)S(1)} collective-permute-done((bf16[128,1152]{1,0:T(8,128)(2,1)S(1)}, bf16[128,1152]{1,0:T(8,128)(2,1)S(1)}, u32[]{:S(2)}, u32[]{:S(2)}) %collective-permute-start.5) | collective-permute-done | bytes 294944 | tf_op jit(solution)/shard_map/ppermute | solution.py:183
  28.7 3.4 %score.1 = (bf16[512,1152]{1,0:T(8,128)(2,1)S(1)}, bf16[1024,1152]{1,0:T(8,128)(2,1)S(1)}, bf16[512,1024]{1,0:T(8,128)(2,1)S(1)}, f32[8,128]{1,0:T(8,128)S(1)}) custom-call(f32[2]{0:T(128)S(1)} %pad_maximum_fusion.1.scalar_ref, bf16[128,1152]{1,0:T(8,128)(2,1)S(1)} %copy-done.1, bf16[128,1152]{1,0:T(8,128)(2,1)S(1)} %collective-permute-done.2.i1, ...), custom_call_target="tpu_custom_call" | custom-call | tf_op jit(solution)/shard_map/score/pallas_call | solution.py:62
  32.2 0.4 collective-permute-start.8
  32.6 1.6 %text_sums.1 = (f32[128,1152]{1,0:T(8,128)S(1)}, f32[128,1152]{1,0:T(8,128)S(1)}, f32[128,1152]{1,0:T(8,128)S(1)}, f32[128,1152]{1,0:T(8,128)S(1)}, f32[512,1152]{1,0:T(8,128)S(1)}) custom-call(bf16[512,1024]{1,0:T(8,128)(2,1)S(1)} %get-tuple-element.47.coefs, bf16[512,1152]{1,0:T(8,128)(2,1)S(1)} %get-tuple-element.48.images), custom_call_target="tpu_custom_call" | custom-call | tf_op jit(solution)/shard_map/text_sums/pallas_call | solution.py:93
  34.2 0.2 multiply_convert_fusion
  34.4 0.2 collective-permute-start.9
  34.7 0.5 copy-done.3
  35.3 0.8 collective-permute-start.10
  36.1 1.5 %image_sums.1 = (f32[128,1152]{1,0:T(8,128)S(1)}, f32[128,1152]{1,0:T(8,128)S(1)}, f32[128,1152]{1,0:T(8,128)S(1)}, f32[128,1152]{1,0:T(8,128)S(1)}) custom-call(bf16[512,1024]{1,0:T(8,128)(2,1)S(1)} %get-tuple-element.47.coefs, bf16[1024,1152]{1,0:T(8,128)(2,1)S(1)} %get-tuple-element.54.texts), custom_call_target="tpu_custom_call" | custom-call | tf_op jit(solution)/shard_map/image_sums/pallas_call | solution.py:109
  37.7 1.5 %collective-permute-done.10 = f32[8,128]{1,0:T(8,128)S(1)} collective-permute-done((f32[8,128]{1,0:T(8,128)S(1)}, f32[8,128]{1,0:T(8,128)S(1)}, u32[]{:S(2)}, u32[]{:S(2)}) %collective-permute-start.10) | collective-permute-done | bytes 4128 | tf_op jit(solution)/shard_map/ppermute | solution.py:117
  39.2 0.4 collective-permute-start.13
  39.5 2.8 %collective-permute-start.14 = (f32[8,128]{1,0:T(8,128)S(1)}, f32[8,128]{1,0:T(8,128)S(1)}, u32[]{:S(2)}, u32[]{:S(2)}) collective-permute-start(f32[8,128]{1,0:T(8,128)S(1)} %add.86), channel_id=1, source_target_pairs={{0,4},{2,6},{4,0},{6,2},{1,5},{3,7},{5,1},{7,3},{8,12},{10,14},{12... | collective-permute-start | bytes 12296 | tf_op jit(solution)/shard_map/ppermute | solution.py:171
  42.4 1.1 %collective-permute-start.15 = (f32[8,128]{1,0:T(8,128)S(1)}, f32[8,128]{1,0:T(8,128)S(1)}, u32[]{:S(2)}, u32[]{:S(2)}) collective-permute-start(f32[8,128]{1,0:T(8,128)S(1)} %add.86), channel_id=1, source_target_pairs={{0,6},{2,0},{4,2},{6,4},{1,7},{3,1},{5,3},{7,5},{8,14},{10,8},{12,... | collective-permute-start | bytes 12296 | tf_op jit(solution)/shard_map/ppermute | solution.py:171
  43.6 1.8 %collective-permute-start.12 = (f16[128,1152]{1,0:T(8,128)(2,1)S(1)}, f16[128,1152]{1,0:T(8,128)(2,1)S(1)}, u32[]{:S(2)}, u32[]{:S(2)}) collective-permute-start(f16[128,1152]{1,0:T(8,128)(2,1)S(1)} %multiply_convert_fusion.5), channel_id=1, source_target_pairs={{24,0},{26,2},{28,4},{30,6},{16,8},{18,10},{20,12},{22,14},{40,16}... | collective-permute-start | bytes 884744 | tf_op jit(solution)/shard_map/ppermute | solution.py:201
  45.4 0.2 collective-permute-start.11
  46.0 5.7 %collective-permute-done.12 = f16[128,1152]{1,0:T(8,128)(2,1)S(1)} collective-permute-done((f16[128,1152]{1,0:T(8,128)(2,1)S(1)}, f16[128,1152]{1,0:T(8,128)(2,1)S(1)}, u32[]{:S(2)}, u32[]{:S(2)}) %collective-permute-start.12) | collective-permute-done | bytes 294944 | tf_op jit(solution)/shard_map/ppermute | solution.py:201
  51.6 0.6 collective-permute-done.11
  52.2 1.8 %collective-permute-start.20 = (f32[8,128]{1,0:T(8,128)S(1)}, f32[8,128]{1,0:T(8,128)S(1)}, u32[]{:S(2)}, u32[]{:S(2)}) collective-permute-start(f32[8,128]{1,0:T(8,128)S(1)} %add_add_fusion.1), channel_id=1, source_target_pairs={{0,16},{16,0},{32,48},{48,32},{64,80},{80,64},{96,112},{112,96},{1... | collective-permute-start | bytes 12296 | tf_op jit(solution)/shard_map/ppermute | solution.py:171
  54.0 4.3 %collective-permute-start.21 = (f32[8,128]{1,0:T(8,128)S(1)}, f32[8,128]{1,0:T(8,128)S(1)}, u32[]{:S(2)}, u32[]{:S(2)}) collective-permute-start(f32[8,128]{1,0:T(8,128)S(1)} %add_add_fusion.1), channel_id=1, source_target_pairs={{0,32},{16,48},{32,0},{48,16},{64,96},{80,112},{96,64},{112,80},{1... | collective-permute-start | bytes 12296 | tf_op jit(solution)/shard_map/ppermute | solution.py:171
  58.4 0.2 multiply_convert_fusion.1
  58.6 0.3 collective-permute-start.18
  58.9 1.8 %collective-permute-start.19 = (f16[128,1152]{1,0:T(8,128)(2,1)S(1)}, f16[128,1152]{1,0:T(8,128)(2,1)S(1)}, u32[]{:S(2)}, u32[]{:S(2)}) collective-permute-start(f16[128,1152]{1,0:T(8,128)(2,1)S(1)} %get-tuple-element.75), channel_id=1, source_target_pairs={{0,2},{2,4},{4,6},{6,0},{1,3},{3,5},{5,7},{7,1},{8,10},{10,12},{12... | collective-permute-start | bytes 884744 | tf_op jit(solution)/shard_map/ppermute | solution.py:121
  60.7 0.3 multiply_convert_fusion.3
  61.1 1.7 %collective-permute-start.16 = (f16[128,1152]{1,0:T(8,128)(2,1)S(1)}, f16[128,1152]{1,0:T(8,128)(2,1)S(1)}, u32[]{:S(2)}, u32[]{:S(2)}) collective-permute-start(f16[128,1152]{1,0:T(8,128)(2,1)S(1)} %get-tuple-element.74), channel_id=1, source_target_pairs={{24,0},{16,8},{40,16},{32,24},{56,32},{48,40},{72,48},{64,56},{88,... | collective-permute-start | bytes 884744 | tf_op jit(solution)/shard_map/ppermute | solution.py:138
  62.8 1.7 %collective-permute-done.22 = f32[8,128]{1,0:T(8,128)S(1)} collective-permute-done((f32[8,128]{1,0:T(8,128)S(1)}, f32[8,128]{1,0:T(8,128)S(1)}, u32[]{:S(2)}, u32[]{:S(2)}) %collective-permute-start.22) | collective-permute-done | bytes 4128 | tf_op jit(solution)/shard_map/ppermute | solution.py:171
  64.5 0.9 %collective-permute-done.18 = f16[128,1152]{1,0:T(8,128)(2,1)S(1)} collective-permute-done((f16[128,1152]{1,0:T(8,128)(2,1)S(1)}, f16[128,1152]{1,0:T(8,128)(2,1)S(1)}, u32[]{:S(2)}, u32[]{:S(2)}) %collective-permute-start.18) | collective-permute-done | bytes 294944 | tf_op jit(solution)/shard_map/ppermute | solution.py:121
  65.4 1.4 %collective-permute-done.19 = f16[128,1152]{1,0:T(8,128)(2,1)S(1)} collective-permute-done((f16[128,1152]{1,0:T(8,128)(2,1)S(1)}, f16[128,1152]{1,0:T(8,128)(2,1)S(1)}, u32[]{:S(2)}, u32[]{:S(2)}) %collective-permute-start.19) | collective-permute-done | bytes 294944 | tf_op jit(solution)/shard_map/ppermute | solution.py:121
  66.8 2.6 %collective-permute-done.16 = f16[128,1152]{1,0:T(8,128)(2,1)S(1)} collective-permute-done((f16[128,1152]{1,0:T(8,128)(2,1)S(1)}, f16[128,1152]{1,0:T(8,128)(2,1)S(1)}, u32[]{:S(2)}, u32[]{:S(2)}) %collective-permute-start.16) | collective-permute-done | bytes 294944 | tf_op jit(solution)/shard_map/ppermute | solution.py:138
  69.5 4.2 %collective-permute-start.23 = (f32[8,128]{1,0:T(8,128)S(1)}, f32[8,128]{1,0:T(8,128)S(1)}, u32[]{:S(2)}, u32[]{:S(2)}) collective-permute-start(f32[8,128]{1,0:T(8,128)S(1)} %add_add_fusion), channel_id=1, source_target_pairs={{0,64},{32,96},{64,0},{96,32},{128,192},{160,224},{192,128},{224,1... | collective-permute-start | bytes 12296 | tf_op jit(solution)/shard_map/ppermute | solution.py:171
  73.6 4.3 %collective-permute-start.24 = (f32[8,128]{1,0:T(8,128)S(1)}, f32[8,128]{1,0:T(8,128)S(1)}, u32[]{:S(2)}, u32[]{:S(2)}) collective-permute-start(f32[8,128]{1,0:T(8,128)S(1)} %add_add_fusion), channel_id=1, source_target_pairs={{0,128},{32,160},{64,192},{96,224},{128,0},{160,32},{192,64},{224,... | collective-permute-start | bytes 12296 | tf_op jit(solution)/shard_map/ppermute | solution.py:171
  78.0 0.3 multiply_reduce_fusion.1
  78.3 0.4 multiply_reduce_fusion
  78.6 1.5 %subtract_divide_fusion = (f32[128,1152]{1,0:T(8,128)}, f32[128,1152]{1,0:T(8,128)}) fusion(bf16[128,1152]{1,0:T(8,128)(2,1)S(1)} %copy-done.2, f32[128]{0:T(128)S(1)} %multiply_reduce_fusion, f32[128]{0:T(128)S(1)} %add_sqrt_fusion, f16[128,1152]{1,0:T(8,128)(2,1)S(1)} %collective-permute-done.17, f16[128,1152]{1,0:T(8,128)(2,1)S(1)} %collective-permute-done.16, ...), kind=kLoop, calls=%fused_computation.8 | loop fusion | flops 3981312 | bytes 4425732 | tf_op jit(solution)/shard_map/div | solution.py:163
  80.2 1.0 %collective-permute-done.24 = f32[8,128]{1,0:T(8,128)S(1)} collective-permute-done((f32[8,128]{1,0:T(8,128)S(1)}, f32[8,128]{1,0:T(8,128)S(1)}, u32[]{:S(2)}, u32[]{:S(2)}) %collective-permute-start.24) | collective-permute-done | bytes 4128 | tf_op jit(solution)/shard_map/ppermute | solution.py:171
  81.2 2.5 %collective-permute-done.25 = f32[8,128]{1,0:T(8,128)S(1)} collective-permute-done((f32[8,128]{1,0:T(8,128)S(1)}, f32[8,128]{1,0:T(8,128)S(1)}, u32[]{:S(2)}, u32[]{:S(2)}) %collective-permute-start.25) | collective-permute-done | bytes 4128 | tf_op jit(solution)/shard_map/ppermute | solution.py:171
  83.7 0.6 add_reduce_fusion
  (37 shorter events, 1.1 us)
Async XLA Ops:
  2.7 11.1 %collective-permute-start = (bf16[128,1152]{1,0:T(8,128)(2,1)}, bf16[128,1152]{1,0:T(8,128)(2,1)S(1)}, u32[]{:S(2)}, u32[]{:S(2)}) collective-permute-start(bf16[128,1152]{1,0:T(8,128)(2,1)} %get-tuple-element.39.t0), channel_id=1, source_target_pairs={{0,24},{8,16},{16,40},{24,32},{32,56},{40,48},{48,72},{56,64},{64,... | collective-permute-start | bytes 884744 | tf_op jit(solution)/shard_map/ppermute | solution.py:134
  5.4 8.7 %collective-permute-start.1 = (bf16[128,1152]{1,0:T(8,128)(2,1)}, bf16[128,1152]{1,0:T(8,128)(2,1)S(1)}, u32[]{:S(2)}, u32[]{:S(2)}) collective-permute-start(bf16[128,1152]{1,0:T(8,128)(2,1)} %get-tuple-element.39.t0), channel_id=1, source_target_pairs={{0,8},{8,0},{1,9},{9,1},{2,10},{10,2},{3,11},{11,3},{4,12},{12,4},... | collective-permute-start | bytes 884744 | tf_op jit(solution)/shard_map/ppermute | solution.py:117
  5.7 9.7 %collective-permute-start.2 = (bf16[128,1152]{1,0:T(8,128)(2,1)}, bf16[128,1152]{1,0:T(8,128)(2,1)S(1)}, u32[]{:S(2)}, u32[]{:S(2)}) collective-permute-start(bf16[128,1152]{1,0:T(8,128)(2,1)} %get-tuple-element.38.i0), channel_id=1, source_target_pairs={{0,2},{2,4},{4,6},{6,0},{1,3},{3,5},{5,7},{7,1},{8,10},{10,12},{12... | collective-permute-start | bytes 884744 | tf_op jit(solution)/shard_map/ppermute | solution.py:121
  7.2 8.2 %collective-permute-start.3 = (bf16[128,1152]{1,0:T(8,128)(2,1)}, bf16[128,1152]{1,0:T(8,128)(2,1)S(1)}, u32[]{:S(2)}, u32[]{:S(2)}) collective-permute-start(bf16[128,1152]{1,0:T(8,128)(2,1)} %get-tuple-element.38.i0), channel_id=1, source_target_pairs={{0,6},{2,0},{4,2},{6,4},{1,7},{3,1},{5,3},{7,5},{8,14},{10,8},{12,... | collective-permute-start | bytes 884744 | tf_op jit(solution)/shard_map/ppermute | solution.py:121
  8.9 19.8 %copy-start = (bf16[128,1152]{1,0:T(8,128)(2,1)S(1)}, bf16[128,1152]{1,0:T(8,128)(2,1)}, u32[]{:S(2)}) copy-start(bf16[128,1152]{1,0:T(8,128)(2,1)} %get-tuple-element.39.t0) | copy-start | bytes 884740
  8.9 19.8 %copy-start.1 = (bf16[128,1152]{1,0:T(8,128)(2,1)S(1)}, bf16[128,1152]{1,0:T(8,128)(2,1)}, u32[]{:S(2)}) copy-start(bf16[128,1152]{1,0:T(8,128)(2,1)} %get-tuple-element.38.i0) | copy-start | bytes 884740
  16.4 10.7 %collective-permute-start.6 = (bf16[384,1152]{1,0:T(8,128)(2,1)S(1)}, bf16[384,1152]{1,0:T(8,128)(2,1)S(1)}, u32[]{:S(2)}, u32[]{:S(2)}) collective-permute-start(bf16[384,1152]{1,0:T(8,128)(2,1)S(1)} %pad_maximum_fusion), channel_id=1, source_target_pairs={{0,1},{1,0},{2,3},{3,2},{4,5},{5,4},{6,7},{7,6},{8,9},{9,8},{10,11... | collective-permute-start | bytes 2654216 | tf_op jit(solution)/shard_map/ppermute | solution.py:117
  16.6 8.9 %collective-permute-start.4 = (bf16[128,1152]{1,0:T(8,128)(2,1)S(1)}, bf16[128,1152]{1,0:T(8,128)(2,1)S(1)}, u32[]{:S(2)}, u32[]{:S(2)}) collective-permute-start(bf16[128,1152]{1,0:T(8,128)(2,1)S(1)} %broadcast_select_fusion.1), channel_id=1, source_target_pairs={{0,24},{2,26},{4,28},{6,30},{8,16},{10,18},{12,20},{14,22},{16,40}... | collective-permute-start | bytes 884744 | tf_op jit(solution)/shard_map/ppermute | solution.py:182
  19.1 8.0 %collective-permute-start.5 = (bf16[128,1152]{1,0:T(8,128)(2,1)S(1)}, bf16[128,1152]{1,0:T(8,128)(2,1)S(1)}, u32[]{:S(2)}, u32[]{:S(2)}) collective-permute-start(bf16[128,1152]{1,0:T(8,128)(2,1)S(1)} %broadcast_select_fusion), channel_id=1, source_target_pairs={{0,2},{2,4},{4,6},{6,0},{1,7},{3,1},{5,3},{7,5},{8,10},{10,12},{12... | collective-permute-start | bytes 884744 | tf_op jit(solution)/shard_map/ppermute | solution.py:183
  27.1 1.6 %collective-permute-start.7 = (bf16[128,1152]{1,0:T(8,128)(2,1)S(1)}, bf16[128,1152]{1,0:T(8,128)(2,1)S(1)}, u32[]{:S(2)}, u32[]{:S(2)}) collective-permute-start(bf16[128,1152]{1,0:T(8,128)(2,1)S(1)} %collective-permute-done.4.s1), channel_id=1, source_target_pairs={{0,1},{1,0},{2,3},{3,2},{4,5},{5,4},{6,7},{7,6},{8,9},{9,8},{10,11... | collective-permute-start | bytes 884744 | tf_op jit(solution)/shard_map/ppermute | solution.py:117
  32.2 2.2 %collective-permute-start.8 = (f32[8,128]{1,0:T(8,128)S(1)}, f32[8,128]{1,0:T(8,128)S(1)}, u32[]{:S(2)}, u32[]{:S(2)}) collective-permute-start(f32[8,128]{1,0:T(8,128)S(1)} %get-tuple-element.51), channel_id=1, source_target_pairs={{0,1},{1,0},{2,3},{3,2},{4,5},{5,4},{6,7},{7,6},{8,9},{9,8},{10,11... | collective-permute-start | bytes 12296 | tf_op jit(solution)/shard_map/ppermute | solution.py:117
  34.2 1.0 %copy-start.3 = (bf16[128,1152]{1,0:T(8,128)(2,1)S(1)}, bf16[128,1152]{1,0:T(8,128)(2,1)}, u32[]{:S(2)}) copy-start(bf16[128,1152]{1,0:T(8,128)(2,1)} %image_ref.1) | copy-start | bytes 884740
  34.4 4.7 %collective-permute-start.9 = (f16[512,1152]{1,0:T(8,128)(2,1)S(1)}, f16[512,1152]{1,0:T(8,128)(2,1)S(1)}, u32[]{:S(2)}, u32[]{:S(2)}) collective-permute-start(f16[512,1152]{1,0:T(8,128)(2,1)S(1)} %multiply_convert_fusion), channel_id=1, source_target_pairs={{0,1},{1,0},{2,3},{3,2},{4,5},{5,4},{6,7},{7,6},{8,9},{9,8},{10,11... | collective-permute-start | bytes 3538952 | tf_op jit(solution)/shard_map/ppermute | solution.py:117
  35.3 3.9 %collective-permute-start.10 = (f32[8,128]{1,0:T(8,128)S(1)}, f32[8,128]{1,0:T(8,128)S(1)}, u32[]{:S(2)}, u32[]{:S(2)}) collective-permute-start(f32[8,128]{1,0:T(8,128)S(1)} %add.85), channel_id=1, source_target_pairs={{0,8},{8,0},{1,9},{9,1},{2,10},{10,2},{3,11},{11,3},{4,12},{12,4},... | collective-permute-start | bytes 12296 | tf_op jit(solution)/shard_map/ppermute | solution.py:117
  37.6 8.0 %copy-start.2 = (bf16[128,1152]{1,0:T(8,128)(2,1)S(1)}, bf16[128,1152]{1,0:T(8,128)(2,1)}, u32[]{:S(2)}) copy-start(bf16[128,1152]{1,0:T(8,128)(2,1)} %text_ref.1) | copy-start | bytes 884740
  39.2 6.6 %collective-permute-start.13 = (f32[8,128]{1,0:T(8,128)S(1)}, f32[8,128]{1,0:T(8,128)S(1)}, u32[]{:S(2)}, u32[]{:S(2)}) collective-permute-start(f32[8,128]{1,0:T(8,128)S(1)} %add.86), channel_id=1, source_target_pairs={{0,2},{2,4},{4,6},{6,0},{1,3},{3,5},{5,7},{7,1},{8,10},{10,12},{12... | collective-permute-start | bytes 12296 | tf_op jit(solution)/shard_map/ppermute | solution.py:171
  39.5 6.3 %collective-permute-start.14 = (f32[8,128]{1,0:T(8,128)S(1)}, f32[8,128]{1,0:T(8,128)S(1)}, u32[]{:S(2)}, u32[]{:S(2)}) collective-permute-start(f32[8,128]{1,0:T(8,128)S(1)} %add.86), channel_id=1, source_target_pairs={{0,4},{2,6},{4,0},{6,2},{1,5},{3,7},{5,1},{7,3},{8,12},{10,14},{12... | collective-permute-start | bytes 12296 | tf_op jit(solution)/shard_map/ppermute | solution.py:171
  42.4 3.6 %collective-permute-start.15 = (f32[8,128]{1,0:T(8,128)S(1)}, f32[8,128]{1,0:T(8,128)S(1)}, u32[]{:S(2)}, u32[]{:S(2)}) collective-permute-start(f32[8,128]{1,0:T(8,128)S(1)} %add.86), channel_id=1, source_target_pairs={{0,6},{2,0},{4,2},{6,4},{1,7},{3,1},{5,3},{7,5},{8,14},{10,8},{12,... | collective-permute-start | bytes 12296 | tf_op jit(solution)/shard_map/ppermute | solution.py:171
  43.6 8.0 %collective-permute-start.12 = (f16[128,1152]{1,0:T(8,128)(2,1)S(1)}, f16[128,1152]{1,0:T(8,128)(2,1)S(1)}, u32[]{:S(2)}, u32[]{:S(2)}) collective-permute-start(f16[128,1152]{1,0:T(8,128)(2,1)S(1)} %multiply_convert_fusion.5), channel_id=1, source_target_pairs={{24,0},{26,2},{28,4},{30,6},{16,8},{18,10},{20,12},{22,14},{40,16}... | collective-permute-start | bytes 884744 | tf_op jit(solution)/shard_map/ppermute | solution.py:201
  45.4 6.8 %collective-permute-start.11 = (f16[128,1152]{1,0:T(8,128)(2,1)S(1)}, f16[128,1152]{1,0:T(8,128)(2,1)S(1)}, u32[]{:S(2)}, u32[]{:S(2)}) collective-permute-start(f16[128,1152]{1,0:T(8,128)(2,1)S(1)} %multiply_convert_fusion.6), channel_id=1, source_target_pairs={{2,0},{4,2},{6,4},{0,6},{7,1},{1,3},{3,5},{5,7},{10,8},{12,10},{14... | collective-permute-start | bytes 884744 | tf_op jit(solution)/shard_map/ppermute | solution.py:200
  52.2 8.8 %collective-permute-start.20 = (f32[8,128]{1,0:T(8,128)S(1)}, f32[8,128]{1,0:T(8,128)S(1)}, u32[]{:S(2)}, u32[]{:S(2)}) collective-permute-start(f32[8,128]{1,0:T(8,128)S(1)} %add_add_fusion.1), channel_id=1, source_target_pairs={{0,16},{16,0},{32,48},{48,32},{64,80},{80,64},{96,112},{112,96},{1... | collective-permute-start | bytes 12296 | tf_op jit(solution)/shard_map/ppermute | solution.py:171
  54.0 8.7 %collective-permute-start.21 = (f32[8,128]{1,0:T(8,128)S(1)}, f32[8,128]{1,0:T(8,128)S(1)}, u32[]{:S(2)}, u32[]{:S(2)}) collective-permute-start(f32[8,128]{1,0:T(8,128)S(1)} %add_add_fusion.1), channel_id=1, source_target_pairs={{0,32},{16,48},{32,0},{48,16},{64,96},{80,112},{96,64},{112,80},{1... | collective-permute-start | bytes 12296 | tf_op jit(solution)/shard_map/ppermute | solution.py:171
  58.4 6.1 %collective-permute-start.22 = (f32[8,128]{1,0:T(8,128)S(1)}, f32[8,128]{1,0:T(8,128)S(1)}, u32[]{:S(2)}, u32[]{:S(2)}) collective-permute-start(f32[8,128]{1,0:T(8,128)S(1)} %add_add_fusion.1), channel_id=1, source_target_pairs={{0,48},{16,32},{32,16},{48,0},{64,112},{80,96},{96,80},{112,64},{1... | collective-permute-start | bytes 12296 | tf_op jit(solution)/shard_map/ppermute | solution.py:171
  58.6 6.8 %collective-permute-start.18 = (f16[128,1152]{1,0:T(8,128)(2,1)S(1)}, f16[128,1152]{1,0:T(8,128)(2,1)S(1)}, u32[]{:S(2)}, u32[]{:S(2)}) collective-permute-start(f16[128,1152]{1,0:T(8,128)(2,1)S(1)} %get-tuple-element.76), channel_id=1, source_target_pairs={{0,6},{2,0},{4,2},{6,4},{1,7},{3,1},{5,3},{7,5},{8,14},{10,8},{12,... | collective-permute-start | bytes 884744 | tf_op jit(solution)/shard_map/ppermute | solution.py:121
  58.9 7.9 %collective-permute-start.19 = (f16[128,1152]{1,0:T(8,128)(2,1)S(1)}, f16[128,1152]{1,0:T(8,128)(2,1)S(1)}, u32[]{:S(2)}, u32[]{:S(2)}) collective-permute-start(f16[128,1152]{1,0:T(8,128)(2,1)S(1)} %get-tuple-element.75), channel_id=1, source_target_pairs={{0,2},{2,4},{4,6},{6,0},{1,3},{3,5},{5,7},{7,1},{8,10},{10,12},{12... | collective-permute-start | bytes 884744 | tf_op jit(solution)/shard_map/ppermute | solution.py:121
  61.1 8.4 %collective-permute-start.16 = (f16[128,1152]{1,0:T(8,128)(2,1)S(1)}, f16[128,1152]{1,0:T(8,128)(2,1)S(1)}, u32[]{:S(2)}, u32[]{:S(2)}) collective-permute-start(f16[128,1152]{1,0:T(8,128)(2,1)S(1)} %get-tuple-element.74), channel_id=1, source_target_pairs={{24,0},{16,8},{40,16},{32,24},{56,32},{48,40},{72,48},{64,56},{88,... | collective-permute-start | bytes 884744 | tf_op jit(solution)/shard_map/ppermute | solution.py:138
  62.8 6.7 %collective-permute-start.17 = (f16[128,1152]{1,0:T(8,128)(2,1)S(1)}, f16[128,1152]{1,0:T(8,128)(2,1)S(1)}, u32[]{:S(2)}, u32[]{:S(2)}) collective-permute-start(f16[128,1152]{1,0:T(8,128)(2,1)S(1)} %get-tuple-element.73), channel_id=1, source_target_pairs={{0,8},{8,0},{1,9},{9,1},{2,10},{10,2},{3,11},{11,3},{4,12},{12,4},... | collective-permute-start | bytes 884744 | tf_op jit(solution)/shard_map/ppermute | solution.py:117
  69.5 10.7 %collective-permute-start.23 = (f32[8,128]{1,0:T(8,128)S(1)}, f32[8,128]{1,0:T(8,128)S(1)}, u32[]{:S(2)}, u32[]{:S(2)}) collective-permute-start(f32[8,128]{1,0:T(8,128)S(1)} %add_add_fusion), channel_id=1, source_target_pairs={{0,64},{32,96},{64,0},{96,32},{128,192},{160,224},{192,128},{224,1... | collective-permute-start | bytes 12296 | tf_op jit(solution)/shard_map/ppermute | solution.py:171
  73.6 7.5 %collective-permute-start.24 = (f32[8,128]{1,0:T(8,128)S(1)}, f32[8,128]{1,0:T(8,128)S(1)}, u32[]{:S(2)}, u32[]{:S(2)}) collective-permute-start(f32[8,128]{1,0:T(8,128)S(1)} %add_add_fusion), channel_id=1, source_target_pairs={{0,128},{32,160},{64,192},{96,224},{128,0},{160,32},{192,64},{224,... | collective-permute-start | bytes 12296 | tf_op jit(solution)/shard_map/ppermute | solution.py:171
  78.0 5.7 %collective-permute-start.25 = (f32[8,128]{1,0:T(8,128)S(1)}, f32[8,128]{1,0:T(8,128)S(1)}, u32[]{:S(2)}, u32[]{:S(2)}) collective-permute-start(f32[8,128]{1,0:T(8,128)S(1)} %add_add_fusion), channel_id=1, source_target_pairs={{0,192},{32,224},{64,128},{96,160},{128,64},{160,96},{192,0},{224,... | collective-permute-start | bytes 12296 | tf_op jit(solution)/shard_map/ppermute | solution.py:171

commit v3 on v0

v3 whole, which is shorter than its diff:
```python
import jax
import jax.numpy as jnp
from jax import lax
from jax.experimental import pallas as pl
from jax.experimental.pallas import tpu as pltpu
from jax.sharding import Mesh, PartitionSpec as P

STEPS = 2
ROWS = 128
TILE = 256
AXES = ("z", "xh", "xl", "y", "c")
SHAPE = (8, 2, 2, 4, 2)
VMEM = pl.BlockSpec(memory_space=pltpu.VMEM)
SMEM = pl.BlockSpec(memory_space=pltpu.SMEM)
F32 = jnp.float32
BF16 = jnp.bfloat16


def call(kernel, outs, cost, limit, *args, scratch=()):
    shapes = tuple(jax.ShapeDtypeStruct(shape, dtype) for shape, dtype in outs)
    return pl.pallas_call(
        kernel,
        out_shape=shapes,
        in_specs=[SMEM if a.ndim == 1 else VMEM for a in args],
        out_specs=tuple(SMEM if len(s.shape) == 1 else VMEM for s in shapes),
        scratch_shapes=list(scratch),
        compiler_params=pltpu.CompilerParams(vmem_limit_bytes=limit * 2**20),
        cost_estimate=pl.CostEstimate(flops=int(cost * 1.0e9), bytes_accessed=int(cost * 3.0e6), transcendentals=0),
        name=kernel.__name__,
    )(*args)


def inverse_norm(rows):
    values = rows.astype(F32)
    return 1.0 / jnp.sqrt(jnp.sum(values * values, axis=1, keepdims=True) + 1e-06)


def as_row(column):
    eye = lax.broadcasted_iota(jnp.int32, (ROWS, ROWS), 0) == lax.broadcasted_iota(jnp.int32, (ROWS, ROWS), 1)
    parts = [
        jnp.sum(jnp.where(eye, column[n:n + ROWS], 0.0), axis=0, keepdims=True)
        for n in range(0, column.shape[0], ROWS)]
    return jnp.concatenate(parts, axis=1) if len(parts) > 1 else parts[0]


def dot_t(a, b):
    return lax.dot_general(a, b, (((1,), (1,)), ((), ())), preferred_element_type=F32)


def t_dot(a, b):
    return lax.dot_general(a, b, (((0,), (0,)), ((), ())), preferred_element_type=F32)


def dot(a, b):
    return jnp.dot(a, b, preferred_element_type=F32)


def terms(scalar_ref, products, image_inverse, text_inverse, own=False):
    z = products * (scalar_ref[0] * image_inverse) * text_inverse + scalar_ref[1]
    if own:
        row = lax.broadcasted_iota(jnp.int32, z.shape, 0)
        positive = (row == lax.broadcasted_iota(jnp.int32, z.shape, 1)) & (row < ROWS)
        z = jnp.where(positive, -z, z)
    small = jnp.exp(-jnp.abs(z))
    term = jnp.maximum(z, 0.0) + jnp.log1p(small)
    coef = jnp.where(z >= 0.0, 1.0, small) / (1.0 + small)
    if own:
        coef = jnp.where(positive, -coef, coef)
    total = sum(
        jnp.sum(term[:, n:n + 128].reshape(-1, 8, 128), axis=0) for n in range(0, z.shape[1], 128))
    return total, (coef * text_inverse).astype(BF16), (coef * image_inverse).astype(BF16)


def near(scalar_ref, i0, ia, ib, t0, t1, s0, t0x, t1x, s0x,
         images, texts, image_inverse, text_inverse, loss, ht0, ht1, hs0, htx, hi, coefs):
    for n, ref in enumerate((i0, ia, ib)):
        images[pl.ds(n * ROWS, ROWS), :] = ref[...]
    for n, ref in enumerate((t0, t1, s0, t0x, t1x, s0x)):
        texts[pl.ds(n * ROWS, ROWS), :] = ref[...]
    column = inverse_norm(images[...])
    image_inverse[...] = jnp.broadcast_to(column, image_inverse.shape)
    total = jnp.zeros((8, 128), F32)
    outs = (ht0, ht1, hs0)
    for tile in range(3):
        span = pl.ds(tile * TILE, TILE)
        block = texts[span, :]
        row = as_row(inverse_norm(block))
        text_inverse[:, span] = jnp.broadcast_to(row, (8, TILE))
        part, by_text, by_image = terms(scalar_ref, dot_t(images[...], block), column, row, own=tile == 0)
        total = total + part
        coefs[:, span] = by_text
        update = t_dot(by_image, images[...])
        for half in range(2):
            n = 2 * tile + half
            piece = update[half * ROWS:(half + 1) * ROWS]
            if n < 3:
                outs[n][...] = piece
            else:
                htx[pl.ds((n - 3) * ROWS, ROWS), :] = piece
    hi[...] = dot(coefs[...], texts[...])
    loss[...] = total


def far(scalar_ref, i2, s1, sx, images, texts, image_inverse, text_inverse, loss_in,
        loss, by_near_text, by_near_image, by_far_text, by_far_image, four, pair):
    four[pl.ds(0, 3 * ROWS), :] = images[...]
    four[pl.ds(3 * ROWS, ROWS), :] = i2[...]
    pair[pl.ds(0, ROWS), :] = s1[...]
    pair[pl.ds(ROWS, ROWS), :] = sx[...]
    column = inverse_norm(i2[...])
    total, by_text, by_image = terms(scalar_ref, dot_t(i2[...], texts[...]), column, text_inverse[0:1, :])
    by_near_text[...] = by_text
    by_near_image[...] = by_image
    columns = jnp.concatenate([image_inverse[:, 0:1], column], axis=0)
    part, by_text, by_image = terms(
        scalar_ref, dot_t(four[...], pair[...]), columns, as_row(inverse_norm(pair[...])))
    by_far_text[...] = by_text
    by_far_image[...] = by_image
    loss[...] = loss_in[...] + total + part


def sums(core_ref, by_near_text, by_near_image, by_far_text, by_far_image, i2, four, pair, texts,
         ht0, ht1, hs0, htx, hi, own_text, own_image, blocks):
    second = core_ref[0]

    def put(on_first, on_second, value):
        at = pl.multiple_of((on_first + (on_second - on_first) * second) * ROWS, ROWS)
        blocks[pl.ds(at, ROWS), :] = value

    for n, old in enumerate((ht0, ht1, hs0)):
        value = old[...] + t_dot(by_near_image[:, n * ROWS:(n + 1) * ROWS], i2[...])
        if n == 0:
            own_text[...] = value
        else:
            put(7 + 2 * (n - 1), 1 + 2 * (n - 1) + 1, value)
    for n in range(3):
        value = htx[pl.ds(n * ROWS, ROWS), :] + t_dot(
            by_near_image[:, (n + 3) * ROWS:(n + 4) * ROWS], i2[...])
        if n == 0:
            blocks[pl.ds(0, ROWS), :] = value
        else:
            put(7 + 2 * (n - 1) + 1, 1 + 2 * (n - 1), value)
    value = t_dot(by_far_image[...], four[...])
    put(11, 6, value[:ROWS])
    put(12, 5, value[ROWS:])
    for n in range(3):
        put(2 + 2 * n, 7 + 2 * n, jnp.zeros_like(own_text))
    rest = dot(by_far_text[...], pair[...])
    own_image[...] = hi[pl.ds(0, ROWS), :] + rest[:ROWS]
    for n in (1, 2):
        put(2 * n - 1, 6 + 2 * n, hi[pl.ds(n * ROWS, ROWS), :] + rest[n * ROWS:(n + 1) * ROWS])
    put(5, 12, dot(by_near_text[...], texts[...]) + rest[3 * ROWS:])


def everyone(loss, out):
    out[...] = jnp.broadcast_to(jnp.sum(loss[...], axis=0, keepdims=True), out.shape)


def finish(scalar_ref, raw, hat_ref, *rest):
    if len(rest) == 3:
        parts, out, loss = rest
        loss[0] = jnp.sum(parts[...]) / (ROWS * 256 * STEPS * ROWS * 16)
    else:
        out, = rest
    inverse = inverse_norm(raw[...])
    unit = raw[...].astype(F32) * inverse
    hat = scalar_ref[0] * hat_ref[...]
    out[...] = (hat - unit * jnp.sum(unit * hat, axis=1, keepdims=True)) * inverse


def inner(group, side, y):
    return group, 1 - side, y


def outer(group, side, y):
    return (group + 1) % 16, 1 - side, y


def outer_back(group, side, y):
    return (group + 15) % 16, 1 - side, y


def far_back(group, side, y):
    return (group + 15) % 16, side, y


def up(group, side, y):
    return group, side, (y + 1) % 4


def down(group, side, y):
    return group, side, (y + 3) % 4


def across(group, side, y):
    return group, side, (y + 2) % 4


def move(block, first, second=None):
    route = []
    for chip in range(128):
        place = (chip // 8, chip // 4 % 2, chip % 4)
        for core, to in enumerate((first, second or first)):
            group, side, y = to(*place)
            route.append((chip * 2 + core, (group * 8 + side * 4 + y) * 2 + core))
    return lax.ppermute(block, AXES, route)


def swap_cores(block):
    return lax.ppermute(block, "c", [(0, 1), (1, 0)])


def narrow(block):
    return (block * 32.0).astype(jnp.float16)


def widen(block):
    return block.astype(F32) * (1.0 / 32.0)


def together(*arrays):
    return lax.optimization_barrier(arrays)


def body(image_embed, text_embed, log_scale, logit_bias):
    width = image_embed.shape[1]
    scalars = jnp.stack([jnp.exp(log_scale[0]), logit_bias[0]])
    core = jnp.reshape(lax.axis_index("c"), (1,))
    first = lax.axis_index("c") == 0
    i0, t0 = image_embed, text_embed
    block = ((ROWS, width), F32)

    t0x, ib, ia, t1, s0 = together(swap_cores(t0), move(i0, down), move(i0, up), move(t0, inner), move(t0, outer))

    s1 = move(jnp.where(first, t1, s0), outer, inner)
    i2 = move(jnp.where(first, ia, ib), up, down)
    t1x, s0x = swap_cores(t1), swap_cores(s0)
    images, texts, image_inverse, text_inverse, loss, ht0, ht1, hs0, htx, hi = call(
        near,
        (((3 * ROWS, width), BF16), ((6 * ROWS, width), BF16), ((3 * ROWS, 128), F32), ((8, 6 * ROWS), F32),
         ((8, 128), F32), block, block, block, ((3 * ROWS, width), F32), ((3 * ROWS, width), F32)),
        8.0, 26, scalars, i0, ia, ib, t0, t1, s0, t0x, t1x, s0x, scratch=(pltpu.VMEM((3 * ROWS, 6 * ROWS), BF16),))
    s1, i2, loss = together(s1, i2, loss)
    sx = swap_cores(s1)
    loss, by_near_text, by_near_image, by_far_text, by_far_image, four, pair = call(
        far,
        (((8, 128), F32), ((ROWS, 6 * ROWS), BF16), ((ROWS, 6 * ROWS), BF16), ((4 * ROWS, 2 * ROWS), BF16),
         ((4 * ROWS, 2 * ROWS), BF16), ((4 * ROWS, width), BF16), ((2 * ROWS, width), BF16)),
        2.0, 16, scalars, i2, s1, sx, images, texts, image_inverse, text_inverse, loss)
    loss_c = swap_cores(loss)
    own_text, own_image, blocks = call(
        sums, (block, block, ((13 * ROWS, width), F32)), 4.0, 28, core,
        by_near_text, by_near_image, by_far_text, by_far_image, i2, four, pair, texts, ht0, ht1, hs0, htx, hi)
    loss = loss + loss_c
    blocks, loss = together(blocks, loss)
    other = swap_cores(narrow(blocks[:7 * ROWS]))
    loss = loss + move(loss, inner)
    other, loss = together(other, loss)
    own_text = own_text + widen(other[:ROWS])
    outs = [
        narrow(blocks[n * ROWS:(n + 2) * ROWS] + widen(other[(n - 6) * ROWS:(n - 4) * ROWS])) for n in (7, 9, 11)]
    back = (
        move(outs[0], inner, down),
        move(outs[1], outer_back, up),
        move(outs[2], far_back, across))
    loss, = call(everyone, (((64, 128), F32),), 20.0, 8, loss)
    loss = lax.all_to_all(loss, ("z", "xh", "y"), 0, 0, tiled=True)
    *back, loss = together(*back, loss)
    back = sum(widen(part) for part in back)
    stay = jnp.where(first, back[:ROWS], back[ROWS:])
    swapped = widen(swap_cores(narrow(jnp.where(first, back[ROWS:], back[:ROWS]))))
    text_hat = own_text + jnp.where(first, stay, swapped)
    image_hat = own_image + jnp.where(first, swapped, stay)
    image_grad, = call(finish, (block,), 20.0, 8, scalars, image_embed, image_hat)
    text_grad, loss = call(finish, (block, ((1,), F32)), 20.0, 8, scalars, text_embed, text_hat, loss)
    return loss, image_grad, text_grad


def solution(mesh):
    grid = Mesh(mesh.devices.reshape(SHAPE), AXES)
    rows = P(AXES, None)
    return jax.shard_map(
        body, mesh=grid, in_specs=(rows, rows, P(), P()), out_specs=(P(), rows, rows), check_vma=False)
```

time: 357 us -> 73.3 us (0.21)
  waiting for transfers between devices: 212 us -> 15.2 us
  blocking collectives: 78.1 us -> 16.8 us
  matrix products: 28 us -> 0 us
  between operations: 18.2 us -> 2.27 us
  Pallas kernels: 0 us -> 12.7 us
  starting transfers between devices: 11.7 us -> 24.3 us
  other arithmetic: 7.41 us -> 1.9 us
    reduce_scatter x2 -> x0, waiting for transfers between devices: 140 us -> none  [body(): lax.psum_scatter(update, 'mp', scatter_dimension=0, tiled=True)]
    psum x1 -> x0, blocking collectives: 78.1 us -> none  [body(): whole_total = lax.psum(total, ('dp', 'mp'))]
    all_gather x2 -> x0, waiting for transfers between devices: 59.6 us -> none  [body(): piece = lax.all_gather(text_now, 'mp', axis=0, tiled=True)]
    dot_general x6 -> x0, matrix products: 28 us -> none  [the longest x2 10.4 us: body(): lax.dot_general(coef, image_low, (((0,), (0,)), ((), ())), preferred_elem...]
    all_to_all x0 -> x1, blocking collectives: none -> 16.8 us  [body(): loss = lax.all_to_all(loss, ('z', 'xh', 'y'), 0, 0, tiled=True)]
    ppermute x3 -> x17, starting transfers between devices: 11.5 us -> 24.3 us  [the longest x7 12.2 us: swap_cores(): return lax.ppermute(block, 'c', [(0, 1), (1, 0)])]
    pallas_call x0 -> x6, Pallas kernels: none -> 12.7 us  [call(): pl.pallas_call(kernel, out_shape=shapes, in_specs=[SMEM if a.ndim == 1 el...]
    ppermute x3 -> x17, waiting for transfers between devices: 12.2 us -> 15.2 us  [the longest x10 11.2 us: move(): return lax.ppermute(block, AXES, route)]
  transfers between devices with their start and end apart: 7 -> 17, of which waited for: 5 -> 6; matrix products, arithmetic and copies ran while one was open for 8% -> 0% of each run, Pallas kernels for 0% -> 10%
where the time goes in v3:
time: 73.3 us; the launch traced here: 73.1 us
  starting transfers between devices  24.3 us (33%)
  blocking collectives  16.8 us (23%)
  waiting for transfers between devices  15.2 us (21%)
  Pallas kernels  12.7 us (17%)
  between operations  2.27 us (3%)
  other arithmetic  1.9 us (3%)
    all_to_all x1, blocking collectives, body(): loss = lax.all_to_all(loss, ('z', 'xh', 'y'), 0, 0, tiled=True)  16.8 us
    pallas_call x6, Pallas kernels, call(): pl.pallas_call(kernel, out_shape=shapes, in_specs=[SMEM if a.ndim == 1 el...  12.7 us
    ppermute x7, starting transfers between devices, swap_cores(): return lax.ppermute(block, 'c', [(0, 1), (1, 0)])  12.2 us
    ppermute x10, starting transfers between devices, move(): return lax.ppermute(block, AXES, route)  12.1 us
    ppermute x10, waiting for transfers between devices, move(): return lax.ppermute(block, AXES, route)  11.2 us
    ppermute x7, waiting for transfers between devices, swap_cores(): return lax.ppermute(block, 'c', [(0, 1), (1, 0)])  3.95 us
  transfers between devices with their start and end apart: 17, of which 6 were waited for; matrix products, arithmetic and copies ran while one was open for 0% of the time, Pallas kernels for 10%

profile of v3, /device:TPU:1, one launch (start us, length us, event | category | flops | bytes accessed | tf_op | source)
XLA Modules:
  0.0 73.1 jit_solution(6995168931190774156)
XLA Ops:
  0.6 0.0 copy-start
  0.6 0.0 copy-start.1
  0.7 2.2 %collective-permute-start.2 = (bf16[128,1152]{1,0:T(8,128)(2,1)}, bf16[128,1152]{1,0:T(8,128)(2,1)S(1)}, u32[]{:S(2)}, u32[]{:S(2)}) collective-permute-start(bf16[128,1152]{1,0:T(8,128)(2,1)} %raw.3), channel_id=1, source_target_pairs={{0,2},{1,3},{2,4},{3,5},{4,6},{5,7},{6,0},{7,1},{8,10},{9,11},{10,... | collective-permute-start | bytes 884744 | tf_op jit(solution)/shard_map/ppermute | solution.py:206
  2.9 1.5 %collective-permute-start.1 = (bf16[128,1152]{1,0:T(8,128)(2,1)}, bf16[128,1152]{1,0:T(8,128)(2,1)S(1)}, u32[]{:S(2)}, u32[]{:S(2)}) collective-permute-start(bf16[128,1152]{1,0:T(8,128)(2,1)} %raw.3), channel_id=1, source_target_pairs={{0,6},{1,7},{2,0},{3,1},{4,2},{5,3},{6,4},{7,5},{8,14},{9,15},{10,... | collective-permute-start | bytes 884744 | tf_op jit(solution)/shard_map/ppermute | solution.py:206
  4.4 2.5 %collective-permute-start.4 = (bf16[128,1152]{1,0:T(8,128)(2,1)}, bf16[128,1152]{1,0:T(8,128)(2,1)S(1)}, u32[]{:S(2)}, u32[]{:S(2)}) collective-permute-start(bf16[128,1152]{1,0:T(8,128)(2,1)} %raw.2), channel_id=1, source_target_pairs={{0,24},{1,25},{2,26},{3,27},{4,28},{5,29},{6,30},{7,31},{8,16},{9,... | collective-permute-start | bytes 884744 | tf_op jit(solution)/shard_map/ppermute | solution.py:206
  6.9 0.0 collective-permute-start.3
  6.9 1.6 %collective-permute-start = (bf16[128,1152]{1,0:T(8,128)(2,1)}, bf16[128,1152]{1,0:T(8,128)(2,1)S(1)}, u32[]{:S(2)}, u32[]{:S(2)}) collective-permute-start(bf16[128,1152]{1,0:T(8,128)(2,1)} %raw.2), channel_id=1, source_target_pairs={{0,1},{1,0},{2,3},{3,2},{4,5},{5,4},{6,7},{7,6},{8,9},{9,8},{10,11... | collective-permute-start | bytes 884744 | tf_op jit(solution)/shard_map/ppermute | solution.py:210
  9.8 0.1 pad_maximum_fusion.scalar_ref
  9.9 0.0 collective-permute-done.2.ia
  9.9 0.5 collective-permute-done.1.ib
  10.4 8.3 %collective-permute-done.4.s0 = bf16[128,1152]{1,0:T(8,128)(2,1)S(1)} collective-permute-done((bf16[128,1152]{1,0:T(8,128)(2,1)}, bf16[128,1152]{1,0:T(8,128)(2,1)S(1)}, u32[]{:S(2)}, u32[]{:S(2)}) %collective-permute-start.4) | collective-permute-done | bytes 294944 | tf_op jit(solution)/shard_map/ppermute | solution.py:206
  18.6 0.0 collective-permute-done.3.t1
  18.6 0.0 collective-permute-done.t0x
  18.6 1.7 %collective-permute-start.7 = (bf16[128,1152]{1,0:T(8,128)(2,1)S(1)}, bf16[128,1152]{1,0:T(8,128)(2,1)S(1)}, u32[]{:S(2)}, u32[]{:S(2)}) collective-permute-start(bf16[128,1152]{1,0:T(8,128)(2,1)S(1)} %collective-permute-done.3.t1), channel_id=1, source_target_pairs={{0,1},{1,0},{2,3},{3,2},{4,5},{5,4},{6,7},{7,6},{8,9},{9,8},{10,11... | collective-permute-start | bytes 884744 | tf_op jit(solution)/shard_map/ppermute | solution.py:210
  20.3 0.1 collective-permute-start.8
  20.5 0.1 collective-permute-start.5
  20.6 1.5 %collective-permute-start.6 = (bf16[128,1152]{1,0:T(8,128)(2,1)S(1)}, bf16[128,1152]{1,0:T(8,128)(2,1)S(1)}, u32[]{:S(2)}, u32[]{:S(2)}) collective-permute-start(bf16[128,1152]{1,0:T(8,128)(2,1)S(1)} %broadcast_select_fusion), channel_id=1, source_target_pairs={{0,2},{1,7},{2,4},{3,1},{4,6},{5,3},{6,0},{7,5},{8,10},{9,15},{10,... | collective-permute-start | bytes 884744 | tf_op jit(solution)/shard_map/ppermute | solution.py:206
  22.1 0.0 collective-permute-done.7.t1x
  22.1 0.0 collective-permute-done.8.s0x
  22.1 5.1 %near.1 = (bf16[384,1152]{1,0:T(8,128)(2,1)S(1)}, bf16[768,1152]{1,0:T(8,128)(2,1)S(1)}, f32[384,128]{1,0:T(8,128)S(1)}, f32[8,768]{1,0:T(8,128)S(1)}, f32[8,128...) custom-call(f32[2]{0:T(128)S(1)} %pad_maximum_fusion.scalar_ref, ...), custom_call_target="tpu_custom_call" | custom-call | flops 8000000000 | bytes 24000000 | tf_op jit(solution)/shard_map/near/pallas_call | solution.py:21
  27.2 0.0 collective-permute-done.5.s1
  27.2 0.0 collective-permute-done.6.i2
  27.2 3.8 %collective-permute-start.9 = (bf16[128,1152]{1,0:T(8,128)(2,1)S(1)}, bf16[128,1152]{1,0:T(8,128)(2,1)S(1)}, u32[]{:S(2)}, u32[]{:S(2)}) collective-permute-start(bf16[128,1152]{1,0:T(8,128)(2,1)S(1)} %collective-permute-done.5.s1), channel_id=1, source_target_pairs={{0,1},{1,0},{2,3},{3,2},{4,5},{5,4},{6,7},{7,6},{8,9},{9,8},{10,11... | collective-permute-start | bytes 884744 | tf_op jit(solution)/shard_map/ppermute | solution.py:210
  31.0 1.2 %collective-permute-done.9.sx = bf16[128,1152]{1,0:T(8,128)(2,1)S(1)} collective-permute-done((bf16[128,1152]{1,0:T(8,128)(2,1)S(1)}, bf16[128,1152]{1,0:T(8,128)(2,1)S(1)}, u32[]{:S(2)}, u32[]{:S(2)}) %collective-permute-start.9) | collective-permute-done | bytes 294944 | tf_op jit(solution)/shard_map/ppermute | solution.py:210
  32.2 2.3 %far.1 = (f32[8,128]{1,0:T(8,128)S(1)}, bf16[128,768]{1,0:T(8,128)(2,1)S(1)}, bf16[128,768]{1,0:T(8,128)(2,1)S(1)}, bf16[512,256]{1,0:T(8,128)(2,1)S(1)}, bf16[5...) custom-call(f32[2]{0:T(128)S(1)} %pad_maximum_fusion.scalar_ref, ...), custom_call_target="tpu_custom_call" | custom-call | flops 2000000000 | bytes 6000000 | tf_op jit(solution)/shard_map/far/pallas_call | solution.py:21
  34.6 0.5 collective-permute-start.10
  35.0 1.9 %sums.1 = (f32[128,1152]{1,0:T(8,128)S(1)}, f32[128,1152]{1,0:T(8,128)S(1)}, f32[1664,1152]{1,0:T(8,128)S(1)}) custom-call(s32[1]{0:T(128)} %bitcast.core_ref, bf16[128,768]{1,0:T(8,128)(2,1)S(1)} %get-tuple-element.54.by_near_text, bf16[128,768]{1,0:T(8,128)(2,1)S(1)} %get-tuple-element.55.by_near_image, ...), custom_call_target="tpu_custom_call" | custom-call | flops 4000000000 | bytes 12000000 | tf_op jit(solution)/shard_map/sums/pallas_call | solution.py:21
  37.0 0.0 collective-permute-done.10
  37.0 0.4 multiply_convert_fusion
  37.4 0.2 collective-permute-start.11
  37.6 0.0 collective-permute-start.12
  37.6 2.5 %collective-permute-done.12 = f32[8,128]{1,0:T(8,128)S(1)} collective-permute-done((f32[8,128]{1,0:T(8,128)S(1)}, f32[8,128]{1,0:T(8,128)S(1)}, u32[]{:S(2)}, u32[]{:S(2)}) %collective-permute-start.12) | collective-permute-done | bytes 4128 | tf_op jit(solution)/shard_map/ppermute | solution.py:206
  40.1 1.5 %collective-permute-done.11 = f16[896,1152]{1,0:T(8,128)(2,1)S(1)} collective-permute-done((f16[896,1152]{1,0:T(8,128)(2,1)S(1)}, f16[896,1152]{1,0:T(8,128)(2,1)S(1)}, u32[]{:S(2)}, u32[]{:S(2)}) %collective-permute-start.11) | collective-permute-done | bytes 2064416 | tf_op jit(solution)/shard_map/ppermute | solution.py:210
  41.6 0.8 %multiply_convert_fusion.1 = (f16[256,1152]{1,0:T(8,128)(2,1)S(1)}, f16[256,1152]{1,0:T(8,128)(2,1)S(1)}, f16[256,1152]{1,0:T(8,128)(2,1)S(1)}) fusion(f32[1664,1152]{1,0:T(8,128)S(1)} %get-tuple-element.68, f16[896,1152]{1,0:T(8,128)(2,1)S(1)} %collective-permute-done.11), kind=kLoop, calls=%fused_computation.2 | loop fusion | flops 4423680 | bytes 7077888 | tf_op jit(solution)/shard_map/convert_element_type | solution.py:214
  42.4 1.6 %collective-permute-start.15 = (f16[256,1152]{1,0:T(8,128)(2,1)S(1)}, f16[256,1152]{1,0:T(8,128)(2,1)S(1)}, u32[]{:S(2)}, u32[]{:S(2)}) collective-permute-start(f16[256,1152]{1,0:T(8,128)(2,1)S(1)} %get-tuple-element.79), channel_id=1, source_target_pairs={{0,240},{1,5},{2,242},{3,7},{4,244},{5,1},{6,246},{7,3},{8,248},{9... | collective-permute-start | bytes 1769480 | tf_op jit(solution)/shard_map/ppermute | solution.py:206
  44.0 0.4 collective-permute-start.14
  44.4 2.3 %collective-permute-start.13 = (f16[256,1152]{1,0:T(8,128)(2,1)S(1)}, f16[256,1152]{1,0:T(8,128)(2,1)S(1)}, u32[]{:S(2)}, u32[]{:S(2)}) collective-permute-start(f16[256,1152]{1,0:T(8,128)(2,1)S(1)} %get-tuple-element.81), channel_id=1, source_target_pairs={{0,8},{1,7},{2,10},{3,1},{4,12},{5,3},{6,14},{7,5},{8,0},{9,15},{1... | collective-permute-start | bytes 1769480 | tf_op jit(solution)/shard_map/ppermute | solution.py:206
  46.7 16.8 %all_to_all.12 = f32[64,1,128]{2,1,0:T(1,128)S(1)} all-to-all(f32[64,1,128]{2,1,0:T(1,128)S(1)} %bitcast.6), channel_id=1, replica_groups=mesh['z'=8,'xh'=2,'xl'=2,'y'=4,'c'=2] {'z','xh','y'}, dimensions={0} | all-to-all | bytes 65536 | tf_op jit(solution)/shard_map/all_to_all | solution.py:267
  63.5 0.0 collective-permute-done.15
  63.5 0.0 collective-permute-done.14
  63.5 0.0 collective-permute-done.13
  63.5 0.2 add_multiply_fusion
  63.7 0.1 multiply_convert_fusion.4
  63.8 4.4 %collective-permute-start.16 = (f16[128,1152]{1,0:T(8,128)(2,1)S(1)}, f16[128,1152]{1,0:T(8,128)(2,1)S(1)}, u32[]{:S(2)}, u32[]{:S(2)}) collective-permute-start(f16[128,1152]{1,0:T(8,128)(2,1)S(1)} %multiply_convert_fusion.4), channel_id=1, source_target_pairs={{0,1},{1,0},{2,3},{3,2},{4,5},{5,4},{6,7},{7,6},{8,9},{9,8},{10,11... | collective-permute-start | bytes 884744 | tf_op jit(solution)/shard_map/ppermute | solution.py:210
  68.2 1.2 %collective-permute-done.16 = f16[128,1152]{1,0:T(8,128)(2,1)S(1)} collective-permute-done((f16[128,1152]{1,0:T(8,128)(2,1)S(1)}, f16[128,1152]{1,0:T(8,128)(2,1)S(1)}, u32[]{:S(2)}, u32[]{:S(2)}) %collective-permute-start.16) | collective-permute-done | bytes 294944 | tf_op jit(solution)/shard_map/ppermute | solution.py:210
  69.5 0.2 select_add_fusion
  69.7 1.6 %finish.3 = f32[128,1152]{1,0:T(8,128)} custom-call(f32[2]{0:T(128)S(1)} %pad_maximum_fusion.scalar_ref, bf16[128,1152]{1,0:T(8,128)(2,1)S(1)} %copy-done, f32[128,1152]{1,0:T(8,128)S(1)} %get-tuple-element.82.hat_ref), custom_call_target="tpu_custom_call" | custom-call | flops 20000000000 | bytes 60000000 | tf_op jit(solution)/shard_map/finish/pallas_call | solution.py:21
  71.3 1.6 %finish.2 = (f32[128,1152]{1,0:T(8,128)}, f32[1]{0:T(128)}) custom-call(f32[2]{0:T(128)S(1)} %pad_maximum_fusion.scalar_ref, bf16[128,1152]{1,0:T(8,128)(2,1)S(1)} %copy-done.1, f32[128,1152]{1,0:T(8,128)S(1)} %get-tuple-element.83.hat_ref, f32[64,128]{1,0:T(8,128)S(1)} %bitcast.5), custom_call_target="tpu_custom_call" | custom-call | flops 20000000000 | bytes 60000000 | tf_op jit(solution)/shard_map/finish/pallas_call | solution.py:21
  (7 shorter events, 0.1 us)
Async XLA Ops:
  0.6 21.4 %copy-start = (bf16[128,1152]{1,0:T(8,128)(2,1)S(1)}, bf16[128,1152]{1,0:T(8,128)(2,1)}, u32[]{:S(2)}) copy-start(bf16[128,1152]{1,0:T(8,128)(2,1)} %raw.3) | copy-start | bytes 884740
  0.6 21.4 %copy-start.1 = (bf16[128,1152]{1,0:T(8,128)(2,1)S(1)}, bf16[128,1152]{1,0:T(8,128)(2,1)}, u32[]{:S(2)}) copy-start(bf16[128,1152]{1,0:T(8,128)(2,1)} %raw.2) | copy-start | bytes 884740
  0.7 9.2 %collective-permute-start.2 = (bf16[128,1152]{1,0:T(8,128)(2,1)}, bf16[128,1152]{1,0:T(8,128)(2,1)S(1)}, u32[]{:S(2)}, u32[]{:S(2)}) collective-permute-start(bf16[128,1152]{1,0:T(8,128)(2,1)} %raw.3), channel_id=1, source_target_pairs={{0,2},{1,3},{2,4},{3,5},{4,6},{5,7},{6,0},{7,1},{8,10},{9,11},{10,... | collective-permute-start | bytes 884744 | tf_op jit(solution)/shard_map/ppermute | solution.py:206
  2.9 7.5 %collective-permute-start.1 = (bf16[128,1152]{1,0:T(8,128)(2,1)}, bf16[128,1152]{1,0:T(8,128)(2,1)S(1)}, u32[]{:S(2)}, u32[]{:S(2)}) collective-permute-start(bf16[128,1152]{1,0:T(8,128)(2,1)} %raw.3), channel_id=1, source_target_pairs={{0,6},{1,7},{2,0},{3,1},{4,2},{5,3},{6,4},{7,5},{8,14},{9,15},{10,... | collective-permute-start | bytes 884744 | tf_op jit(solution)/shard_map/ppermute | solution.py:206
  4.4 14.2 %collective-permute-start.4 = (bf16[128,1152]{1,0:T(8,128)(2,1)}, bf16[128,1152]{1,0:T(8,128)(2,1)S(1)}, u32[]{:S(2)}, u32[]{:S(2)}) collective-permute-start(bf16[128,1152]{1,0:T(8,128)(2,1)} %raw.2), channel_id=1, source_target_pairs={{0,24},{1,25},{2,26},{3,27},{4,28},{5,29},{6,30},{7,31},{8,16},{9,... | collective-permute-start | bytes 884744 | tf_op jit(solution)/shard_map/ppermute | solution.py:206
  6.9 11.8 %collective-permute-start.3 = (bf16[128,1152]{1,0:T(8,128)(2,1)}, bf16[128,1152]{1,0:T(8,128)(2,1)S(1)}, u32[]{:S(2)}, u32[]{:S(2)}) collective-permute-start(bf16[128,1152]{1,0:T(8,128)(2,1)} %raw.2), channel_id=1, source_target_pairs={{0,8},{1,9},{2,10},{3,11},{4,12},{5,13},{6,14},{7,15},{8,0},{9,1},... | collective-permute-start | bytes 884744 | tf_op jit(solution)/shard_map/ppermute | solution.py:206
  6.9 11.8 %collective-permute-start = (bf16[128,1152]{1,0:T(8,128)(2,1)}, bf16[128,1152]{1,0:T(8,128)(2,1)S(1)}, u32[]{:S(2)}, u32[]{:S(2)}) collective-permute-start(bf16[128,1152]{1,0:T(8,128)(2,1)} %raw.2), channel_id=1, source_target_pairs={{0,1},{1,0},{2,3},{3,2},{4,5},{5,4},{6,7},{7,6},{8,9},{9,8},{10,11... | collective-permute-start | bytes 884744 | tf_op jit(solution)/shard_map/ppermute | solution.py:210
  18.6 3.4 %collective-permute-start.7 = (bf16[128,1152]{1,0:T(8,128)(2,1)S(1)}, bf16[128,1152]{1,0:T(8,128)(2,1)S(1)}, u32[]{:S(2)}, u32[]{:S(2)}) collective-permute-start(bf16[128,1152]{1,0:T(8,128)(2,1)S(1)} %collective-permute-done.3.t1), channel_id=1, source_target_pairs={{0,1},{1,0},{2,3},{3,2},{4,5},{5,4},{6,7},{7,6},{8,9},{9,8},{10,11... | collective-permute-start | bytes 884744 | tf_op jit(solution)/shard_map/ppermute | solution.py:210
  20.3 1.7 %collective-permute-start.8 = (bf16[128,1152]{1,0:T(8,128)(2,1)S(1)}, bf16[128,1152]{1,0:T(8,128)(2,1)S(1)}, u32[]{:S(2)}, u32[]{:S(2)}) collective-permute-start(bf16[128,1152]{1,0:T(8,128)(2,1)S(1)} %collective-permute-done.4.s0), channel_id=1, source_target_pairs={{0,1},{1,0},{2,3},{3,2},{4,5},{5,4},{6,7},{7,6},{8,9},{9,8},{10,11... | collective-permute-start | bytes 884744 | tf_op jit(solution)/shard_map/ppermute | solution.py:210
  20.5 6.8 %collective-permute-start.5 = (bf16[128,1152]{1,0:T(8,128)(2,1)S(1)}, bf16[128,1152]{1,0:T(8,128)(2,1)S(1)}, u32[]{:S(2)}, u32[]{:S(2)}) collective-permute-start(bf16[128,1152]{1,0:T(8,128)(2,1)S(1)} %broadcast_select_fusion.1), channel_id=1, source_target_pairs={{0,24},{1,9},{2,26},{3,11},{4,28},{5,13},{6,30},{7,15},{8,16},{9,1... | collective-permute-start | bytes 884744 | tf_op jit(solution)/shard_map/ppermute | solution.py:206
  20.6 6.6 %collective-permute-start.6 = (bf16[128,1152]{1,0:T(8,128)(2,1)S(1)}, bf16[128,1152]{1,0:T(8,128)(2,1)S(1)}, u32[]{:S(2)}, u32[]{:S(2)}) collective-permute-start(bf16[128,1152]{1,0:T(8,128)(2,1)S(1)} %broadcast_select_fusion), channel_id=1, source_target_pairs={{0,2},{1,7},{2,4},{3,1},{4,6},{5,3},{6,0},{7,5},{8,10},{9,15},{10,... | collective-permute-start | bytes 884744 | tf_op jit(solution)/shard_map/ppermute | solution.py:206
  27.2 5.0 %collective-permute-start.9 = (bf16[128,1152]{1,0:T(8,128)(2,1)S(1)}, bf16[128,1152]{1,0:T(8,128)(2,1)S(1)}, u32[]{:S(2)}, u32[]{:S(2)}) collective-permute-start(bf16[128,1152]{1,0:T(8,128)(2,1)S(1)} %collective-permute-done.5.s1), channel_id=1, source_target_pairs={{0,1},{1,0},{2,3},{3,2},{4,5},{5,4},{6,7},{7,6},{8,9},{9,8},{10,11... | collective-permute-start | bytes 884744 | tf_op jit(solution)/shard_map/ppermute | solution.py:210
  34.6 2.4 %collective-permute-start.10 = (f32[8,128]{1,0:T(8,128)S(1)}, f32[8,128]{1,0:T(8,128)S(1)}, u32[]{:S(2)}, u32[]{:S(2)}) collective-permute-start(f32[8,128]{1,0:T(8,128)S(1)} %get-tuple-element.67), channel_id=1, source_target_pairs={{0,1},{1,0},{2,3},{3,2},{4,5},{5,4},{6,7},{7,6},{8,9},{9,8},{10,11... | collective-permute-start | bytes 12296 | tf_op jit(solution)/shard_map/ppermute | solution.py:210
  37.4 4.2 %collective-permute-start.11 = (f16[896,1152]{1,0:T(8,128)(2,1)S(1)}, f16[896,1152]{1,0:T(8,128)(2,1)S(1)}, u32[]{:S(2)}, u32[]{:S(2)}) collective-permute-start(f16[896,1152]{1,0:T(8,128)(2,1)S(1)} %multiply_convert_fusion), channel_id=1, source_target_pairs={{0,1},{1,0},{2,3},{3,2},{4,5},{5,4},{6,7},{7,6},{8,9},{9,8},{10,11... | collective-permute-start | bytes 6193160 | tf_op jit(solution)/shard_map/ppermute | solution.py:210
  37.6 2.5 %collective-permute-start.12 = (f32[8,128]{1,0:T(8,128)S(1)}, f32[8,128]{1,0:T(8,128)S(1)}, u32[]{:S(2)}, u32[]{:S(2)}) collective-permute-start(f32[8,128]{1,0:T(8,128)S(1)} %add.32), channel_id=1, source_target_pairs={{0,8},{1,9},{2,10},{3,11},{4,12},{5,13},{6,14},{7,15},{8,0},{9,1},... | collective-permute-start | bytes 12296 | tf_op jit(solution)/shard_map/ppermute | solution.py:206
  42.4 21.1 %collective-permute-start.15 = (f16[256,1152]{1,0:T(8,128)(2,1)S(1)}, f16[256,1152]{1,0:T(8,128)(2,1)S(1)}, u32[]{:S(2)}, u32[]{:S(2)}) collective-permute-start(f16[256,1152]{1,0:T(8,128)(2,1)S(1)} %get-tuple-element.79), channel_id=1, source_target_pairs={{0,240},{1,5},{2,242},{3,7},{4,244},{5,1},{6,246},{7,3},{8,248},{9... | collective-permute-start | bytes 1769480 | tf_op jit(solution)/shard_map/ppermute | solution.py:206
  44.0 19.5 %collective-permute-start.14 = (f16[256,1152]{1,0:T(8,128)(2,1)S(1)}, f16[256,1152]{1,0:T(8,128)(2,1)S(1)}, u32[]{:S(2)}, u32[]{:S(2)}) collective-permute-start(f16[256,1152]{1,0:T(8,128)(2,1)S(1)} %get-tuple-element.80), channel_id=1, source_target_pairs={{0,248},{1,3},{2,250},{3,5},{4,252},{5,7},{6,254},{7,1},{8,240},{9... | collective-permute-start | bytes 1769480 | tf_op jit(solution)/shard_map/ppermute | solution.py:206
  44.4 19.1 %collective-permute-start.13 = (f16[256,1152]{1,0:T(8,128)(2,1)S(1)}, f16[256,1152]{1,0:T(8,128)(2,1)S(1)}, u32[]{:S(2)}, u32[]{:S(2)}) collective-permute-start(f16[256,1152]{1,0:T(8,128)(2,1)S(1)} %get-tuple-element.81), channel_id=1, source_target_pairs={{0,8},{1,7},{2,10},{3,1},{4,12},{5,3},{6,14},{7,5},{8,0},{9,15},{1... | collective-permute-start | bytes 1769480 | tf_op jit(solution)/shard_map/ppermute | solution.py:206
  63.8 5.6 %collective-permute-start.16 = (f16[128,1152]{1,0:T(8,128)(2,1)S(1)}, f16[128,1152]{1,0:T(8,128)(2,1)S(1)}, u32[]{:S(2)}, u32[]{:S(2)}) collective-permute-start(f16[128,1152]{1,0:T(8,128)(2,1)S(1)} %multiply_convert_fusion.4), channel_id=1, source_target_pairs={{0,1},{1,0},{2,3},{3,2},{4,5},{5,4},{6,7},{7,6},{8,9},{9,8},{10,11... | collective-permute-start | bytes 884744 | tf_op jit(solution)/shard_map/ppermute | solution.py:210

commit v4 on v3

--- a/solution.py
+++ b/solution.py
@@ -156,16 +156,13 @@
     out[...] = jnp.broadcast_to(jnp.sum(loss[...], axis=0, keepdims=True), out.shape)
 
 
-def finish(scalar_ref, raw, hat_ref, *rest):
-    if len(rest) == 3:
-        parts, out, loss = rest
-        loss[0] = jnp.sum(parts[...]) / (ROWS * 256 * STEPS * ROWS * 16)
-    else:
-        out, = rest
-    inverse = inverse_norm(raw[...])
-    unit = raw[...].astype(F32) * inverse
-    hat = scalar_ref[0] * hat_ref[...]
-    out[...] = (hat - unit * jnp.sum(unit * hat, axis=1, keepdims=True)) * inverse
+def finish(scalar_ref, image, text, image_hat, text_hat, parts, image_grad, text_grad, loss):
+    for raw, hat_ref, out in ((image, image_hat, image_grad), (text, text_hat, text_grad)):
+        inverse = inverse_norm(raw[...])
+        unit = raw[...].astype(F32) * inverse
+        hat = scalar_ref[0] * hat_ref[...]
+        out[...] = (hat - unit * jnp.sum(unit * hat, axis=1, keepdims=True)) * inverse
+    loss[0] = jnp.sum(parts[...]) / (ROWS * 256 * STEPS * ROWS * 16)
 
 
 def inner(group, side, y):
@@ -230,11 +227,13 @@
     i0, t0 = image_embed, text_embed
     block = ((ROWS, width), F32)
 
-    t0x, ib, ia, t1, s0 = together(swap_cores(t0), move(i0, down), move(i0, up), move(t0, inner), move(t0, outer))
-
+    s0, t1 = move(t0, outer), move(t0, inner)
+    ia, ib, t0x = move(i0, up), move(i0, down), swap_cores(t0)
+    s0x, t1x = swap_cores(s0), swap_cores(t1)
+    s0, t1 = together(s0, t1)
     s1 = move(jnp.where(first, t1, s0), outer, inner)
+    ia, ib, t0x, s0x, t1x = together(ia, ib, t0x, s0x, t1x)
     i2 = move(jnp.where(first, ia, ib), up, down)
-    t1x, s0x = swap_cores(t1), swap_cores(s0)
     images, texts, image_inverse, text_inverse, loss, ht0, ht1, hs0, htx, hi = call(
         near,
         (((3 * ROWS, width), BF16), ((6 * ROWS, width), BF16), ((3 * ROWS, 128), F32), ((8, 6 * ROWS), F32),
@@ -247,15 +246,17 @@
         (((8, 128), F32), ((ROWS, 6 * ROWS), BF16), ((ROWS, 6 * ROWS), BF16), ((4 * ROWS, 2 * ROWS), BF16),
          ((4 * ROWS, 2 * ROWS), BF16), ((4 * ROWS, width), BF16), ((2 * ROWS, width), BF16)),
         2.0, 16, scalars, i2, s1, sx, images, texts, image_inverse, text_inverse, loss)
-    loss_c = swap_cores(loss)
+    loss_y = lax.ppermute(loss, "y", [(i, i ^ 1) for i in range(4)])
     own_text, own_image, blocks = call(
         sums, (block, block, ((13 * ROWS, width), F32)), 4.0, 28, core,
         by_near_text, by_near_image, by_far_text, by_far_image, i2, four, pair, texts, ht0, ht1, hs0, htx, hi)
-    loss = loss + loss_c
+    loss = loss + loss_y
     blocks, loss = together(blocks, loss)
-    other = swap_cores(narrow(blocks[:7 * ROWS]))
+    message = narrow(blocks[:7 * ROWS])
+    other = swap_cores(message)
     loss = loss + move(loss, inner)
     other, loss = together(other, loss)
+    loss = loss + lax.ppermute(loss, "y", [(i, i ^ 2) for i in range(4)])
     own_text = own_text + widen(other[:ROWS])
     outs = [
         narrow(blocks[n * ROWS:(n + 2) * ROWS] + widen(other[(n - 6) * ROWS:(n - 4) * ROWS])) for n in (7, 9, 11)]
@@ -263,16 +264,17 @@
         move(outs[0], inner, down),
         move(outs[1], outer_back, up),
         move(outs[2], far_back, across))
-    loss, = call(everyone, (((64, 128), F32),), 20.0, 8, loss)
-    loss = lax.all_to_all(loss, ("z", "xh", "y"), 0, 0, tiled=True)
+    loss, = call(everyone, (((16, 128), F32),), 20.0, 4, loss)
+    loss = lax.all_to_all(loss, ("z", "xh"), 0, 0, tiled=True)
     *back, loss = together(*back, loss)
     back = sum(widen(part) for part in back)
     stay = jnp.where(first, back[:ROWS], back[ROWS:])
     swapped = widen(swap_cores(narrow(jnp.where(first, back[ROWS:], back[:ROWS]))))
+    loss = loss + swap_cores(loss)
     text_hat = own_text + jnp.where(first, stay, swapped)
     image_hat = own_image + jnp.where(first, swapped, stay)
-    image_grad, = call(finish, (block,), 20.0, 8, scalars, image_embed, image_hat)
-    text_grad, loss = call(finish, (block, ((1,), F32)), 20.0, 8, scalars, text_embed, text_hat, loss)
+    image_grad, text_grad, loss = call(
+        finish, (block, block, ((1,), F32)), 20.0, 12, scalars, image_embed, text_embed, image_hat, text_hat, loss)
     return loss, image_grad, text_grad
 
 

time: 73.3 us -> 70.5 us (0.962)
  starting transfers between devices: 24.3 us -> 26.6 us
  blocking collectives: 16.8 us -> 14.7 us
  waiting for transfers between devices: 15.2 us -> 13.5 us
  Pallas kernels: 12.7 us -> 11.4 us
    ppermute x0 -> x2, starting transfers between devices: none -> 4.3 us  [the longest x1 2.92 us: body(): loss = loss + lax.ppermute(loss, 'y', [(i, i ^ 2) for i in range(4)])]
    ppermute x7, starting transfers between devices: 12.2 us -> 9.57 us  [swap_cores(): return lax.ppermute(block, 'c', [(0, 1), (1, 0)])]
    ppermute x10, waiting for transfers between devices: 11.2 us -> 8.77 us  [move(): return lax.ppermute(block, AXES, route)]
    all_to_all x1, blocking collectives: 16.8 us -> 14.7 us  [body(): loss = lax.all_to_all(loss, ('z', 'xh'), 0, 0, tiled=True)]
    pallas_call x6 -> x5, Pallas kernels: 12.7 us -> 11.4 us  [call(): pl.pallas_call(kernel, out_shape=shapes, in_specs=[SMEM if a.ndim == 1 el...]
    ppermute x7, waiting for transfers between devices: 3.95 us -> 4.77 us  [swap_cores(): return lax.ppermute(block, 'c', [(0, 1), (1, 0)])]
  transfers between devices with their start and end apart: 17 -> 19, of which waited for: 6 -> 7; matrix products, arithmetic and copies ran while one was open for 0% -> 1% of each run, Pallas kernels for 10% -> 10%
where the time goes in v4:
time: 70.5 us; the launch traced here: 70.4 us
  starting transfers between devices  26.6 us (38%)
  blocking collectives  14.7 us (21%)
  waiting for transfers between devices  13.5 us (19%)
  Pallas kernels  11.4 us (16%)
  between operations  2.26 us (3%)
  other arithmetic  1.77 us (3%)
    all_to_all x1, blocking collectives, body(): loss = lax.all_to_all(loss, ('z', 'xh'), 0, 0, tiled=True)  14.7 us
    ppermute x10, starting transfers between devices, move(): return lax.ppermute(block, AXES, route)  12.8 us
    pallas_call x5, Pallas kernels, call(): pl.pallas_call(kernel, out_shape=shapes, in_specs=[SMEM if a.ndim == 1 el...  11.4 us
    ppermute x7, starting transfers between devices, swap_cores(): return lax.ppermute(block, 'c', [(0, 1), (1, 0)])  9.57 us
    ppermute x10, waiting for transfers between devices, move(): return lax.ppermute(block, AXES, route)  8.77 us
    ppermute x7, waiting for transfers between devices, swap_cores(): return lax.ppermute(block, 'c', [(0, 1), (1, 0)])  4.77 us
    ppermute x1, starting transfers between devices, body(): loss = loss + lax.ppermute(loss, 'y', [(i, i ^ 2) for i in range(4)])  2.92 us
  transfers between devices with their start and end apart: 19, of which 7 were waited for; matrix products, arithmetic and copies ran while one was open for 1% of the time, Pallas kernels for 10%

profile of v4, /device:TPU:1, one launch (start us, length us, event | category | flops | bytes accessed | tf_op | source)
XLA Modules:
  0.0 70.4 jit_solution(9955426669309675542)
XLA Ops:
  0.7 2.1 %collective-permute-start.1 = (bf16[128,1152]{1,0:T(8,128)(2,1)}, bf16[128,1152]{1,0:T(8,128)(2,1)S(1)}, u32[]{:S(2)}, u32[]{:S(2)}) collective-permute-start(bf16[128,1152]{1,0:T(8,128)(2,1)} %text.1), channel_id=1, source_target_pairs={{0,8},{1,9},{2,10},{3,11},{4,12},{5,13},{6,14},{7,15},{8,0},{9,1},... | collective-permute-start | bytes 884744 | tf_op jit(solution)/shard_map/ppermute | solution.py:203
  2.8 1.8 %collective-permute-start = (bf16[128,1152]{1,0:T(8,128)(2,1)}, bf16[128,1152]{1,0:T(8,128)(2,1)S(1)}, u32[]{:S(2)}, u32[]{:S(2)}) collective-permute-start(bf16[128,1152]{1,0:T(8,128)(2,1)} %text.1), channel_id=1, source_target_pairs={{0,24},{1,25},{2,26},{3,27},{4,28},{5,29},{6,30},{7,31},{8,16},{9,... | collective-permute-start | bytes 884744 | tf_op jit(solution)/shard_map/ppermute | solution.py:203
  4.6 2.7 %collective-permute-start.4 = (bf16[128,1152]{1,0:T(8,128)(2,1)}, bf16[128,1152]{1,0:T(8,128)(2,1)S(1)}, u32[]{:S(2)}, u32[]{:S(2)}) collective-permute-start(bf16[128,1152]{1,0:T(8,128)(2,1)} %image.1), channel_id=1, source_target_pairs={{0,6},{1,7},{2,0},{3,1},{4,2},{5,3},{6,4},{7,5},{8,14},{9,15},{10,... | collective-permute-start | bytes 884744 | tf_op jit(solution)/shard_map/ppermute | solution.py:203
  7.3 0.0 collective-permute-start.3
  7.3 1.5 %collective-permute-start.5 = (bf16[128,1152]{1,0:T(8,128)(2,1)}, bf16[128,1152]{1,0:T(8,128)(2,1)S(1)}, u32[]{:S(2)}, u32[]{:S(2)}) collective-permute-start(bf16[128,1152]{1,0:T(8,128)(2,1)} %text.1), channel_id=1, source_target_pairs={{0,1},{1,0},{2,3},{3,2},{4,5},{5,4},{6,7},{7,6},{8,9},{9,8},{10,11... | collective-permute-start | bytes 884744 | tf_op jit(solution)/shard_map/ppermute | solution.py:207
  10.2 0.1 pad_maximum_fusion.scalar_ref
  10.3 0.0 collective-permute-done.1.t1
  10.3 6.3 %collective-permute-done.s0 = bf16[128,1152]{1,0:T(8,128)(2,1)S(1)} collective-permute-done((bf16[128,1152]{1,0:T(8,128)(2,1)}, bf16[128,1152]{1,0:T(8,128)(2,1)S(1)}, u32[]{:S(2)}, u32[]{:S(2)}) %collective-permute-start) | collective-permute-done | bytes 294944 | tf_op jit(solution)/shard_map/ppermute | solution.py:203
  16.5 1.5 %collective-permute-start.7 = (bf16[128,1152]{1,0:T(8,128)(2,1)S(1)}, bf16[128,1152]{1,0:T(8,128)(2,1)S(1)}, u32[]{:S(2)}, u32[]{:S(2)}) collective-permute-start(bf16[128,1152]{1,0:T(8,128)(2,1)S(1)} %collective-permute-done.1.t1), channel_id=1, source_target_pairs={{0,1},{1,0},{2,3},{3,2},{4,5},{5,4},{6,7},{7,6},{8,9},{9,8},{10,11... | collective-permute-start | bytes 884744 | tf_op jit(solution)/shard_map/ppermute | solution.py:207
  18.1 0.0 collective-permute-start.6
  18.1 0.0 collective-permute-done.4.ib
  18.1 0.4 collective-permute-start.2
  18.5 0.0 collective-permute-done.3.ia
  18.5 0.0 collective-permute-done.5.t0x
  18.5 0.8 %collective-permute-done.7.t1x = bf16[128,1152]{1,0:T(8,128)(2,1)S(1)} collective-permute-done((bf16[128,1152]{1,0:T(8,128)(2,1)S(1)}, bf16[128,1152]{1,0:T(8,128)(2,1)S(1)}, u32[]{:S(2)}, u32[]{:S(2)}) %collective-permute-start.7) | collective-permute-done | bytes 294944 | tf_op jit(solution)/shard_map/ppermute | solution.py:207
  19.3 0.4 collective-permute-done.6.s0x
  19.8 2.8 %collective-permute-start.8 = (bf16[128,1152]{1,0:T(8,128)(2,1)S(1)}, bf16[128,1152]{1,0:T(8,128)(2,1)S(1)}, u32[]{:S(2)}, u32[]{:S(2)}) collective-permute-start(bf16[128,1152]{1,0:T(8,128)(2,1)S(1)} %broadcast_select_fusion), channel_id=1, source_target_pairs={{0,2},{1,7},{2,4},{3,1},{4,6},{5,3},{6,0},{7,5},{8,10},{9,15},{10,... | collective-permute-start | bytes 884744 | tf_op jit(solution)/shard_map/ppermute | solution.py:203
  22.6 5.1 %near.1 = (bf16[384,1152]{1,0:T(8,128)(2,1)S(1)}, bf16[768,1152]{1,0:T(8,128)(2,1)S(1)}, f32[384,128]{1,0:T(8,128)S(1)}, f32[8,768]{1,0:T(8,128)S(1)}, f32[8,128...) custom-call(f32[2]{0:T(128)S(1)} %pad_maximum_fusion.scalar_ref, ...), custom_call_target="tpu_custom_call" | custom-call | flops 8000000000 | bytes 24000000 | tf_op jit(solution)/shard_map/near/pallas_call | solution.py:21
  27.7 0.0 collective-permute-done.2.s1
  27.7 0.0 collective-permute-done.8.i2
  27.7 1.0 %collective-permute-start.9 = (bf16[128,1152]{1,0:T(8,128)(2,1)S(1)}, bf16[128,1152]{1,0:T(8,128)(2,1)S(1)}, u32[]{:S(2)}, u32[]{:S(2)}) collective-permute-start(bf16[128,1152]{1,0:T(8,128)(2,1)S(1)} %collective-permute-done.2.s1), channel_id=1, source_target_pairs={{0,1},{1,0},{2,3},{3,2},{4,5},{5,4},{6,7},{7,6},{8,9},{9,8},{10,11... | collective-permute-start | bytes 884744 | tf_op jit(solution)/shard_map/ppermute | solution.py:207
  28.8 1.2 %collective-permute-done.9.sx = bf16[128,1152]{1,0:T(8,128)(2,1)S(1)} collective-permute-done((bf16[128,1152]{1,0:T(8,128)(2,1)S(1)}, bf16[128,1152]{1,0:T(8,128)(2,1)S(1)}, u32[]{:S(2)}, u32[]{:S(2)}) %collective-permute-start.9) | collective-permute-done | bytes 294944 | tf_op jit(solution)/shard_map/ppermute | solution.py:207
  30.0 2.3 %far.1 = (f32[8,128]{1,0:T(8,128)S(1)}, bf16[128,768]{1,0:T(8,128)(2,1)S(1)}, bf16[128,768]{1,0:T(8,128)(2,1)S(1)}, bf16[512,256]{1,0:T(8,128)(2,1)S(1)}, bf16[5...) custom-call(f32[2]{0:T(128)S(1)} %pad_maximum_fusion.scalar_ref, ...), custom_call_target="tpu_custom_call" | custom-call | flops 2000000000 | bytes 6000000 | tf_op jit(solution)/shard_map/far/pallas_call | solution.py:21
  32.3 1.4 %collective-permute-start.10 = (f32[8,128]{1,0:T(8,128)S(1)}, f32[8,128]{1,0:T(8,128)S(1)}, u32[]{:S(2)}, u32[]{:S(2)}) collective-permute-start(f32[8,128]{1,0:T(8,128)S(1)} %get-tuple-element.72), channel_id=1, source_target_pairs={{0,2},{2,0},{4,6},{6,4},{1,3},{3,1},{5,7},{7,5},{8,10},{10,8},{12,... | collective-permute-start | bytes 12296 | tf_op jit(solution)/shard_map/ppermute | solution.py:249
  33.7 1.9 %sums.1 = (f32[128,1152]{1,0:T(8,128)S(1)}, f32[128,1152]{1,0:T(8,128)S(1)}, f32[1664,1152]{1,0:T(8,128)S(1)}) custom-call(s32[1]{0:T(128)} %bitcast.core_ref, bf16[128,768]{1,0:T(8,128)(2,1)S(1)} %get-tuple-element.59.by_near_text, bf16[128,768]{1,0:T(8,128)(2,1)S(1)} %get-tuple-element.60.by_near_image, ...), custom_call_target="tpu_custom_call" | custom-call | flops 4000000000 | bytes 12000000 | tf_op jit(solution)/shard_map/sums/pallas_call | solution.py:21
  35.6 0.0 collective-permute-done.10
  35.7 0.4 multiply_convert_fusion
  36.1 0.8 %collective-permute-start.11 = (f16[896,1152]{1,0:T(8,128)(2,1)S(1)}, f16[896,1152]{1,0:T(8,128)(2,1)S(1)}, u32[]{:S(2)}, u32[]{:S(2)}) collective-permute-start(f16[896,1152]{1,0:T(8,128)(2,1)S(1)} %multiply_convert_fusion), channel_id=1, source_target_pairs={{0,1},{1,0},{2,3},{3,2},{4,5},{5,4},{6,7},{7,6},{8,9},{9,8},{10,11... | collective-permute-start | bytes 6193160 | tf_op jit(solution)/shard_map/ppermute | solution.py:207
  36.9 0.0 collective-permute-start.12
  36.9 2.5 %collective-permute-done.12 = f32[8,128]{1,0:T(8,128)S(1)} collective-permute-done((f32[8,128]{1,0:T(8,128)S(1)}, f32[8,128]{1,0:T(8,128)S(1)}, u32[]{:S(2)}, u32[]{:S(2)}) %collective-permute-start.12) | collective-permute-done | bytes 4128 | tf_op jit(solution)/shard_map/ppermute | solution.py:203
  39.4 1.3 %collective-permute-done.11 = f16[896,1152]{1,0:T(8,128)(2,1)S(1)} collective-permute-done((f16[896,1152]{1,0:T(8,128)(2,1)S(1)}, f16[896,1152]{1,0:T(8,128)(2,1)S(1)}, u32[]{:S(2)}, u32[]{:S(2)}) %collective-permute-start.11) | collective-permute-done | bytes 2064416 | tf_op jit(solution)/shard_map/ppermute | solution.py:207
  40.7 2.9 %collective-permute-start.16 = (f32[8,128]{1,0:T(8,128)S(1)}, f32[8,128]{1,0:T(8,128)S(1)}, u32[]{:S(2)}, u32[]{:S(2)}) collective-permute-start(f32[8,128]{1,0:T(8,128)S(1)} %add.39), channel_id=1, source_target_pairs={{0,4},{2,6},{4,0},{6,2},{1,5},{3,7},{5,1},{7,3},{8,12},{10,14},{12... | collective-permute-start | bytes 12296 | tf_op jit(solution)/shard_map/ppermute | solution.py:259
  43.6 0.7 multiply_convert_fusion.1
  44.2 0.1 collective-permute-start.15
  44.4 1.3 %collective-permute-start.14 = (f16[256,1152]{1,0:T(8,128)(2,1)S(1)}, f16[256,1152]{1,0:T(8,128)(2,1)S(1)}, u32[]{:S(2)}, u32[]{:S(2)}) collective-permute-start(f16[256,1152]{1,0:T(8,128)(2,1)S(1)} %get-tuple-element.86), channel_id=1, source_target_pairs={{0,248},{1,3},{2,250},{3,5},{4,252},{5,7},{6,254},{7,1},{8,240},{9... | collective-permute-start | bytes 1769480 | tf_op jit(solution)/shard_map/ppermute | solution.py:203
  45.7 1.4 %collective-permute-start.13 = (f16[256,1152]{1,0:T(8,128)(2,1)S(1)}, f16[256,1152]{1,0:T(8,128)(2,1)S(1)}, u32[]{:S(2)}, u32[]{:S(2)}) collective-permute-start(f16[256,1152]{1,0:T(8,128)(2,1)S(1)} %get-tuple-element.87), channel_id=1, source_target_pairs={{0,8},{1,7},{2,10},{3,1},{4,12},{5,3},{6,14},{7,5},{8,0},{9,15},{1... | collective-permute-start | bytes 1769480 | tf_op jit(solution)/shard_map/ppermute | solution.py:203
  47.1 0.0 collective-permute-done.16
  47.1 14.7 %all_to_all.12 = f32[16,1,128]{2,1,0:T(1,128)S(1)} all-to-all(f32[16,1,128]{2,1,0:T(1,128)S(1)} %bitcast.5), channel_id=1, replica_groups=mesh['z'=8,'xh'=2,'xl'=2,'y'=4,'c'=2] {'z','xh'}, dimensions={0} | all-to-all | bytes 16384 | tf_op jit(solution)/shard_map/all_to_all | solution.py:268
  61.9 0.0 collective-permute-done.15
  61.9 0.0 collective-permute-done.14
  61.9 0.2 add_multiply_fusion
  62.1 0.1 multiply_convert_fusion.4
  62.2 4.6 %collective-permute-start.17 = (f16[128,1152]{1,0:T(8,128)(2,1)S(1)}, f16[128,1152]{1,0:T(8,128)(2,1)S(1)}, u32[]{:S(2)}, u32[]{:S(2)}) collective-permute-start(f16[128,1152]{1,0:T(8,128)(2,1)S(1)} %multiply_convert_fusion.4), channel_id=1, source_target_pairs={{0,1},{1,0},{2,3},{3,2},{4,5},{5,4},{6,7},{7,6},{8,9},{9,8},{10,11... | collective-permute-start | bytes 884744 | tf_op jit(solution)/shard_map/ppermute | solution.py:207
  66.8 0.1 collective-permute-start.18
  66.9 1.1 %collective-permute-done.18 = f32[16,128]{1,0:T(8,128)S(1)} collective-permute-done((f32[16,128]{1,0:T(8,128)S(1)}, f32[16,128]{1,0:T(8,128)S(1)}, u32[]{:S(2)}, u32[]{:S(2)}) %collective-permute-start.18) | collective-permute-done | bytes 8224 | tf_op jit(solution)/shard_map/ppermute | solution.py:207
  68.0 0.0 collective-permute-done.17
  68.0 0.2 select_add_fusion
  68.2 2.0 %finish.1 = (f32[128,1152]{1,0:T(8,128)}, f32[128,1152]{1,0:T(8,128)}, f32[1]{0:T(128)}) custom-call(f32[2]{0:T(128)S(1)} %pad_maximum_fusion.scalar_ref, bf16[128,1152]{1,0:T(8,128)(2,1)S(1)} %copy-done, bf16[128,1152]{1,0:T(8,128)(2,1)S(1)} %copy-done.1, f32[128,1152]{1,0:T(8,128)S(1)} %get-tuple-element.89.image_hat, ...), custom_call_target="tpu_custom_call" | custom-call | flops 20000000000 | bytes 60000000 | tf_op jit(solution)/shard_map/finish/pallas_call | solution.py:21
  (12 shorter events, 0.1 us)
Async XLA Ops:
  0.6 21.9 %copy-start.1 = (bf16[128,1152]{1,0:T(8,128)(2,1)S(1)}, bf16[128,1152]{1,0:T(8,128)(2,1)}, u32[]{:S(2)}) copy-start(bf16[128,1152]{1,0:T(8,128)(2,1)} %text.1) | copy-start | bytes 884740
  0.6 21.9 %copy-start = (bf16[128,1152]{1,0:T(8,128)(2,1)S(1)}, bf16[128,1152]{1,0:T(8,128)(2,1)}, u32[]{:S(2)}) copy-start(bf16[128,1152]{1,0:T(8,128)(2,1)} %image.1) | copy-start | bytes 884740
  0.7 9.6 %collective-permute-start.1 = (bf16[128,1152]{1,0:T(8,128)(2,1)}, bf16[128,1152]{1,0:T(8,128)(2,1)S(1)}, u32[]{:S(2)}, u32[]{:S(2)}) collective-permute-start(bf16[128,1152]{1,0:T(8,128)(2,1)} %text.1), channel_id=1, source_target_pairs={{0,8},{1,9},{2,10},{3,11},{4,12},{5,13},{6,14},{7,15},{8,0},{9,1},... | collective-permute-start | bytes 884744 | tf_op jit(solution)/shard_map/ppermute | solution.py:203
  2.8 13.8 %collective-permute-start = (bf16[128,1152]{1,0:T(8,128)(2,1)}, bf16[128,1152]{1,0:T(8,128)(2,1)S(1)}, u32[]{:S(2)}, u32[]{:S(2)}) collective-permute-start(bf16[128,1152]{1,0:T(8,128)(2,1)} %text.1), channel_id=1, source_target_pairs={{0,24},{1,25},{2,26},{3,27},{4,28},{5,29},{6,30},{7,31},{8,16},{9,... | collective-permute-start | bytes 884744 | tf_op jit(solution)/shard_map/ppermute | solution.py:203
  4.6 13.5 %collective-permute-start.4 = (bf16[128,1152]{1,0:T(8,128)(2,1)}, bf16[128,1152]{1,0:T(8,128)(2,1)S(1)}, u32[]{:S(2)}, u32[]{:S(2)}) collective-permute-start(bf16[128,1152]{1,0:T(8,128)(2,1)} %image.1), channel_id=1, source_target_pairs={{0,6},{1,7},{2,0},{3,1},{4,2},{5,3},{6,4},{7,5},{8,14},{9,15},{10,... | collective-permute-start | bytes 884744 | tf_op jit(solution)/shard_map/ppermute | solution.py:203
  7.3 11.2 %collective-permute-start.3 = (bf16[128,1152]{1,0:T(8,128)(2,1)}, bf16[128,1152]{1,0:T(8,128)(2,1)S(1)}, u32[]{:S(2)}, u32[]{:S(2)}) collective-permute-start(bf16[128,1152]{1,0:T(8,128)(2,1)} %image.1), channel_id=1, source_target_pairs={{0,2},{1,3},{2,4},{3,5},{4,6},{5,7},{6,0},{7,1},{8,10},{9,11},{10,... | collective-permute-start | bytes 884744 | tf_op jit(solution)/shard_map/ppermute | solution.py:203
  7.3 11.2 %collective-permute-start.5 = (bf16[128,1152]{1,0:T(8,128)(2,1)}, bf16[128,1152]{1,0:T(8,128)(2,1)S(1)}, u32[]{:S(2)}, u32[]{:S(2)}) collective-permute-start(bf16[128,1152]{1,0:T(8,128)(2,1)} %text.1), channel_id=1, source_target_pairs={{0,1},{1,0},{2,3},{3,2},{4,5},{5,4},{6,7},{7,6},{8,9},{9,8},{10,11... | collective-permute-start | bytes 884744 | tf_op jit(solution)/shard_map/ppermute | solution.py:207
  16.5 2.8 %collective-permute-start.7 = (bf16[128,1152]{1,0:T(8,128)(2,1)S(1)}, bf16[128,1152]{1,0:T(8,128)(2,1)S(1)}, u32[]{:S(2)}, u32[]{:S(2)}) collective-permute-start(bf16[128,1152]{1,0:T(8,128)(2,1)S(1)} %collective-permute-done.1.t1), channel_id=1, source_target_pairs={{0,1},{1,0},{2,3},{3,2},{4,5},{5,4},{6,7},{7,6},{8,9},{9,8},{10,11... | collective-permute-start | bytes 884744 | tf_op jit(solution)/shard_map/ppermute | solution.py:207
  18.1 1.6 %collective-permute-start.6 = (bf16[128,1152]{1,0:T(8,128)(2,1)S(1)}, bf16[128,1152]{1,0:T(8,128)(2,1)S(1)}, u32[]{:S(2)}, u32[]{:S(2)}) collective-permute-start(bf16[128,1152]{1,0:T(8,128)(2,1)S(1)} %collective-permute-done.s0), channel_id=1, source_target_pairs={{0,1},{1,0},{2,3},{3,2},{4,5},{5,4},{6,7},{7,6},{8,9},{9,8},{10,11... | collective-permute-start | bytes 884744 | tf_op jit(solution)/shard_map/ppermute | solution.py:207
  18.1 9.6 %collective-permute-start.2 = (bf16[128,1152]{1,0:T(8,128)(2,1)S(1)}, bf16[128,1152]{1,0:T(8,128)(2,1)S(1)}, u32[]{:S(2)}, u32[]{:S(2)}) collective-permute-start(bf16[128,1152]{1,0:T(8,128)(2,1)S(1)} %broadcast_select_fusion.1), channel_id=1, source_target_pairs={{0,24},{1,9},{2,26},{3,11},{4,28},{5,13},{6,30},{7,15},{8,16},{9,1... | collective-permute-start | bytes 884744 | tf_op jit(solution)/shard_map/ppermute | solution.py:203
  19.8 8.0 %collective-permute-start.8 = (bf16[128,1152]{1,0:T(8,128)(2,1)S(1)}, bf16[128,1152]{1,0:T(8,128)(2,1)S(1)}, u32[]{:S(2)}, u32[]{:S(2)}) collective-permute-start(bf16[128,1152]{1,0:T(8,128)(2,1)S(1)} %broadcast_select_fusion), channel_id=1, source_target_pairs={{0,2},{1,7},{2,4},{3,1},{4,6},{5,3},{6,0},{7,5},{8,10},{9,15},{10,... | collective-permute-start | bytes 884744 | tf_op jit(solution)/shard_map/ppermute | solution.py:203
  27.7 2.2 %collective-permute-start.9 = (bf16[128,1152]{1,0:T(8,128)(2,1)S(1)}, bf16[128,1152]{1,0:T(8,128)(2,1)S(1)}, u32[]{:S(2)}, u32[]{:S(2)}) collective-permute-start(bf16[128,1152]{1,0:T(8,128)(2,1)S(1)} %collective-permute-done.2.s1), channel_id=1, source_target_pairs={{0,1},{1,0},{2,3},{3,2},{4,5},{5,4},{6,7},{7,6},{8,9},{9,8},{10,11... | collective-permute-start | bytes 884744 | tf_op jit(solution)/shard_map/ppermute | solution.py:207
  32.3 3.3 %collective-permute-start.10 = (f32[8,128]{1,0:T(8,128)S(1)}, f32[8,128]{1,0:T(8,128)S(1)}, u32[]{:S(2)}, u32[]{:S(2)}) collective-permute-start(f32[8,128]{1,0:T(8,128)S(1)} %get-tuple-element.72), channel_id=1, source_target_pairs={{0,2},{2,0},{4,6},{6,4},{1,3},{3,1},{5,7},{7,5},{8,10},{10,8},{12,... | collective-permute-start | bytes 12296 | tf_op jit(solution)/shard_map/ppermute | solution.py:249
  36.1 4.5 %collective-permute-start.11 = (f16[896,1152]{1,0:T(8,128)(2,1)S(1)}, f16[896,1152]{1,0:T(8,128)(2,1)S(1)}, u32[]{:S(2)}, u32[]{:S(2)}) collective-permute-start(f16[896,1152]{1,0:T(8,128)(2,1)S(1)} %multiply_convert_fusion), channel_id=1, source_target_pairs={{0,1},{1,0},{2,3},{3,2},{4,5},{5,4},{6,7},{7,6},{8,9},{9,8},{10,11... | collective-permute-start | bytes 6193160 | tf_op jit(solution)/shard_map/ppermute | solution.py:207
  36.9 2.5 %collective-permute-start.12 = (f32[8,128]{1,0:T(8,128)S(1)}, f32[8,128]{1,0:T(8,128)S(1)}, u32[]{:S(2)}, u32[]{:S(2)}) collective-permute-start(f32[8,128]{1,0:T(8,128)S(1)} %add.38), channel_id=1, source_target_pairs={{0,8},{1,9},{2,10},{3,11},{4,12},{5,13},{6,14},{7,15},{8,0},{9,1},... | collective-permute-start | bytes 12296 | tf_op jit(solution)/shard_map/ppermute | solution.py:203
  40.7 6.5 %collective-permute-start.16 = (f32[8,128]{1,0:T(8,128)S(1)}, f32[8,128]{1,0:T(8,128)S(1)}, u32[]{:S(2)}, u32[]{:S(2)}) collective-permute-start(f32[8,128]{1,0:T(8,128)S(1)} %add.39), channel_id=1, source_target_pairs={{0,4},{2,6},{4,0},{6,2},{1,5},{3,7},{5,1},{7,3},{8,12},{10,14},{12... | collective-permute-start | bytes 12296 | tf_op jit(solution)/shard_map/ppermute | solution.py:259
  44.2 17.6 %collective-permute-start.15 = (f16[256,1152]{1,0:T(8,128)(2,1)S(1)}, f16[256,1152]{1,0:T(8,128)(2,1)S(1)}, u32[]{:S(2)}, u32[]{:S(2)}) collective-permute-start(f16[256,1152]{1,0:T(8,128)(2,1)S(1)} %get-tuple-element.85), channel_id=1, source_target_pairs={{0,240},{1,5},{2,242},{3,7},{4,244},{5,1},{6,246},{7,3},{8,248},{9... | collective-permute-start | bytes 1769480 | tf_op jit(solution)/shard_map/ppermute | solution.py:203
  44.4 17.5 %collective-permute-start.14 = (f16[256,1152]{1,0:T(8,128)(2,1)S(1)}, f16[256,1152]{1,0:T(8,128)(2,1)S(1)}, u32[]{:S(2)}, u32[]{:S(2)}) collective-permute-start(f16[256,1152]{1,0:T(8,128)(2,1)S(1)} %get-tuple-element.86), channel_id=1, source_target_pairs={{0,248},{1,3},{2,250},{3,5},{4,252},{5,7},{6,254},{7,1},{8,240},{9... | collective-permute-start | bytes 1769480 | tf_op jit(solution)/shard_map/ppermute | solution.py:203
  45.7 16.2 %collective-permute-start.13 = (f16[256,1152]{1,0:T(8,128)(2,1)S(1)}, f16[256,1152]{1,0:T(8,128)(2,1)S(1)}, u32[]{:S(2)}, u32[]{:S(2)}) collective-permute-start(f16[256,1152]{1,0:T(8,128)(2,1)S(1)} %get-tuple-element.87), channel_id=1, source_target_pairs={{0,8},{1,7},{2,10},{3,1},{4,12},{5,3},{6,14},{7,5},{8,0},{9,15},{1... | collective-permute-start | bytes 1769480 | tf_op jit(solution)/shard_map/ppermute | solution.py:203
  62.2 5.8 %collective-permute-start.17 = (f16[128,1152]{1,0:T(8,128)(2,1)S(1)}, f16[128,1152]{1,0:T(8,128)(2,1)S(1)}, u32[]{:S(2)}, u32[]{:S(2)}) collective-permute-start(f16[128,1152]{1,0:T(8,128)(2,1)S(1)} %multiply_convert_fusion.4), channel_id=1, source_target_pairs={{0,1},{1,0},{2,3},{3,2},{4,5},{5,4},{6,7},{7,6},{8,9},{9,8},{10,11... | collective-permute-start | bytes 884744 | tf_op jit(solution)/shard_map/ppermute | solution.py:207
  66.8 1.2 %collective-permute-start.18 = (f32[16,128]{1,0:T(8,128)S(1)}, f32[16,128]{1,0:T(8,128)S(1)}, u32[]{:S(2)}, u32[]{:S(2)}) collective-permute-start(f32[16,128]{1,0:T(8,128)S(1)} %bitcast.6), channel_id=1, source_target_pairs={{0,1},{1,0},{2,3},{3,2},{4,5},{5,4},{6,7},{7,6},{8,9},{9,8},{10,11... | collective-permute-start | bytes 24584 | tf_op jit(solution)/shard_map/ppermute | solution.py:207

commit v5 on v4

--- a/solution.py
+++ b/solution.py
@@ -72,7 +72,7 @@
 
 
 def near(scalar_ref, i0, ia, ib, t0, t1, s0, t0x, t1x, s0x,
-         images, texts, image_inverse, text_inverse, loss, ht0, ht1, hs0, htx, hi, coefs):
+         images, texts, image_inverse, text_inverse, loss, by_text, by_image):
     for n, ref in enumerate((i0, ia, ib)):
         images[pl.ds(n * ROWS, ROWS), :] = ref[...]
     for n, ref in enumerate((t0, t1, s0, t0x, t1x, s0x)):
@@ -80,16 +80,21 @@
     column = inverse_norm(images[...])
     image_inverse[...] = jnp.broadcast_to(column, image_inverse.shape)
     total = jnp.zeros((8, 128), F32)
-    outs = (ht0, ht1, hs0)
     for tile in range(3):
         span = pl.ds(tile * TILE, TILE)
         block = texts[span, :]
         row = as_row(inverse_norm(block))
         text_inverse[:, span] = jnp.broadcast_to(row, (8, TILE))
-        part, by_text, by_image = terms(scalar_ref, dot_t(images[...], block), column, row, own=tile == 0)
+        part, by_text[:, span], by_image[:, span] = terms(
+            scalar_ref, dot_t(images[...], block), column, row, own=tile == 0)
         total = total + part
-        coefs[:, span] = by_text
-        update = t_dot(by_image, images[...])
+    loss[...] = total
+
+
+def near_sums(by_text, by_image, images, texts, ht0, ht1, hs0, htx, hi):
+    outs = (ht0, ht1, hs0)
+    for tile in range(3):
+        update = t_dot(by_image[:, tile * TILE:(tile + 1) * TILE], images[...])
         for half in range(2):
             n = 2 * tile + half
             piece = update[half * ROWS:(half + 1) * ROWS]
@@ -97,8 +102,7 @@
                 outs[n][...] = piece
             else:
                 htx[pl.ds((n - 3) * ROWS, ROWS), :] = piece
-    hi[...] = dot(coefs[...], texts[...])
-    loss[...] = total
+    hi[...] = dot(by_text[...], texts[...])
 
 
 def far(scalar_ref, i2, s1, sx, images, texts, image_inverse, text_inverse, loss_in,
@@ -229,18 +233,22 @@
 
     s0, t1 = move(t0, outer), move(t0, inner)
     ia, ib, t0x = move(i0, up), move(i0, down), swap_cores(t0)
-    s0x, t1x = swap_cores(s0), swap_cores(t1)
     s0, t1 = together(s0, t1)
     s1 = move(jnp.where(first, t1, s0), outer, inner)
-    ia, ib, t0x, s0x, t1x = together(ia, ib, t0x, s0x, t1x)
+    ia, ib, t0x, t1, s0 = together(ia, ib, t0x, t1, s0)
     i2 = move(jnp.where(first, ia, ib), up, down)
-    images, texts, image_inverse, text_inverse, loss, ht0, ht1, hs0, htx, hi = call(
+    s0x, t1x = swap_cores(s0), swap_cores(t1)
+    pairs = ((3 * ROWS, 6 * ROWS), BF16)
+    images, texts, image_inverse, text_inverse, loss, near_by_text, near_by_image = call(
         near,
         (((3 * ROWS, width), BF16), ((6 * ROWS, width), BF16), ((3 * ROWS, 128), F32), ((8, 6 * ROWS), F32),
-         ((8, 128), F32), block, block, block, ((3 * ROWS, width), F32), ((3 * ROWS, width), F32)),
-        8.0, 26, scalars, i0, ia, ib, t0, t1, s0, t0x, t1x, s0x, scratch=(pltpu.VMEM((3 * ROWS, 6 * ROWS), BF16),))
-    s1, i2, loss = together(s1, i2, loss)
+         ((8, 128), F32), pairs, pairs),
+        8.0, 20, scalars, i0, ia, ib, t0, t1, s0, t0x, t1x, s0x)
+    s1, loss = together(s1, loss)
     sx = swap_cores(s1)
+    ht0, ht1, hs0, htx, hi = call(
+        near_sums, (block, block, block, ((3 * ROWS, width), F32), ((3 * ROWS, width), F32)), 4.0, 20,
+        near_by_text, near_by_image, images, texts)
     loss, by_near_text, by_near_image, by_far_text, by_far_image, four, pair = call(
         far,
         (((8, 128), F32), ((ROWS, 6 * ROWS), BF16), ((ROWS, 6 * ROWS), BF16), ((4 * ROWS, 2 * ROWS), BF16),
@@ -264,13 +272,12 @@
         move(outs[0], inner, down),
         move(outs[1], outer_back, up),
         move(outs[2], far_back, across))
-    loss, = call(everyone, (((16, 128), F32),), 20.0, 4, loss)
-    loss = lax.all_to_all(loss, ("z", "xh"), 0, 0, tiled=True)
+    loss, = call(everyone, (((32, 128), F32),), 20.0, 4, loss)
+    loss = lax.all_to_all(loss, ("z", "xh", "c"), 0, 0, tiled=True)
     *back, loss = together(*back, loss)
     back = sum(widen(part) for part in back)
     stay = jnp.where(first, back[:ROWS], back[ROWS:])
     swapped = widen(swap_cores(narrow(jnp.where(first, back[ROWS:], back[:ROWS]))))
-    loss = loss + swap_cores(loss)
     text_hat = own_text + jnp.where(first, stay, swapped)
     image_hat = own_image + jnp.where(first, swapped, stay)
     image_grad, text_grad, loss = call(

time: 70.5 us -> 69.3 us (0.983)
  blocking collectives: 14.7 us -> 17.5 us
  waiting for transfers between devices: 13.5 us -> 11.3 us
  starting transfers between devices: 26.6 us -> 25.1 us
    all_to_all x1, blocking collectives: 14.7 us -> 17.5 us  [body(): loss = lax.all_to_all(loss, ('z', 'xh', 'c'), 0, 0, tiled=True)]
    ppermute x7 -> x6, waiting for transfers between devices: 4.77 us -> 2.53 us  [swap_cores(): return lax.ppermute(block, 'c', [(0, 1), (1, 0)])]
    ppermute x7 -> x6, starting transfers between devices: 9.57 us -> 8.07 us  [swap_cores(): return lax.ppermute(block, 'c', [(0, 1), (1, 0)])]
    pallas_call x5 -> x6, Pallas kernels: 11.4 us -> 11.2 us  [call(): pl.pallas_call(kernel, out_shape=shapes, in_specs=[SMEM if a.ndim == 1 el...]
  transfers between devices with their start and end apart: 19 -> 18, of which waited for: 7 -> 4; matrix products, arithmetic and copies ran while one was open for 1% -> 1% of each run, Pallas kernels for 10% -> 10%
where the time goes in v5:
time: 69.3 us; the launch traced here: 69.1 us
  starting transfers between devices  25.1 us (36%)
  blocking collectives  17.5 us (25%)
  waiting for transfers between devices  11.3 us (16%)
  Pallas kernels  11.2 us (16%)
  between operations  2.27 us (3%)
  other arithmetic  1.76 us (3%)
    all_to_all x1, blocking collectives, body(): loss = lax.all_to_all(loss, ('z', 'xh', 'c'), 0, 0, tiled=True)  17.5 us
    ppermute x10, starting transfers between devices, move(): return lax.ppermute(block, AXES, route)  12.8 us
    pallas_call x6, Pallas kernels, call(): pl.pallas_call(kernel, out_shape=shapes, in_specs=[SMEM if a.ndim == 1 el...  11.2 us
    ppermute x10, waiting for transfers between devices, move(): return lax.ppermute(block, AXES, route)  8.75 us
    ppermute x6, starting transfers between devices, swap_cores(): return lax.ppermute(block, 'c', [(0, 1), (1, 0)])  8.07 us
    ppermute x1, starting transfers between devices, body(): loss = loss + lax.ppermute(loss, 'y', [(i, i ^ 2) for i in range(4)])  2.87 us
    ppermute x6, waiting for transfers between devices, swap_cores(): return lax.ppermute(block, 'c', [(0, 1), (1, 0)])  2.53 us
  transfers between devices with their start and end apart: 18, of which 4 were waited for; matrix products, arithmetic and copies ran while one was open for 1% of the time, Pallas kernels for 10%

profile of v5, /device:TPU:1, one launch (start us, length us, event | category | flops | bytes accessed | tf_op | source)
XLA Modules:
  0.0 69.1 jit_solution(1810953762995666552)
XLA Ops:
  0.7 2.1 %collective-permute-start.4 = (bf16[128,1152]{1,0:T(8,128)(2,1)}, bf16[128,1152]{1,0:T(8,128)(2,1)S(1)}, u32[]{:S(2)}, u32[]{:S(2)}) collective-permute-start(bf16[128,1152]{1,0:T(8,128)(2,1)} %text.1), channel_id=1, source_target_pairs={{0,8},{1,9},{2,10},{3,11},{4,12},{5,13},{6,14},{7,15},{8,0},{9,1},... | collective-permute-start | bytes 884744 | tf_op jit(solution)/shard_map/ppermute | solution.py:207
  2.8 1.8 %collective-permute-start.3 = (bf16[128,1152]{1,0:T(8,128)(2,1)}, bf16[128,1152]{1,0:T(8,128)(2,1)S(1)}, u32[]{:S(2)}, u32[]{:S(2)}) collective-permute-start(bf16[128,1152]{1,0:T(8,128)(2,1)} %text.1), channel_id=1, source_target_pairs={{0,24},{1,25},{2,26},{3,27},{4,28},{5,29},{6,30},{7,31},{8,16},{9,... | collective-permute-start | bytes 884744 | tf_op jit(solution)/shard_map/ppermute | solution.py:207
  4.6 2.7 %collective-permute-start.1 = (bf16[128,1152]{1,0:T(8,128)(2,1)}, bf16[128,1152]{1,0:T(8,128)(2,1)S(1)}, u32[]{:S(2)}, u32[]{:S(2)}) collective-permute-start(bf16[128,1152]{1,0:T(8,128)(2,1)} %image.1), channel_id=1, source_target_pairs={{0,6},{1,7},{2,0},{3,1},{4,2},{5,3},{6,4},{7,5},{8,14},{9,15},{10,... | collective-permute-start | bytes 884744 | tf_op jit(solution)/shard_map/ppermute | solution.py:207
  7.3 0.0 collective-permute-start
  7.3 1.5 %collective-permute-start.2 = (bf16[128,1152]{1,0:T(8,128)(2,1)}, bf16[128,1152]{1,0:T(8,128)(2,1)S(1)}, u32[]{:S(2)}, u32[]{:S(2)}) collective-permute-start(bf16[128,1152]{1,0:T(8,128)(2,1)} %text.1), channel_id=1, source_target_pairs={{0,1},{1,0},{2,3},{3,2},{4,5},{5,4},{6,7},{7,6},{8,9},{9,8},{10,11... | collective-permute-start | bytes 884744 | tf_op jit(solution)/shard_map/ppermute | solution.py:211
  10.2 0.1 pad_maximum_fusion.scalar_ref
  10.3 0.0 collective-permute-done.4.t1
  10.3 6.3 %collective-permute-done.3.s0 = bf16[128,1152]{1,0:T(8,128)(2,1)S(1)} collective-permute-done((bf16[128,1152]{1,0:T(8,128)(2,1)}, bf16[128,1152]{1,0:T(8,128)(2,1)S(1)}, u32[]{:S(2)}, u32[]{:S(2)}) %collective-permute-start.3) | collective-permute-done | bytes 294944 | tf_op jit(solution)/shard_map/ppermute | solution.py:207
  16.6 0.4 collective-permute-start.6
  17.0 0.0 collective-permute-done.1.ib
  17.0 0.0 collective-permute-done.ia
  17.0 0.0 collective-permute-done.2.t0x
  17.0 1.4 %collective-permute-start.7 = (bf16[128,1152]{1,0:T(8,128)(2,1)S(1)}, bf16[128,1152]{1,0:T(8,128)(2,1)S(1)}, u32[]{:S(2)}, u32[]{:S(2)}) collective-permute-start(bf16[128,1152]{1,0:T(8,128)(2,1)S(1)} %collective-permute-done.4.t1), channel_id=1, source_target_pairs={{0,1},{1,0},{2,3},{3,2},{4,5},{5,4},{6,7},{7,6},{8,9},{9,8},{10,11... | collective-permute-start | bytes 884744 | tf_op jit(solution)/shard_map/ppermute | solution.py:211
  18.3 0.1 collective-permute-start.8
  18.5 2.8 %collective-permute-start.5 = (bf16[128,1152]{1,0:T(8,128)(2,1)S(1)}, bf16[128,1152]{1,0:T(8,128)(2,1)S(1)}, u32[]{:S(2)}, u32[]{:S(2)}) collective-permute-start(bf16[128,1152]{1,0:T(8,128)(2,1)S(1)} %broadcast_select_fusion.1), channel_id=1, source_target_pairs={{0,2},{1,7},{2,4},{3,1},{4,6},{5,3},{6,0},{7,5},{8,10},{9,15},{10,... | collective-permute-start | bytes 884744 | tf_op jit(solution)/shard_map/ppermute | solution.py:207
  21.3 0.0 collective-permute-done.7.t1x
  21.3 0.0 collective-permute-done.8.s0x
  21.3 2.9 %near.1 = (bf16[384,1152]{1,0:T(8,128)(2,1)S(1)}, bf16[768,1152]{1,0:T(8,128)(2,1)S(1)}, f32[384,128]{1,0:T(8,128)S(1)}, f32[8,768]{1,0:T(8,128)S(1)}, f32[8,128...) custom-call(f32[2]{0:T(128)S(1)} %pad_maximum_fusion.scalar_ref, ...), custom_call_target="tpu_custom_call" | custom-call | flops 8000000000 | bytes 24000000 | tf_op jit(solution)/shard_map/near/pallas_call | solution.py:21
  24.3 0.0 collective-permute-done.6.s1
  24.3 4.0 %collective-permute-start.9 = (bf16[128,1152]{1,0:T(8,128)(2,1)S(1)}, bf16[128,1152]{1,0:T(8,128)(2,1)S(1)}, u32[]{:S(2)}, u32[]{:S(2)}) collective-permute-start(bf16[128,1152]{1,0:T(8,128)(2,1)S(1)} %collective-permute-done.6.s1), channel_id=1, source_target_pairs={{0,1},{1,0},{2,3},{3,2},{4,5},{5,4},{6,7},{7,6},{8,9},{9,8},{10,11... | collective-permute-start | bytes 884744 | tf_op jit(solution)/shard_map/ppermute | solution.py:211
  28.3 1.9 %near_sums.1 = (f32[128,1152]{1,0:T(8,128)S(1)}, f32[128,1152]{1,0:T(8,128)S(1)}, f32[128,1152]{1,0:T(8,128)S(1)}, f32[384,1152]{1,0:T(8,128)S(1)}, f32[384,1152]{1,0:T(8,128)S(1)}) custom-call(bf16[384,768]{1,0:T(8,128)(2,1)S(1)} %get-tuple-element.65.by_text, bf16[384,768]{1,0:T(8,128)(2,1)S(1)} %get-tuple-element.66.by_image, ...), custom_call_target="tpu_custom_call" | custom-call | flops 4000000000 | bytes 12000000 | tf_op jit(solution)/shard_map/near_sums/pallas_call | solution.py:21
  30.2 0.0 collective-permute-done.5.i2
  30.2 0.0 collective-permute-done.9.sx
  30.2 2.4 %far.1 = (f32[8,128]{1,0:T(8,128)S(1)}, bf16[128,768]{1,0:T(8,128)(2,1)S(1)}, bf16[128,768]{1,0:T(8,128)(2,1)S(1)}, bf16[512,256]{1,0:T(8,128)(2,1)S(1)}, bf16[5...) custom-call(f32[2]{0:T(128)S(1)} %pad_maximum_fusion.scalar_ref, ...), custom_call_target="tpu_custom_call" | custom-call | flops 2000000000 | bytes 6000000 | tf_op jit(solution)/shard_map/far/pallas_call | solution.py:21
  32.6 1.4 %collective-permute-start.10 = (f32[8,128]{1,0:T(8,128)S(1)}, f32[8,128]{1,0:T(8,128)S(1)}, u32[]{:S(2)}, u32[]{:S(2)}) collective-permute-start(f32[8,128]{1,0:T(8,128)S(1)} %get-tuple-element.74), channel_id=1, source_target_pairs={{0,2},{2,0},{4,6},{6,4},{1,3},{3,1},{5,7},{7,5},{8,10},{10,8},{12,... | collective-permute-start | bytes 12296 | tf_op jit(solution)/shard_map/ppermute | solution.py:257
  34.0 2.0 %sums.1 = (f32[128,1152]{1,0:T(8,128)S(1)}, f32[128,1152]{1,0:T(8,128)S(1)}, f32[1664,1152]{1,0:T(8,128)S(1)}) custom-call(s32[1]{0:T(128)} %bitcast.core_ref, bf16[128,768]{1,0:T(8,128)(2,1)S(1)} %get-tuple-element.59.by_near_text, bf16[128,768]{1,0:T(8,128)(2,1)S(1)} %get-tuple-element.60.by_near_image, ...), custom_call_target="tpu_custom_call" | custom-call | flops 4000000000 | bytes 12000000 | tf_op jit(solution)/shard_map/sums/pallas_call | solution.py:21
  35.9 0.0 collective-permute-done.10
  36.0 0.4 multiply_convert_fusion
  36.4 0.4 collective-permute-start.11
  36.8 0.0 collective-permute-start.12
  36.8 2.5 %collective-permute-done.12 = f32[8,128]{1,0:T(8,128)S(1)} collective-permute-done((f32[8,128]{1,0:T(8,128)S(1)}, f32[8,128]{1,0:T(8,128)S(1)}, u32[]{:S(2)}, u32[]{:S(2)}) %collective-permute-start.12) | collective-permute-done | bytes 4128 | tf_op jit(solution)/shard_map/ppermute | solution.py:207
  39.3 1.3 %collective-permute-done.11 = f16[896,1152]{1,0:T(8,128)(2,1)S(1)} collective-permute-done((f16[896,1152]{1,0:T(8,128)(2,1)S(1)}, f16[896,1152]{1,0:T(8,128)(2,1)S(1)}, u32[]{:S(2)}, u32[]{:S(2)}) %collective-permute-start.11) | collective-permute-done | bytes 2064416 | tf_op jit(solution)/shard_map/ppermute | solution.py:211
  40.6 2.9 %collective-permute-start.16 = (f32[8,128]{1,0:T(8,128)S(1)}, f32[8,128]{1,0:T(8,128)S(1)}, u32[]{:S(2)}, u32[]{:S(2)}) collective-permute-start(f32[8,128]{1,0:T(8,128)S(1)} %add.36), channel_id=1, source_target_pairs={{0,4},{2,6},{4,0},{6,2},{1,5},{3,7},{5,1},{7,3},{8,12},{10,14},{12... | collective-permute-start | bytes 12296 | tf_op jit(solution)/shard_map/ppermute | solution.py:267
  43.5 0.7 multiply_convert_fusion.1
  44.1 0.2 collective-permute-start.15
  44.3 1.3 %collective-permute-start.14 = (f16[256,1152]{1,0:T(8,128)(2,1)S(1)}, f16[256,1152]{1,0:T(8,128)(2,1)S(1)}, u32[]{:S(2)}, u32[]{:S(2)}) collective-permute-start(f16[256,1152]{1,0:T(8,128)(2,1)S(1)} %get-tuple-element.88), channel_id=1, source_target_pairs={{0,248},{1,3},{2,250},{3,5},{4,252},{5,7},{6,254},{7,1},{8,240},{9... | collective-permute-start | bytes 1769480 | tf_op jit(solution)/shard_map/ppermute | solution.py:207
  45.6 1.4 %collective-permute-start.13 = (f16[256,1152]{1,0:T(8,128)(2,1)S(1)}, f16[256,1152]{1,0:T(8,128)(2,1)S(1)}, u32[]{:S(2)}, u32[]{:S(2)}) collective-permute-start(f16[256,1152]{1,0:T(8,128)(2,1)S(1)} %get-tuple-element.89), channel_id=1, source_target_pairs={{0,8},{1,7},{2,10},{3,1},{4,12},{5,3},{6,14},{7,5},{8,0},{9,15},{1... | collective-permute-start | bytes 1769480 | tf_op jit(solution)/shard_map/ppermute | solution.py:207
  47.0 0.0 collective-permute-done.16
  47.0 17.5 %all_to_all.12 = f32[32,1,128]{2,1,0:T(1,128)S(1)} all-to-all(f32[32,1,128]{2,1,0:T(1,128)S(1)} %bitcast.6), channel_id=1, replica_groups=mesh['z'=8,'xh'=2,'xl'=2,'y'=4,'c'=2] {'z','xh','c'}, dimensions={0} | all-to-all | bytes 32768 | tf_op jit(solution)/shard_map/all_to_all | solution.py:276
  64.5 0.0 collective-permute-done.15
  64.5 0.0 collective-permute-done.14
  64.5 0.0 collective-permute-done.13
  64.5 0.2 add_multiply_fusion
  64.8 0.1 multiply_convert_fusion.4
  64.9 0.7 %collective-permute-start.17 = (f16[128,1152]{1,0:T(8,128)(2,1)S(1)}, f16[128,1152]{1,0:T(8,128)(2,1)S(1)}, u32[]{:S(2)}, u32[]{:S(2)}) collective-permute-start(f16[128,1152]{1,0:T(8,128)(2,1)S(1)} %multiply_convert_fusion.4), channel_id=1, source_target_pairs={{0,1},{1,0},{2,3},{3,2},{4,5},{5,4},{6,7},{7,6},{8,9},{9,8},{10,11... | collective-permute-start | bytes 884744 | tf_op jit(solution)/shard_map/ppermute | solution.py:211
  65.6 1.2 %collective-permute-done.17 = f16[128,1152]{1,0:T(8,128)(2,1)S(1)} collective-permute-done((f16[128,1152]{1,0:T(8,128)(2,1)S(1)}, f16[128,1152]{1,0:T(8,128)(2,1)S(1)}, u32[]{:S(2)}, u32[]{:S(2)}) %collective-permute-start.17) | collective-permute-done | bytes 294944 | tf_op jit(solution)/shard_map/ppermute | solution.py:211
  66.8 0.2 select_add_fusion
  67.0 2.0 %finish.1 = (f32[128,1152]{1,0:T(8,128)}, f32[128,1152]{1,0:T(8,128)}, f32[1]{0:T(128)}) custom-call(f32[2]{0:T(128)S(1)} %pad_maximum_fusion.scalar_ref, bf16[128,1152]{1,0:T(8,128)(2,1)S(1)} %copy-done, bf16[128,1152]{1,0:T(8,128)(2,1)S(1)} %copy-done.1, f32[128,1152]{1,0:T(8,128)S(1)} %get-tuple-element.91.image_hat, ...), custom_call_target="tpu_custom_call" | custom-call | flops 20000000000 | bytes 60000000 | tf_op jit(solution)/shard_map/finish/pallas_call | solution.py:21
  (10 shorter events, 0.1 us)
Async XLA Ops:
  0.6 20.7 %copy-start.1 = (bf16[128,1152]{1,0:T(8,128)(2,1)S(1)}, bf16[128,1152]{1,0:T(8,128)(2,1)}, u32[]{:S(2)}) copy-start(bf16[128,1152]{1,0:T(8,128)(2,1)} %text.1) | copy-start | bytes 884740
  0.6 20.7 %copy-start = (bf16[128,1152]{1,0:T(8,128)(2,1)S(1)}, bf16[128,1152]{1,0:T(8,128)(2,1)}, u32[]{:S(2)}) copy-start(bf16[128,1152]{1,0:T(8,128)(2,1)} %image.1) | copy-start | bytes 884740
  0.7 9.6 %collective-permute-start.4 = (bf16[128,1152]{1,0:T(8,128)(2,1)}, bf16[128,1152]{1,0:T(8,128)(2,1)S(1)}, u32[]{:S(2)}, u32[]{:S(2)}) collective-permute-start(bf16[128,1152]{1,0:T(8,128)(2,1)} %text.1), channel_id=1, source_target_pairs={{0,8},{1,9},{2,10},{3,11},{4,12},{5,13},{6,14},{7,15},{8,0},{9,1},... | collective-permute-start | bytes 884744 | tf_op jit(solution)/shard_map/ppermute | solution.py:207
  2.8 13.8 %collective-permute-start.3 = (bf16[128,1152]{1,0:T(8,128)(2,1)}, bf16[128,1152]{1,0:T(8,128)(2,1)S(1)}, u32[]{:S(2)}, u32[]{:S(2)}) collective-permute-start(bf16[128,1152]{1,0:T(8,128)(2,1)} %text.1), channel_id=1, source_target_pairs={{0,24},{1,25},{2,26},{3,27},{4,28},{5,29},{6,30},{7,31},{8,16},{9,... | collective-permute-start | bytes 884744 | tf_op jit(solution)/shard_map/ppermute | solution.py:207
  4.6 12.4 %collective-permute-start.1 = (bf16[128,1152]{1,0:T(8,128)(2,1)}, bf16[128,1152]{1,0:T(8,128)(2,1)S(1)}, u32[]{:S(2)}, u32[]{:S(2)}) collective-permute-start(bf16[128,1152]{1,0:T(8,128)(2,1)} %image.1), channel_id=1, source_target_pairs={{0,6},{1,7},{2,0},{3,1},{4,2},{5,3},{6,4},{7,5},{8,14},{9,15},{10,... | collective-permute-start | bytes 884744 | tf_op jit(solution)/shard_map/ppermute | solution.py:207
  7.3 9.6 %collective-permute-start = (bf16[128,1152]{1,0:T(8,128)(2,1)}, bf16[128,1152]{1,0:T(8,128)(2,1)S(1)}, u32[]{:S(2)}, u32[]{:S(2)}) collective-permute-start(bf16[128,1152]{1,0:T(8,128)(2,1)} %image.1), channel_id=1, source_target_pairs={{0,2},{1,3},{2,4},{3,5},{4,6},{5,7},{6,0},{7,1},{8,10},{9,11},{10,... | collective-permute-start | bytes 884744 | tf_op jit(solution)/shard_map/ppermute | solution.py:207
  7.3 9.6 %collective-permute-start.2 = (bf16[128,1152]{1,0:T(8,128)(2,1)}, bf16[128,1152]{1,0:T(8,128)(2,1)S(1)}, u32[]{:S(2)}, u32[]{:S(2)}) collective-permute-start(bf16[128,1152]{1,0:T(8,128)(2,1)} %text.1), channel_id=1, source_target_pairs={{0,1},{1,0},{2,3},{3,2},{4,5},{5,4},{6,7},{7,6},{8,9},{9,8},{10,11... | collective-permute-start | bytes 884744 | tf_op jit(solution)/shard_map/ppermute | solution.py:211
  16.6 7.7 %collective-permute-start.6 = (bf16[128,1152]{1,0:T(8,128)(2,1)S(1)}, bf16[128,1152]{1,0:T(8,128)(2,1)S(1)}, u32[]{:S(2)}, u32[]{:S(2)}) collective-permute-start(bf16[128,1152]{1,0:T(8,128)(2,1)S(1)} %broadcast_select_fusion), channel_id=1, source_target_pairs={{0,24},{1,9},{2,26},{3,11},{4,28},{5,13},{6,30},{7,15},{8,16},{9,1... | collective-permute-start | bytes 884744 | tf_op jit(solution)/shard_map/ppermute | solution.py:207
  17.0 4.3 %collective-permute-start.7 = (bf16[128,1152]{1,0:T(8,128)(2,1)S(1)}, bf16[128,1152]{1,0:T(8,128)(2,1)S(1)}, u32[]{:S(2)}, u32[]{:S(2)}) collective-permute-start(bf16[128,1152]{1,0:T(8,128)(2,1)S(1)} %collective-permute-done.4.t1), channel_id=1, source_target_pairs={{0,1},{1,0},{2,3},{3,2},{4,5},{5,4},{6,7},{7,6},{8,9},{9,8},{10,11... | collective-permute-start | bytes 884744 | tf_op jit(solution)/shard_map/ppermute | solution.py:211
  18.3 3.0 %collective-permute-start.8 = (bf16[128,1152]{1,0:T(8,128)(2,1)S(1)}, bf16[128,1152]{1,0:T(8,128)(2,1)S(1)}, u32[]{:S(2)}, u32[]{:S(2)}) collective-permute-start(bf16[128,1152]{1,0:T(8,128)(2,1)S(1)} %collective-permute-done.3.s0), channel_id=1, source_target_pairs={{0,1},{1,0},{2,3},{3,2},{4,5},{5,4},{6,7},{7,6},{8,9},{9,8},{10,11... | collective-permute-start | bytes 884744 | tf_op jit(solution)/shard_map/ppermute | solution.py:211
  18.5 11.7 %collective-permute-start.5 = (bf16[128,1152]{1,0:T(8,128)(2,1)S(1)}, bf16[128,1152]{1,0:T(8,128)(2,1)S(1)}, u32[]{:S(2)}, u32[]{:S(2)}) collective-permute-start(bf16[128,1152]{1,0:T(8,128)(2,1)S(1)} %broadcast_select_fusion.1), channel_id=1, source_target_pairs={{0,2},{1,7},{2,4},{3,1},{4,6},{5,3},{6,0},{7,5},{8,10},{9,15},{10,... | collective-permute-start | bytes 884744 | tf_op jit(solution)/shard_map/ppermute | solution.py:207
  24.3 5.9 %collective-permute-start.9 = (bf16[128,1152]{1,0:T(8,128)(2,1)S(1)}, bf16[128,1152]{1,0:T(8,128)(2,1)S(1)}, u32[]{:S(2)}, u32[]{:S(2)}) collective-permute-start(bf16[128,1152]{1,0:T(8,128)(2,1)S(1)} %collective-permute-done.6.s1), channel_id=1, source_target_pairs={{0,1},{1,0},{2,3},{3,2},{4,5},{5,4},{6,7},{7,6},{8,9},{9,8},{10,11... | collective-permute-start | bytes 884744 | tf_op jit(solution)/shard_map/ppermute | solution.py:211
  32.6 3.4 %collective-permute-start.10 = (f32[8,128]{1,0:T(8,128)S(1)}, f32[8,128]{1,0:T(8,128)S(1)}, u32[]{:S(2)}, u32[]{:S(2)}) collective-permute-start(f32[8,128]{1,0:T(8,128)S(1)} %get-tuple-element.74), channel_id=1, source_target_pairs={{0,2},{2,0},{4,6},{6,4},{1,3},{3,1},{5,7},{7,5},{8,10},{10,8},{12,... | collective-permute-start | bytes 12296 | tf_op jit(solution)/shard_map/ppermute | solution.py:257
  36.4 4.2 %collective-permute-start.11 = (f16[896,1152]{1,0:T(8,128)(2,1)S(1)}, f16[896,1152]{1,0:T(8,128)(2,1)S(1)}, u32[]{:S(2)}, u32[]{:S(2)}) collective-permute-start(f16[896,1152]{1,0:T(8,128)(2,1)S(1)} %multiply_convert_fusion), channel_id=1, source_target_pairs={{0,1},{1,0},{2,3},{3,2},{4,5},{5,4},{6,7},{7,6},{8,9},{9,8},{10,11... | collective-permute-start | bytes 6193160 | tf_op jit(solution)/shard_map/ppermute | solution.py:211
  36.8 2.5 %collective-permute-start.12 = (f32[8,128]{1,0:T(8,128)S(1)}, f32[8,128]{1,0:T(8,128)S(1)}, u32[]{:S(2)}, u32[]{:S(2)}) collective-permute-start(f32[8,128]{1,0:T(8,128)S(1)} %add.35), channel_id=1, source_target_pairs={{0,8},{1,9},{2,10},{3,11},{4,12},{5,13},{6,14},{7,15},{8,0},{9,1},... | collective-permute-start | bytes 12296 | tf_op jit(solution)/shard_map/ppermute | solution.py:207
  40.6 6.4 %collective-permute-start.16 = (f32[8,128]{1,0:T(8,128)S(1)}, f32[8,128]{1,0:T(8,128)S(1)}, u32[]{:S(2)}, u32[]{:S(2)}) collective-permute-start(f32[8,128]{1,0:T(8,128)S(1)} %add.36), channel_id=1, source_target_pairs={{0,4},{2,6},{4,0},{6,2},{1,5},{3,7},{5,1},{7,3},{8,12},{10,14},{12... | collective-permute-start | bytes 12296 | tf_op jit(solution)/shard_map/ppermute | solution.py:267
  44.1 20.4 %collective-permute-start.15 = (f16[256,1152]{1,0:T(8,128)(2,1)S(1)}, f16[256,1152]{1,0:T(8,128)(2,1)S(1)}, u32[]{:S(2)}, u32[]{:S(2)}) collective-permute-start(f16[256,1152]{1,0:T(8,128)(2,1)S(1)} %get-tuple-element.87), channel_id=1, source_target_pairs={{0,240},{1,5},{2,242},{3,7},{4,244},{5,1},{6,246},{7,3},{8,248},{9... | collective-permute-start | bytes 1769480 | tf_op jit(solution)/shard_map/ppermute | solution.py:207
  44.3 20.2 %collective-permute-start.14 = (f16[256,1152]{1,0:T(8,128)(2,1)S(1)}, f16[256,1152]{1,0:T(8,128)(2,1)S(1)}, u32[]{:S(2)}, u32[]{:S(2)}) collective-permute-start(f16[256,1152]{1,0:T(8,128)(2,1)S(1)} %get-tuple-element.88), channel_id=1, source_target_pairs={{0,248},{1,3},{2,250},{3,5},{4,252},{5,7},{6,254},{7,1},{8,240},{9... | collective-permute-start | bytes 1769480 | tf_op jit(solution)/shard_map/ppermute | solution.py:207
  45.6 19.0 %collective-permute-start.13 = (f16[256,1152]{1,0:T(8,128)(2,1)S(1)}, f16[256,1152]{1,0:T(8,128)(2,1)S(1)}, u32[]{:S(2)}, u32[]{:S(2)}) collective-permute-start(f16[256,1152]{1,0:T(8,128)(2,1)S(1)} %get-tuple-element.89), channel_id=1, source_target_pairs={{0,8},{1,7},{2,10},{3,1},{4,12},{5,3},{6,14},{7,5},{8,0},{9,15},{1... | collective-permute-start | bytes 1769480 | tf_op jit(solution)/shard_map/ppermute | solution.py:207
  64.9 1.9 %collective-permute-start.17 = (f16[128,1152]{1,0:T(8,128)(2,1)S(1)}, f16[128,1152]{1,0:T(8,128)(2,1)S(1)}, u32[]{:S(2)}, u32[]{:S(2)}) collective-permute-start(f16[128,1152]{1,0:T(8,128)(2,1)S(1)} %multiply_convert_fusion.4), channel_id=1, source_target_pairs={{0,1},{1,0},{2,3},{3,2},{4,5},{5,4},{6,7},{7,6},{8,9},{9,8},{10,11... | collective-permute-start | bytes 884744 | tf_op jit(solution)/shard_map/ppermute | solution.py:211

commit v6 on v5

--- a/solution.py
+++ b/solution.py
@@ -91,18 +91,17 @@
     loss[...] = total
 
 
-def near_sums(by_text, by_image, images, texts, ht0, ht1, hs0, htx, hi):
-    outs = (ht0, ht1, hs0)
-    for tile in range(3):
-        update = t_dot(by_image[:, tile * TILE:(tile + 1) * TILE], images[...])
-        for half in range(2):
-            n = 2 * tile + half
-            piece = update[half * ROWS:(half + 1) * ROWS]
-            if n < 3:
-                outs[n][...] = piece
-            else:
-                htx[pl.ds((n - 3) * ROWS, ROWS), :] = piece
-    hi[...] = dot(by_text[...], texts[...])
+def near_sums(by_text, by_image, images, texts, ht1, hs0, htx, hi):
+    update = t_dot(by_image[:, ROWS:3 * ROWS], images[...])
+    ht1[...] = update[:ROWS]
+    hs0[...] = update[ROWS:]
+    htx[...] = t_dot(by_image[:, 3 * ROWS:], images[...])
+    hi[...] = dot(by_text[pl.ds(ROWS, 2 * ROWS), :], texts[...])
+
+
+def own_sums(near_by_text, near_by_image, by_near_image, by_far_text, images, texts, i2, pair, own_text, own_image):
+    own_text[...] = t_dot(near_by_image[:, :ROWS], images[...]) + t_dot(by_near_image[:, :ROWS], i2[...])
+    own_image[...] = dot(near_by_text[pl.ds(0, ROWS), :], texts[...]) + dot(by_far_text[pl.ds(0, ROWS), :], pair[...])
 
 
 def far(scalar_ref, i2, s1, sx, images, texts, image_inverse, text_inverse, loss_in,
@@ -124,19 +123,16 @@
 
 
 def sums(core_ref, by_near_text, by_near_image, by_far_text, by_far_image, i2, four, pair, texts,
-         ht0, ht1, hs0, htx, hi, own_text, own_image, blocks):
+         ht1, hs0, htx, hi, blocks):
     second = core_ref[0]
 
     def put(on_first, on_second, value):
         at = pl.multiple_of((on_first + (on_second - on_first) * second) * ROWS, ROWS)
         blocks[pl.ds(at, ROWS), :] = value
 
-    for n, old in enumerate((ht0, ht1, hs0)):
+    for n, old in ((1, ht1), (2, hs0)):
         value = old[...] + t_dot(by_near_image[:, n * ROWS:(n + 1) * ROWS], i2[...])
-        if n == 0:
-            own_text[...] = value
-        else:
-            put(7 + 2 * (n - 1), 1 + 2 * (n - 1) + 1, value)
+        put(7 + 2 * (n - 1), 1 + 2 * (n - 1) + 1, value)
     for n in range(3):
         value = htx[pl.ds(n * ROWS, ROWS), :] + t_dot(
             by_near_image[:, (n + 3) * ROWS:(n + 4) * ROWS], i2[...])
@@ -148,12 +144,11 @@
     put(11, 6, value[:ROWS])
     put(12, 5, value[ROWS:])
     for n in range(3):
-        put(2 + 2 * n, 7 + 2 * n, jnp.zeros_like(own_text))
-    rest = dot(by_far_text[...], pair[...])
-    own_image[...] = hi[pl.ds(0, ROWS), :] + rest[:ROWS]
+        put(2 + 2 * n, 7 + 2 * n, jnp.zeros_like(i2, dtype=F32))
+    rest = dot(by_far_text[pl.ds(ROWS, 3 * ROWS), :], pair[...])
     for n in (1, 2):
-        put(2 * n - 1, 6 + 2 * n, hi[pl.ds(n * ROWS, ROWS), :] + rest[n * ROWS:(n + 1) * ROWS])
-    put(5, 12, dot(by_near_text[...], texts[...]) + rest[3 * ROWS:])
+        put(2 * n - 1, 6 + 2 * n, hi[pl.ds((n - 1) * ROWS, ROWS), :] + rest[(n - 1) * ROWS:n * ROWS])
+    put(5, 12, dot(by_near_text[...], texts[...]) + rest[2 * ROWS:])
 
 
 def everyone(loss, out):
@@ -231,9 +226,9 @@
     i0, t0 = image_embed, text_embed
     block = ((ROWS, width), F32)
 
-    s0, t1 = move(t0, outer), move(t0, inner)
+    t1, s0 = move(t0, inner), move(t0, outer)
     ia, ib, t0x = move(i0, up), move(i0, down), swap_cores(t0)
-    s0, t1 = together(s0, t1)
+    t1, s0 = together(t1, s0)
     s1 = move(jnp.where(first, t1, s0), outer, inner)
     ia, ib, t0x, t1, s0 = together(ia, ib, t0x, t1, s0)
     i2 = move(jnp.where(first, ia, ib), up, down)
@@ -246,8 +241,8 @@
         8.0, 20, scalars, i0, ia, ib, t0, t1, s0, t0x, t1x, s0x)
     s1, loss = together(s1, loss)
     sx = swap_cores(s1)
-    ht0, ht1, hs0, htx, hi = call(
-        near_sums, (block, block, block, ((3 * ROWS, width), F32), ((3 * ROWS, width), F32)), 4.0, 20,
+    ht1, hs0, htx, hi = call(
+        near_sums, (block, block, ((3 * ROWS, width), F32), ((2 * ROWS, width), F32)), 4.0, 20,
         near_by_text, near_by_image, images, texts)
     loss, by_near_text, by_near_image, by_far_text, by_far_image, four, pair = call(
         far,
@@ -255,23 +250,25 @@
          ((4 * ROWS, 2 * ROWS), BF16), ((4 * ROWS, width), BF16), ((2 * ROWS, width), BF16)),
         2.0, 16, scalars, i2, s1, sx, images, texts, image_inverse, text_inverse, loss)
     loss_y = lax.ppermute(loss, "y", [(i, i ^ 1) for i in range(4)])
-    own_text, own_image, blocks = call(
-        sums, (block, block, ((13 * ROWS, width), F32)), 4.0, 28, core,
-        by_near_text, by_near_image, by_far_text, by_far_image, i2, four, pair, texts, ht0, ht1, hs0, htx, hi)
+    blocks, = call(
+        sums, (((13 * ROWS, width), F32),), 4.0, 28, core,
+        by_near_text, by_near_image, by_far_text, by_far_image, i2, four, pair, texts, ht1, hs0, htx, hi)
     loss = loss + loss_y
     blocks, loss = together(blocks, loss)
     message = narrow(blocks[:7 * ROWS])
     other = swap_cores(message)
     loss = loss + move(loss, inner)
-    other, loss = together(other, loss)
+    own_text, own_image = call(
+        own_sums, (block, block), 2.0, 20,
+        near_by_text, near_by_image, by_near_image, by_far_text, images, texts, i2, pair)
+    other, loss, own_text, own_image = together(other, loss, own_text, own_image)
     loss = loss + lax.ppermute(loss, "y", [(i, i ^ 2) for i in range(4)])
     own_text = own_text + widen(other[:ROWS])
     outs = [
         narrow(blocks[n * ROWS:(n + 2) * ROWS] + widen(other[(n - 6) * ROWS:(n - 4) * ROWS])) for n in (7, 9, 11)]
-    back = (
-        move(outs[0], inner, down),
-        move(outs[1], outer_back, up),
-        move(outs[2], far_back, across))
+    back_far = move(outs[2], far_back, across)
+    back_outer = move(outs[1], outer_back, up)
+    back = (back_far, back_outer, move(outs[0], inner, down))
     loss, = call(everyone, (((32, 128), F32),), 20.0, 4, loss)
     loss = lax.all_to_all(loss, ("z", "xh", "c"), 0, 0, tiled=True)
     *back, loss = together(*back, loss)

time: 69.3 us -> 67.9 us (0.980)
  starting transfers between devices: 25.1 us -> 24 us
    ppermute x10, starting transfers between devices: 12.8 us -> 11.3 us  [move(): return lax.ppermute(block, AXES, route)]
    pallas_call x6 -> x7, Pallas kernels: 11.2 us -> 11.3 us  [call(): pl.pallas_call(kernel, out_shape=shapes, in_specs=[SMEM if a.ndim == 1 el...]
where the time goes in v6:
time: 67.9 us; the launch traced here: 67.8 us
  starting transfers between devices  24 us (35%)
  blocking collectives  17.5 us (26%)
  Pallas kernels  11.3 us (17%)
  waiting for transfers between devices  10.8 us (16%)
  between operations  2.31 us (3%)
  other arithmetic  1.86 us (3%)
    all_to_all x1, blocking collectives, body(): loss = lax.all_to_all(loss, ('z', 'xh', 'c'), 0, 0, tiled=True)  17.5 us
    pallas_call x7, Pallas kernels, call(): pl.pallas_call(kernel, out_shape=shapes, in_specs=[SMEM if a.ndim == 1 el...  11.3 us
    ppermute x10, starting transfers between devices, move(): return lax.ppermute(block, AXES, route)  11.3 us
    ppermute x10, waiting for transfers between devices, move(): return lax.ppermute(block, AXES, route)  8.28 us
    ppermute x6, starting transfers between devices, swap_cores(): return lax.ppermute(block, 'c', [(0, 1), (1, 0)])  8.26 us
    ppermute x1, starting transfers between devices, body(): loss = loss + lax.ppermute(loss, 'y', [(i, i ^ 2) for i in range(4)])  2.92 us
    ppermute x6, waiting for transfers between devices, swap_cores(): return lax.ppermute(block, 'c', [(0, 1), (1, 0)])  2.48 us
    ppermute x1, starting transfers between devices, body(): loss_y = lax.ppermute(loss, 'y', [(i, i ^ 1) for i in range(4)])  1.56 us
  transfers between devices with their start and end apart: 18, of which 4 were waited for; matrix products, arithmetic and copies ran while one was open for 1% of the time, Pallas kernels for 10%

profile of v6, /device:TPU:1, one launch (start us, length us, event | category | flops | bytes accessed | tf_op | source)
XLA Modules:
  0.0 67.8 jit_solution(15178156480952222699)
XLA Ops:
  0.7 3.4 %collective-permute-start.4 = (bf16[128,1152]{1,0:T(8,128)(2,1)}, bf16[128,1152]{1,0:T(8,128)(2,1)S(1)}, u32[]{:S(2)}, u32[]{:S(2)}) collective-permute-start(bf16[128,1152]{1,0:T(8,128)(2,1)} %text.1), channel_id=1, source_target_pairs={{0,24},{1,25},{2,26},{3,27},{4,28},{5,29},{6,30},{7,31},{8,16},{9,... | collective-permute-start | bytes 884744 | tf_op jit(solution)/shard_map/ppermute | solution.py:202
  4.0 0.0 collective-permute-start.3
  4.0 2.7 %collective-permute-start.1 = (bf16[128,1152]{1,0:T(8,128)(2,1)}, bf16[128,1152]{1,0:T(8,128)(2,1)S(1)}, u32[]{:S(2)}, u32[]{:S(2)}) collective-permute-start(bf16[128,1152]{1,0:T(8,128)(2,1)} %image.1), channel_id=1, source_target_pairs={{0,6},{1,7},{2,0},{3,1},{4,2},{5,3},{6,4},{7,5},{8,14},{9,15},{10,... | collective-permute-start | bytes 884744 | tf_op jit(solution)/shard_map/ppermute | solution.py:202
  6.8 0.0 collective-permute-start
  6.8 1.5 %collective-permute-start.2 = (bf16[128,1152]{1,0:T(8,128)(2,1)}, bf16[128,1152]{1,0:T(8,128)(2,1)S(1)}, u32[]{:S(2)}, u32[]{:S(2)}) collective-permute-start(bf16[128,1152]{1,0:T(8,128)(2,1)} %text.1), channel_id=1, source_target_pairs={{0,1},{1,0},{2,3},{3,2},{4,5},{5,4},{6,7},{7,6},{8,9},{9,8},{10,11... | collective-permute-start | bytes 884744 | tf_op jit(solution)/shard_map/ppermute | solution.py:206
  9.6 0.1 pad_maximum_fusion.scalar_ref
  9.7 6.6 %collective-permute-done.4.s0 = bf16[128,1152]{1,0:T(8,128)(2,1)S(1)} collective-permute-done((bf16[128,1152]{1,0:T(8,128)(2,1)}, bf16[128,1152]{1,0:T(8,128)(2,1)S(1)}, u32[]{:S(2)}, u32[]{:S(2)}) %collective-permute-start.4) | collective-permute-done | bytes 294944 | tf_op jit(solution)/shard_map/ppermute | solution.py:202
  16.3 0.0 collective-permute-done.3.t1
  16.3 0.1 collective-permute-start.6
  16.4 0.0 collective-permute-done.1.ib
  16.4 0.0 collective-permute-done.ia
  16.4 0.0 collective-permute-done.2.t0x
  16.4 1.3 %collective-permute-start.7 = (bf16[128,1152]{1,0:T(8,128)(2,1)S(1)}, bf16[128,1152]{1,0:T(8,128)(2,1)S(1)}, u32[]{:S(2)}, u32[]{:S(2)}) collective-permute-start(bf16[128,1152]{1,0:T(8,128)(2,1)S(1)} %collective-permute-done.3.t1), channel_id=1, source_target_pairs={{0,1},{1,0},{2,3},{3,2},{4,5},{5,4},{6,7},{7,6},{8,9},{9,8},{10,11... | collective-permute-start | bytes 884744 | tf_op jit(solution)/shard_map/ppermute | solution.py:206
  17.8 0.1 collective-permute-start.8
  17.9 2.8 %collective-permute-start.5 = (bf16[128,1152]{1,0:T(8,128)(2,1)S(1)}, bf16[128,1152]{1,0:T(8,128)(2,1)S(1)}, u32[]{:S(2)}, u32[]{:S(2)}) collective-permute-start(bf16[128,1152]{1,0:T(8,128)(2,1)S(1)} %broadcast_select_fusion.1), channel_id=1, source_target_pairs={{0,2},{1,7},{2,4},{3,1},{4,6},{5,3},{6,0},{7,5},{8,10},{9,15},{10,... | collective-permute-start | bytes 884744 | tf_op jit(solution)/shard_map/ppermute | solution.py:202
  20.7 0.0 collective-permute-done.7.t1x
  20.7 0.0 collective-permute-done.8.s0x
  20.7 2.9 %near.1 = (bf16[384,1152]{1,0:T(8,128)(2,1)S(1)}, bf16[768,1152]{1,0:T(8,128)(2,1)S(1)}, f32[384,128]{1,0:T(8,128)S(1)}, f32[8,768]{1,0:T(8,128)S(1)}, f32[8,128...) custom-call(f32[2]{0:T(128)S(1)} %pad_maximum_fusion.scalar_ref, ...), custom_call_target="tpu_custom_call" | custom-call | flops 8000000000 | bytes 24000000 | tf_op jit(solution)/shard_map/near/pallas_call | solution.py:21
  23.7 0.0 collective-permute-done.6.s1
  23.7 4.0 %collective-permute-start.9 = (bf16[128,1152]{1,0:T(8,128)(2,1)S(1)}, bf16[128,1152]{1,0:T(8,128)(2,1)S(1)}, u32[]{:S(2)}, u32[]{:S(2)}) collective-permute-start(bf16[128,1152]{1,0:T(8,128)(2,1)S(1)} %collective-permute-done.6.s1), channel_id=1, source_target_pairs={{0,1},{1,0},{2,3},{3,2},{4,5},{5,4},{6,7},{7,6},{8,9},{9,8},{10,11... | collective-permute-start | bytes 884744 | tf_op jit(solution)/shard_map/ppermute | solution.py:206
  27.7 1.5 %near_sums.1 = (f32[128,1152]{1,0:T(8,128)S(1)}, f32[128,1152]{1,0:T(8,128)S(1)}, f32[384,1152]{1,0:T(8,128)S(1)}, f32[256,1152]{1,0:T(8,128)S(1)}) custom-call(bf16[384,768]{1,0:T(8,128)(2,1)S(1)} %get-tuple-element.65.by_text.near_by_text, bf16[384,768]{1,0:T(8,128)(2,1)S(1)} %get-tuple-element.66.by_image.near_by_image, ...), custom_call_target="tpu_custom_call" | custom-call | flops 4000000000 | bytes 12000000 | tf_op jit(solution)/shard_map/near_sums/pallas_call | solution.py:21
  29.2 0.0 collective-permute-done.5.i2
  29.2 0.0 collective-permute-done.9.sx
  29.2 2.3 %far.1 = (f32[8,128]{1,0:T(8,128)S(1)}, bf16[128,768]{1,0:T(8,128)(2,1)S(1)}, bf16[128,768]{1,0:T(8,128)(2,1)S(1)}, bf16[512,256]{1,0:T(8,128)(2,1)S(1)}, bf16[5...) custom-call(f32[2]{0:T(128)S(1)} %pad_maximum_fusion.scalar_ref, ...), custom_call_target="tpu_custom_call" | custom-call | flops 2000000000 | bytes 6000000 | tf_op jit(solution)/shard_map/far/pallas_call | solution.py:21
  31.5 1.6 %collective-permute-start.10 = (f32[8,128]{1,0:T(8,128)S(1)}, f32[8,128]{1,0:T(8,128)S(1)}, u32[]{:S(2)}, u32[]{:S(2)}) collective-permute-start(f32[8,128]{1,0:T(8,128)S(1)} %get-tuple-element.71), channel_id=1, source_target_pairs={{0,2},{2,0},{4,6},{6,4},{1,3},{3,1},{5,7},{7,5},{8,10},{10,8},{12,... | collective-permute-start | bytes 12296 | tf_op jit(solution)/shard_map/ppermute | solution.py:252
  33.1 1.7 %sums.1 = f32[1664,1152]{1,0:T(8,128)S(1)} custom-call(s32[1]{0:T(128)} %bitcast.core_ref, bf16[128,768]{1,0:T(8,128)(2,1)S(1)} %get-tuple-element.59.by_near_text, bf16[128,768]{1,0:T(8,128)(2,1)S(1)} %get-tuple-element.60.by_near_image, bf16[512,256]{1,0:T(8,128)(2,1)S(1)} %get-tuple-element.61.by_far_text, ...), custom_call_target="tpu_custom_call" | custom-call | flops 4000000000 | bytes 12000000 | tf_op jit(solution)/shard_map/sums/pallas_call | solution.py:21
  34.8 0.0 collective-permute-done.10
  34.9 0.4 multiply_convert_fusion
  35.3 0.7 %collective-permute-start.11 = (f16[896,1152]{1,0:T(8,128)(2,1)S(1)}, f16[896,1152]{1,0:T(8,128)(2,1)S(1)}, u32[]{:S(2)}, u32[]{:S(2)}) collective-permute-start(f16[896,1152]{1,0:T(8,128)(2,1)S(1)} %multiply_convert_fusion), channel_id=1, source_target_pairs={{0,1},{1,0},{2,3},{3,2},{4,5},{5,4},{6,7},{7,6},{8,9},{9,8},{10,11... | collective-permute-start | bytes 6193160 | tf_op jit(solution)/shard_map/ppermute | solution.py:206
  36.0 0.0 collective-permute-start.12
  36.0 0.8 %own_sums.1 = (f32[128,1152]{1,0:T(8,128)S(1)}, f32[128,1152]{1,0:T(8,128)S(1)}) custom-call(bf16[384,768]{1,0:T(8,128)(2,1)S(1)} %get-tuple-element.65.by_text.near_by_text, bf16[384,768]{1,0:T(8,128)(2,1)S(1)} %get-tuple-element.66.by_image.near_by_image, bf16[128,768]{1,0:T(8,128)(2,1)S(1)} %get-tuple-element.60.by_near_image, ...), custom_call_target="tpu_custom_call" | custom-call | flops 2000000000 | bytes 6000000 | tf_op jit(solution)/shard_map/own_sums/pallas_call | solution.py:21
  36.8 1.6 %collective-permute-done.12 = f32[8,128]{1,0:T(8,128)S(1)} collective-permute-done((f32[8,128]{1,0:T(8,128)S(1)}, f32[8,128]{1,0:T(8,128)S(1)}, u32[]{:S(2)}, u32[]{:S(2)}) %collective-permute-start.12) | collective-permute-done | bytes 4128 | tf_op jit(solution)/shard_map/ppermute | solution.py:202
  38.5 1.3 %collective-permute-done.11 = f16[896,1152]{1,0:T(8,128)(2,1)S(1)} collective-permute-done((f16[896,1152]{1,0:T(8,128)(2,1)S(1)}, f16[896,1152]{1,0:T(8,128)(2,1)S(1)}, u32[]{:S(2)}, u32[]{:S(2)}) %collective-permute-start.11) | collective-permute-done | bytes 2064416 | tf_op jit(solution)/shard_map/ppermute | solution.py:206
  39.7 2.9 %collective-permute-start.16 = (f32[8,128]{1,0:T(8,128)S(1)}, f32[8,128]{1,0:T(8,128)S(1)}, u32[]{:S(2)}, u32[]{:S(2)}) collective-permute-start(f32[8,128]{1,0:T(8,128)S(1)} %add.36), channel_id=1, source_target_pairs={{0,4},{2,6},{4,0},{6,2},{1,5},{3,7},{5,1},{7,3},{8,12},{10,14},{12... | collective-permute-start | bytes 12296 | tf_op jit(solution)/shard_map/ppermute | solution.py:265
  42.6 0.7 %multiply_convert_fusion.1 = (f16[256,1152]{1,0:T(8,128)(2,1)S(1)}, f16[256,1152]{1,0:T(8,128)(2,1)S(1)}, f16[256,1152]{1,0:T(8,128)(2,1)S(1)}) fusion(f32[1664,1152]{1,0:T(8,128)S(1)} %sums.1, f16[896,1152]{1,0:T(8,128)(2,1)S(1)} %collective-permute-done.11), kind=kLoop, calls=%fused_computation.2 | loop fusion | flops 4423680 | bytes 7077888 | tf_op jit(solution)/shard_map/convert_element_type | solution.py:210
  43.4 0.8 %collective-permute-start.15 = (f16[256,1152]{1,0:T(8,128)(2,1)S(1)}, f16[256,1152]{1,0:T(8,128)(2,1)S(1)}, u32[]{:S(2)}, u32[]{:S(2)}) collective-permute-start(f16[256,1152]{1,0:T(8,128)(2,1)S(1)} %get-tuple-element.87), channel_id=1, source_target_pairs={{0,8},{1,7},{2,10},{3,1},{4,12},{5,3},{6,14},{7,5},{8,0},{9,15},{1... | collective-permute-start | bytes 1769480 | tf_op jit(solution)/shard_map/ppermute | solution.py:202
  44.2 0.7 %collective-permute-start.14 = (f16[256,1152]{1,0:T(8,128)(2,1)S(1)}, f16[256,1152]{1,0:T(8,128)(2,1)S(1)}, u32[]{:S(2)}, u32[]{:S(2)}) collective-permute-start(f16[256,1152]{1,0:T(8,128)(2,1)S(1)} %get-tuple-element.88), channel_id=1, source_target_pairs={{0,248},{1,3},{2,250},{3,5},{4,252},{5,7},{6,254},{7,1},{8,240},{9... | collective-permute-start | bytes 1769480 | tf_op jit(solution)/shard_map/ppermute | solution.py:202
  44.9 0.7 %collective-permute-start.13 = (f16[256,1152]{1,0:T(8,128)(2,1)S(1)}, f16[256,1152]{1,0:T(8,128)(2,1)S(1)}, u32[]{:S(2)}, u32[]{:S(2)}) collective-permute-start(f16[256,1152]{1,0:T(8,128)(2,1)S(1)} %get-tuple-element.89), channel_id=1, source_target_pairs={{0,240},{1,5},{2,242},{3,7},{4,244},{5,1},{6,246},{7,3},{8,248},{9... | collective-permute-start | bytes 1769480 | tf_op jit(solution)/shard_map/ppermute | solution.py:202
  45.7 0.0 collective-permute-done.16
  45.7 17.5 %all_to_all.12 = f32[32,1,128]{2,1,0:T(1,128)S(1)} all-to-all(f32[32,1,128]{2,1,0:T(1,128)S(1)} %bitcast.6), channel_id=1, replica_groups=mesh['z'=8,'xh'=2,'xl'=2,'y'=4,'c'=2] {'z','xh','c'}, dimensions={0} | all-to-all | bytes 32768 | tf_op jit(solution)/shard_map/all_to_all | solution.py:273
  63.2 0.0 collective-permute-done.15
  63.2 0.0 collective-permute-done.13
  63.2 0.2 add_multiply_fusion
  63.4 0.1 multiply_convert_fusion.4
  63.5 0.7 %collective-permute-start.17 = (f16[128,1152]{1,0:T(8,128)(2,1)S(1)}, f16[128,1152]{1,0:T(8,128)(2,1)S(1)}, u32[]{:S(2)}, u32[]{:S(2)}) collective-permute-start(f16[128,1152]{1,0:T(8,128)(2,1)S(1)} %multiply_convert_fusion.4), channel_id=1, source_target_pairs={{0,1},{1,0},{2,3},{3,2},{4,5},{5,4},{6,7},{7,6},{8,9},{9,8},{10,11... | collective-permute-start | bytes 884744 | tf_op jit(solution)/shard_map/ppermute | solution.py:206
  64.2 1.2 %collective-permute-done.17 = f16[128,1152]{1,0:T(8,128)(2,1)S(1)} collective-permute-done((f16[128,1152]{1,0:T(8,128)(2,1)S(1)}, f16[128,1152]{1,0:T(8,128)(2,1)S(1)}, u32[]{:S(2)}, u32[]{:S(2)}) %collective-permute-start.17) | collective-permute-done | bytes 294944 | tf_op jit(solution)/shard_map/ppermute | solution.py:206
  65.4 0.2 select_add_fusion
  65.6 2.0 %finish.1 = (f32[128,1152]{1,0:T(8,128)}, f32[128,1152]{1,0:T(8,128)}, f32[1]{0:T(128)}) custom-call(f32[2]{0:T(128)S(1)} %pad_maximum_fusion.scalar_ref, bf16[128,1152]{1,0:T(8,128)(2,1)S(1)} %copy-done, bf16[128,1152]{1,0:T(8,128)(2,1)S(1)} %copy-done.1, f32[128,1152]{1,0:T(8,128)S(1)} %get-tuple-element.91.image_hat, ...), custom_call_target="tpu_custom_call" | custom-call | flops 20000000000 | bytes 60000000 | tf_op jit(solution)/shard_map/finish/pallas_call | solution.py:21
  (11 shorter events, 0.1 us)
Async XLA Ops:
  0.6 20.1 %copy-start.1 = (bf16[128,1152]{1,0:T(8,128)(2,1)S(1)}, bf16[128,1152]{1,0:T(8,128)(2,1)}, u32[]{:S(2)}) copy-start(bf16[128,1152]{1,0:T(8,128)(2,1)} %text.1) | copy-start | bytes 884740
  0.6 20.1 %copy-start = (bf16[128,1152]{1,0:T(8,128)(2,1)S(1)}, bf16[128,1152]{1,0:T(8,128)(2,1)}, u32[]{:S(2)}) copy-start(bf16[128,1152]{1,0:T(8,128)(2,1)} %image.1) | copy-start | bytes 884740
  0.7 15.6 %collective-permute-start.4 = (bf16[128,1152]{1,0:T(8,128)(2,1)}, bf16[128,1152]{1,0:T(8,128)(2,1)S(1)}, u32[]{:S(2)}, u32[]{:S(2)}) collective-permute-start(bf16[128,1152]{1,0:T(8,128)(2,1)} %text.1), channel_id=1, source_target_pairs={{0,24},{1,25},{2,26},{3,27},{4,28},{5,29},{6,30},{7,31},{8,16},{9,... | collective-permute-start | bytes 884744 | tf_op jit(solution)/shard_map/ppermute | solution.py:202
  4.0 12.2 %collective-permute-start.3 = (bf16[128,1152]{1,0:T(8,128)(2,1)}, bf16[128,1152]{1,0:T(8,128)(2,1)S(1)}, u32[]{:S(2)}, u32[]{:S(2)}) collective-permute-start(bf16[128,1152]{1,0:T(8,128)(2,1)} %text.1), channel_id=1, source_target_pairs={{0,8},{1,9},{2,10},{3,11},{4,12},{5,13},{6,14},{7,15},{8,0},{9,1},... | collective-permute-start | bytes 884744 | tf_op jit(solution)/shard_map/ppermute | solution.py:202
  4.0 12.4 %collective-permute-start.1 = (bf16[128,1152]{1,0:T(8,128)(2,1)}, bf16[128,1152]{1,0:T(8,128)(2,1)S(1)}, u32[]{:S(2)}, u32[]{:S(2)}) collective-permute-start(bf16[128,1152]{1,0:T(8,128)(2,1)} %image.1), channel_id=1, source_target_pairs={{0,6},{1,7},{2,0},{3,1},{4,2},{5,3},{6,4},{7,5},{8,14},{9,15},{10,... | collective-permute-start | bytes 884744 | tf_op jit(solution)/shard_map/ppermute | solution.py:202
  6.8 9.6 %collective-permute-start = (bf16[128,1152]{1,0:T(8,128)(2,1)}, bf16[128,1152]{1,0:T(8,128)(2,1)S(1)}, u32[]{:S(2)}, u32[]{:S(2)}) collective-permute-start(bf16[128,1152]{1,0:T(8,128)(2,1)} %image.1), channel_id=1, source_target_pairs={{0,2},{1,3},{2,4},{3,5},{4,6},{5,7},{6,0},{7,1},{8,10},{9,11},{10,... | collective-permute-start | bytes 884744 | tf_op jit(solution)/shard_map/ppermute | solution.py:202
  6.8 9.7 %collective-permute-start.2 = (bf16[128,1152]{1,0:T(8,128)(2,1)}, bf16[128,1152]{1,0:T(8,128)(2,1)S(1)}, u32[]{:S(2)}, u32[]{:S(2)}) collective-permute-start(bf16[128,1152]{1,0:T(8,128)(2,1)} %text.1), channel_id=1, source_target_pairs={{0,1},{1,0},{2,3},{3,2},{4,5},{5,4},{6,7},{7,6},{8,9},{9,8},{10,11... | collective-permute-start | bytes 884744 | tf_op jit(solution)/shard_map/ppermute | solution.py:206
  16.3 7.3 %collective-permute-start.6 = (bf16[128,1152]{1,0:T(8,128)(2,1)S(1)}, bf16[128,1152]{1,0:T(8,128)(2,1)S(1)}, u32[]{:S(2)}, u32[]{:S(2)}) collective-permute-start(bf16[128,1152]{1,0:T(8,128)(2,1)S(1)} %broadcast_select_fusion), channel_id=1, source_target_pairs={{0,24},{1,9},{2,26},{3,11},{4,28},{5,13},{6,30},{7,15},{8,16},{9,1... | collective-permute-start | bytes 884744 | tf_op jit(solution)/shard_map/ppermute | solution.py:202
  16.4 4.3 %collective-permute-start.7 = (bf16[128,1152]{1,0:T(8,128)(2,1)S(1)}, bf16[128,1152]{1,0:T(8,128)(2,1)S(1)}, u32[]{:S(2)}, u32[]{:S(2)}) collective-permute-start(bf16[128,1152]{1,0:T(8,128)(2,1)S(1)} %collective-permute-done.3.t1), channel_id=1, source_target_pairs={{0,1},{1,0},{2,3},{3,2},{4,5},{5,4},{6,7},{7,6},{8,9},{9,8},{10,11... | collective-permute-start | bytes 884744 | tf_op jit(solution)/shard_map/ppermute | solution.py:206
  17.8 3.0 %collective-permute-start.8 = (bf16[128,1152]{1,0:T(8,128)(2,1)S(1)}, bf16[128,1152]{1,0:T(8,128)(2,1)S(1)}, u32[]{:S(2)}, u32[]{:S(2)}) collective-permute-start(bf16[128,1152]{1,0:T(8,128)(2,1)S(1)} %collective-permute-done.4.s0), channel_id=1, source_target_pairs={{0,1},{1,0},{2,3},{3,2},{4,5},{5,4},{6,7},{7,6},{8,9},{9,8},{10,11... | collective-permute-start | bytes 884744 | tf_op jit(solution)/shard_map/ppermute | solution.py:206
  17.9 11.3 %collective-permute-start.5 = (bf16[128,1152]{1,0:T(8,128)(2,1)S(1)}, bf16[128,1152]{1,0:T(8,128)(2,1)S(1)}, u32[]{:S(2)}, u32[]{:S(2)}) collective-permute-start(bf16[128,1152]{1,0:T(8,128)(2,1)S(1)} %broadcast_select_fusion.1), channel_id=1, source_target_pairs={{0,2},{1,7},{2,4},{3,1},{4,6},{5,3},{6,0},{7,5},{8,10},{9,15},{10,... | collective-permute-start | bytes 884744 | tf_op jit(solution)/shard_map/ppermute | solution.py:202
  23.7 5.5 %collective-permute-start.9 = (bf16[128,1152]{1,0:T(8,128)(2,1)S(1)}, bf16[128,1152]{1,0:T(8,128)(2,1)S(1)}, u32[]{:S(2)}, u32[]{:S(2)}) collective-permute-start(bf16[128,1152]{1,0:T(8,128)(2,1)S(1)} %collective-permute-done.6.s1), channel_id=1, source_target_pairs={{0,1},{1,0},{2,3},{3,2},{4,5},{5,4},{6,7},{7,6},{8,9},{9,8},{10,11... | collective-permute-start | bytes 884744 | tf_op jit(solution)/shard_map/ppermute | solution.py:206
  31.5 3.3 %collective-permute-start.10 = (f32[8,128]{1,0:T(8,128)S(1)}, f32[8,128]{1,0:T(8,128)S(1)}, u32[]{:S(2)}, u32[]{:S(2)}) collective-permute-start(f32[8,128]{1,0:T(8,128)S(1)} %get-tuple-element.71), channel_id=1, source_target_pairs={{0,2},{2,0},{4,6},{6,4},{1,3},{3,1},{5,7},{7,5},{8,10},{10,8},{12,... | collective-permute-start | bytes 12296 | tf_op jit(solution)/shard_map/ppermute | solution.py:252
  35.3 4.4 %collective-permute-start.11 = (f16[896,1152]{1,0:T(8,128)(2,1)S(1)}, f16[896,1152]{1,0:T(8,128)(2,1)S(1)}, u32[]{:S(2)}, u32[]{:S(2)}) collective-permute-start(f16[896,1152]{1,0:T(8,128)(2,1)S(1)} %multiply_convert_fusion), channel_id=1, source_target_pairs={{0,1},{1,0},{2,3},{3,2},{4,5},{5,4},{6,7},{7,6},{8,9},{9,8},{10,11... | collective-permute-start | bytes 6193160 | tf_op jit(solution)/shard_map/ppermute | solution.py:206
  36.0 2.5 %collective-permute-start.12 = (f32[8,128]{1,0:T(8,128)S(1)}, f32[8,128]{1,0:T(8,128)S(1)}, u32[]{:S(2)}, u32[]{:S(2)}) collective-permute-start(f32[8,128]{1,0:T(8,128)S(1)} %add.35), channel_id=1, source_target_pairs={{0,8},{1,9},{2,10},{3,11},{4,12},{5,13},{6,14},{7,15},{8,0},{9,1},... | collective-permute-start | bytes 12296 | tf_op jit(solution)/shard_map/ppermute | solution.py:202
  39.7 5.9 %collective-permute-start.16 = (f32[8,128]{1,0:T(8,128)S(1)}, f32[8,128]{1,0:T(8,128)S(1)}, u32[]{:S(2)}, u32[]{:S(2)}) collective-permute-start(f32[8,128]{1,0:T(8,128)S(1)} %add.36), channel_id=1, source_target_pairs={{0,4},{2,6},{4,0},{6,2},{1,5},{3,7},{5,1},{7,3},{8,12},{10,14},{12... | collective-permute-start | bytes 12296 | tf_op jit(solution)/shard_map/ppermute | solution.py:265
  43.4 19.8 %collective-permute-start.15 = (f16[256,1152]{1,0:T(8,128)(2,1)S(1)}, f16[256,1152]{1,0:T(8,128)(2,1)S(1)}, u32[]{:S(2)}, u32[]{:S(2)}) collective-permute-start(f16[256,1152]{1,0:T(8,128)(2,1)S(1)} %get-tuple-element.87), channel_id=1, source_target_pairs={{0,8},{1,7},{2,10},{3,1},{4,12},{5,3},{6,14},{7,5},{8,0},{9,15},{1... | collective-permute-start | bytes 1769480 | tf_op jit(solution)/shard_map/ppermute | solution.py:202
  44.2 18.9 %collective-permute-start.14 = (f16[256,1152]{1,0:T(8,128)(2,1)S(1)}, f16[256,1152]{1,0:T(8,128)(2,1)S(1)}, u32[]{:S(2)}, u32[]{:S(2)}) collective-permute-start(f16[256,1152]{1,0:T(8,128)(2,1)S(1)} %get-tuple-element.88), channel_id=1, source_target_pairs={{0,248},{1,3},{2,250},{3,5},{4,252},{5,7},{6,254},{7,1},{8,240},{9... | collective-permute-start | bytes 1769480 | tf_op jit(solution)/shard_map/ppermute | solution.py:202
  44.9 18.2 %collective-permute-start.13 = (f16[256,1152]{1,0:T(8,128)(2,1)S(1)}, f16[256,1152]{1,0:T(8,128)(2,1)S(1)}, u32[]{:S(2)}, u32[]{:S(2)}) collective-permute-start(f16[256,1152]{1,0:T(8,128)(2,1)S(1)} %get-tuple-element.89), channel_id=1, source_target_pairs={{0,240},{1,5},{2,242},{3,7},{4,244},{5,1},{6,246},{7,3},{8,248},{9... | collective-permute-start | bytes 1769480 | tf_op jit(solution)/shard_map/ppermute | solution.py:202
  63.5 1.9 %collective-permute-start.17 = (f16[128,1152]{1,0:T(8,128)(2,1)S(1)}, f16[128,1152]{1,0:T(8,128)(2,1)S(1)}, u32[]{:S(2)}, u32[]{:S(2)}) collective-permute-start(f16[128,1152]{1,0:T(8,128)(2,1)S(1)} %multiply_convert_fusion.4), channel_id=1, source_target_pairs={{0,1},{1,0},{2,3},{3,2},{4,5},{5,4},{6,7},{7,6},{8,9},{9,8},{10,11... | collective-permute-start | bytes 884744 | tf_op jit(solution)/shard_map/ppermute | solution.py:206

commit v7 on v6

--- a/solution.py
+++ b/solution.py
@@ -207,11 +207,11 @@
 
 
 def narrow(block):
-    return (block * 32.0).astype(jnp.float16)
+    return (block * 16.0).astype(jnp.float16)
 
 
 def widen(block):
-    return block.astype(F32) * (1.0 / 32.0)
+    return block.astype(F32) * (1.0 / 16.0)
 
 
 def together(*arrays):

time: 67.9 us -> 67.9 us (level)
  no operation moved by 1% of the time
where the time goes in v7:
time: 67.9 us; the launch traced here: 67.8 us
  starting transfers between devices  24 us (35%)
  blocking collectives  17.5 us (26%)
  Pallas kernels  11.3 us (17%)
  waiting for transfers between devices  10.8 us (16%)
  between operations  2.31 us (3%)
  other arithmetic  1.86 us (3%)
    all_to_all x1, blocking collectives, body(): loss = lax.all_to_all(loss, ('z', 'xh', 'c'), 0, 0, tiled=True)  17.5 us
    pallas_call x7, Pallas kernels, call(): pl.pallas_call(kernel, out_shape=shapes, in_specs=[SMEM if a.ndim == 1 el...  11.3 us
    ppermute x10, starting transfers between devices, move(): return lax.ppermute(block, AXES, route)  11.3 us
    ppermute x10, waiting for transfers between devices, move(): return lax.ppermute(block, AXES, route)  8.28 us
    ppermute x6, starting transfers between devices, swap_cores(): return lax.ppermute(block, 'c', [(0, 1), (1, 0)])  8.26 us
    ppermute x1, starting transfers between devices, body(): loss = loss + lax.ppermute(loss, 'y', [(i, i ^ 2) for i in range(4)])  2.92 us
    ppermute x6, waiting for transfers between devices, swap_cores(): return lax.ppermute(block, 'c', [(0, 1), (1, 0)])  2.48 us
    ppermute x1, starting transfers between devices, body(): loss_y = lax.ppermute(loss, 'y', [(i, i ^ 1) for i in range(4)])  1.56 us
  transfers between devices with their start and end apart: 18, of which 4 were waited for; matrix products, arithmetic and copies ran while one was open for 1% of the time, Pallas kernels for 10%

profile of v7, /device:TPU:1, one launch (start us, length us, event | category | flops | bytes accessed | tf_op | source)
XLA Modules:
  0.0 67.8 jit_solution(12708665548613636196)
XLA Ops:
  0.7 3.4 %collective-permute-start.4 = (bf16[128,1152]{1,0:T(8,128)(2,1)}, bf16[128,1152]{1,0:T(8,128)(2,1)S(1)}, u32[]{:S(2)}, u32[]{:S(2)}) collective-permute-start(bf16[128,1152]{1,0:T(8,128)(2,1)} %text.1), channel_id=1, source_target_pairs={{0,24},{1,25},{2,26},{3,27},{4,28},{5,29},{6,30},{7,31},{8,16},{9,... | collective-permute-start | bytes 884744 | tf_op jit(solution)/shard_map/ppermute | solution.py:202
  4.0 0.0 collective-permute-start.3
  4.0 2.7 %collective-permute-start.1 = (bf16[128,1152]{1,0:T(8,128)(2,1)}, bf16[128,1152]{1,0:T(8,128)(2,1)S(1)}, u32[]{:S(2)}, u32[]{:S(2)}) collective-permute-start(bf16[128,1152]{1,0:T(8,128)(2,1)} %image.1), channel_id=1, source_target_pairs={{0,6},{1,7},{2,0},{3,1},{4,2},{5,3},{6,4},{7,5},{8,14},{9,15},{10,... | collective-permute-start | bytes 884744 | tf_op jit(solution)/shard_map/ppermute | solution.py:202
  6.8 0.0 collective-permute-start
  6.8 1.5 %collective-permute-start.2 = (bf16[128,1152]{1,0:T(8,128)(2,1)}, bf16[128,1152]{1,0:T(8,128)(2,1)S(1)}, u32[]{:S(2)}, u32[]{:S(2)}) collective-permute-start(bf16[128,1152]{1,0:T(8,128)(2,1)} %text.1), channel_id=1, source_target_pairs={{0,1},{1,0},{2,3},{3,2},{4,5},{5,4},{6,7},{7,6},{8,9},{9,8},{10,11... | collective-permute-start | bytes 884744 | tf_op jit(solution)/shard_map/ppermute | solution.py:206
  9.6 0.1 pad_maximum_fusion.scalar_ref
  9.7 6.6 %collective-permute-done.4.s0 = bf16[128,1152]{1,0:T(8,128)(2,1)S(1)} collective-permute-done((bf16[128,1152]{1,0:T(8,128)(2,1)}, bf16[128,1152]{1,0:T(8,128)(2,1)S(1)}, u32[]{:S(2)}, u32[]{:S(2)}) %collective-permute-start.4) | collective-permute-done | bytes 294944 | tf_op jit(solution)/shard_map/ppermute | solution.py:202
  16.3 0.0 collective-permute-done.3.t1
  16.3 0.1 collective-permute-start.6
  16.4 0.0 collective-permute-done.1.ib
  16.4 0.0 collective-permute-done.ia
  16.4 0.0 collective-permute-done.2.t0x
  16.4 1.3 %collective-permute-start.7 = (bf16[128,1152]{1,0:T(8,128)(2,1)S(1)}, bf16[128,1152]{1,0:T(8,128)(2,1)S(1)}, u32[]{:S(2)}, u32[]{:S(2)}) collective-permute-start(bf16[128,1152]{1,0:T(8,128)(2,1)S(1)} %collective-permute-done.3.t1), channel_id=1, source_target_pairs={{0,1},{1,0},{2,3},{3,2},{4,5},{5,4},{6,7},{7,6},{8,9},{9,8},{10,11... | collective-permute-start | bytes 884744 | tf_op jit(solution)/shard_map/ppermute | solution.py:206
  17.8 0.1 collective-permute-start.8
  17.9 2.8 %collective-permute-start.5 = (bf16[128,1152]{1,0:T(8,128)(2,1)S(1)}, bf16[128,1152]{1,0:T(8,128)(2,1)S(1)}, u32[]{:S(2)}, u32[]{:S(2)}) collective-permute-start(bf16[128,1152]{1,0:T(8,128)(2,1)S(1)} %broadcast_select_fusion.1), channel_id=1, source_target_pairs={{0,2},{1,7},{2,4},{3,1},{4,6},{5,3},{6,0},{7,5},{8,10},{9,15},{10,... | collective-permute-start | bytes 884744 | tf_op jit(solution)/shard_map/ppermute | solution.py:202
  20.7 0.0 collective-permute-done.7.t1x
  20.7 0.0 collective-permute-done.8.s0x
  20.7 2.9 %near.1 = (bf16[384,1152]{1,0:T(8,128)(2,1)S(1)}, bf16[768,1152]{1,0:T(8,128)(2,1)S(1)}, f32[384,128]{1,0:T(8,128)S(1)}, f32[8,768]{1,0:T(8,128)S(1)}, f32[8,128...) custom-call(f32[2]{0:T(128)S(1)} %pad_maximum_fusion.scalar_ref, ...), custom_call_target="tpu_custom_call" | custom-call | flops 8000000000 | bytes 24000000 | tf_op jit(solution)/shard_map/near/pallas_call | solution.py:21
  23.7 0.0 collective-permute-done.6.s1
  23.7 4.0 %collective-permute-start.9 = (bf16[128,1152]{1,0:T(8,128)(2,1)S(1)}, bf16[128,1152]{1,0:T(8,128)(2,1)S(1)}, u32[]{:S(2)}, u32[]{:S(2)}) collective-permute-start(bf16[128,1152]{1,0:T(8,128)(2,1)S(1)} %collective-permute-done.6.s1), channel_id=1, source_target_pairs={{0,1},{1,0},{2,3},{3,2},{4,5},{5,4},{6,7},{7,6},{8,9},{9,8},{10,11... | collective-permute-start | bytes 884744 | tf_op jit(solution)/shard_map/ppermute | solution.py:206
  27.7 1.5 %near_sums.1 = (f32[128,1152]{1,0:T(8,128)S(1)}, f32[128,1152]{1,0:T(8,128)S(1)}, f32[384,1152]{1,0:T(8,128)S(1)}, f32[256,1152]{1,0:T(8,128)S(1)}) custom-call(bf16[384,768]{1,0:T(8,128)(2,1)S(1)} %get-tuple-element.65.by_text.near_by_text, bf16[384,768]{1,0:T(8,128)(2,1)S(1)} %get-tuple-element.66.by_image.near_by_image, ...), custom_call_target="tpu_custom_call" | custom-call | flops 4000000000 | bytes 12000000 | tf_op jit(solution)/shard_map/near_sums/pallas_call | solution.py:21
  29.2 0.0 collective-permute-done.5.i2
  29.2 0.0 collective-permute-done.9.sx
  29.2 2.3 %far.1 = (f32[8,128]{1,0:T(8,128)S(1)}, bf16[128,768]{1,0:T(8,128)(2,1)S(1)}, bf16[128,768]{1,0:T(8,128)(2,1)S(1)}, bf16[512,256]{1,0:T(8,128)(2,1)S(1)}, bf16[5...) custom-call(f32[2]{0:T(128)S(1)} %pad_maximum_fusion.scalar_ref, ...), custom_call_target="tpu_custom_call" | custom-call | flops 2000000000 | bytes 6000000 | tf_op jit(solution)/shard_map/far/pallas_call | solution.py:21
  31.5 1.6 %collective-permute-start.10 = (f32[8,128]{1,0:T(8,128)S(1)}, f32[8,128]{1,0:T(8,128)S(1)}, u32[]{:S(2)}, u32[]{:S(2)}) collective-permute-start(f32[8,128]{1,0:T(8,128)S(1)} %get-tuple-element.71), channel_id=1, source_target_pairs={{0,2},{2,0},{4,6},{6,4},{1,3},{3,1},{5,7},{7,5},{8,10},{10,8},{12,... | collective-permute-start | bytes 12296 | tf_op jit(solution)/shard_map/ppermute | solution.py:252
  33.1 1.7 %sums.1 = f32[1664,1152]{1,0:T(8,128)S(1)} custom-call(s32[1]{0:T(128)} %bitcast.core_ref, bf16[128,768]{1,0:T(8,128)(2,1)S(1)} %get-tuple-element.59.by_near_text, bf16[128,768]{1,0:T(8,128)(2,1)S(1)} %get-tuple-element.60.by_near_image, bf16[512,256]{1,0:T(8,128)(2,1)S(1)} %get-tuple-element.61.by_far_text, ...), custom_call_target="tpu_custom_call" | custom-call | flops 4000000000 | bytes 12000000 | tf_op jit(solution)/shard_map/sums/pallas_call | solution.py:21
  34.8 0.0 collective-permute-done.10
  34.9 0.4 multiply_convert_fusion
  35.3 0.7 %collective-permute-start.11 = (f16[896,1152]{1,0:T(8,128)(2,1)S(1)}, f16[896,1152]{1,0:T(8,128)(2,1)S(1)}, u32[]{:S(2)}, u32[]{:S(2)}) collective-permute-start(f16[896,1152]{1,0:T(8,128)(2,1)S(1)} %multiply_convert_fusion), channel_id=1, source_target_pairs={{0,1},{1,0},{2,3},{3,2},{4,5},{5,4},{6,7},{7,6},{8,9},{9,8},{10,11... | collective-permute-start | bytes 6193160 | tf_op jit(solution)/shard_map/ppermute | solution.py:206
  36.0 0.0 collective-permute-start.12
  36.0 0.8 %own_sums.1 = (f32[128,1152]{1,0:T(8,128)S(1)}, f32[128,1152]{1,0:T(8,128)S(1)}) custom-call(bf16[384,768]{1,0:T(8,128)(2,1)S(1)} %get-tuple-element.65.by_text.near_by_text, bf16[384,768]{1,0:T(8,128)(2,1)S(1)} %get-tuple-element.66.by_image.near_by_image, bf16[128,768]{1,0:T(8,128)(2,1)S(1)} %get-tuple-element.60.by_near_image, ...), custom_call_target="tpu_custom_call" | custom-call | flops 2000000000 | bytes 6000000 | tf_op jit(solution)/shard_map/own_sums/pallas_call | solution.py:21
  36.8 1.6 %collective-permute-done.12 = f32[8,128]{1,0:T(8,128)S(1)} collective-permute-done((f32[8,128]{1,0:T(8,128)S(1)}, f32[8,128]{1,0:T(8,128)S(1)}, u32[]{:S(2)}, u32[]{:S(2)}) %collective-permute-start.12) | collective-permute-done | bytes 4128 | tf_op jit(solution)/shard_map/ppermute | solution.py:202
  38.5 1.3 %collective-permute-done.11 = f16[896,1152]{1,0:T(8,128)(2,1)S(1)} collective-permute-done((f16[896,1152]{1,0:T(8,128)(2,1)S(1)}, f16[896,1152]{1,0:T(8,128)(2,1)S(1)}, u32[]{:S(2)}, u32[]{:S(2)}) %collective-permute-start.11) | collective-permute-done | bytes 2064416 | tf_op jit(solution)/shard_map/ppermute | solution.py:206
  39.7 2.9 %collective-permute-start.16 = (f32[8,128]{1,0:T(8,128)S(1)}, f32[8,128]{1,0:T(8,128)S(1)}, u32[]{:S(2)}, u32[]{:S(2)}) collective-permute-start(f32[8,128]{1,0:T(8,128)S(1)} %add.36), channel_id=1, source_target_pairs={{0,4},{2,6},{4,0},{6,2},{1,5},{3,7},{5,1},{7,3},{8,12},{10,14},{12... | collective-permute-start | bytes 12296 | tf_op jit(solution)/shard_map/ppermute | solution.py:265
  42.6 0.7 %multiply_convert_fusion.1 = (f16[256,1152]{1,0:T(8,128)(2,1)S(1)}, f16[256,1152]{1,0:T(8,128)(2,1)S(1)}, f16[256,1152]{1,0:T(8,128)(2,1)S(1)}) fusion(f32[1664,1152]{1,0:T(8,128)S(1)} %sums.1, f16[896,1152]{1,0:T(8,128)(2,1)S(1)} %collective-permute-done.11), kind=kLoop, calls=%fused_computation.2 | loop fusion | flops 4423680 | bytes 7077888 | tf_op jit(solution)/shard_map/convert_element_type | solution.py:210
  43.4 0.8 %collective-permute-start.15 = (f16[256,1152]{1,0:T(8,128)(2,1)S(1)}, f16[256,1152]{1,0:T(8,128)(2,1)S(1)}, u32[]{:S(2)}, u32[]{:S(2)}) collective-permute-start(f16[256,1152]{1,0:T(8,128)(2,1)S(1)} %get-tuple-element.87), channel_id=1, source_target_pairs={{0,8},{1,7},{2,10},{3,1},{4,12},{5,3},{6,14},{7,5},{8,0},{9,15},{1... | collective-permute-start | bytes 1769480 | tf_op jit(solution)/shard_map/ppermute | solution.py:202
  44.2 0.7 %collective-permute-start.14 = (f16[256,1152]{1,0:T(8,128)(2,1)S(1)}, f16[256,1152]{1,0:T(8,128)(2,1)S(1)}, u32[]{:S(2)}, u32[]{:S(2)}) collective-permute-start(f16[256,1152]{1,0:T(8,128)(2,1)S(1)} %get-tuple-element.88), channel_id=1, source_target_pairs={{0,248},{1,3},{2,250},{3,5},{4,252},{5,7},{6,254},{7,1},{8,240},{9... | collective-permute-start | bytes 1769480 | tf_op jit(solution)/shard_map/ppermute | solution.py:202
  44.9 0.7 %collective-permute-start.13 = (f16[256,1152]{1,0:T(8,128)(2,1)S(1)}, f16[256,1152]{1,0:T(8,128)(2,1)S(1)}, u32[]{:S(2)}, u32[]{:S(2)}) collective-permute-start(f16[256,1152]{1,0:T(8,128)(2,1)S(1)} %get-tuple-element.89), channel_id=1, source_target_pairs={{0,240},{1,5},{2,242},{3,7},{4,244},{5,1},{6,246},{7,3},{8,248},{9... | collective-permute-start | bytes 1769480 | tf_op jit(solution)/shard_map/ppermute | solution.py:202
  45.7 0.0 collective-permute-done.16
  45.7 17.5 %all_to_all.12 = f32[32,1,128]{2,1,0:T(1,128)S(1)} all-to-all(f32[32,1,128]{2,1,0:T(1,128)S(1)} %bitcast.6), channel_id=1, replica_groups=mesh['z'=8,'xh'=2,'xl'=2,'y'=4,'c'=2] {'z','xh','c'}, dimensions={0} | all-to-all | bytes 32768 | tf_op jit(solution)/shard_map/all_to_all | solution.py:273
  63.2 0.0 collective-permute-done.15
  63.2 0.0 collective-permute-done.13
  63.2 0.2 add_multiply_fusion
  63.4 0.1 multiply_convert_fusion.4
  63.5 0.7 %collective-permute-start.17 = (f16[128,1152]{1,0:T(8,128)(2,1)S(1)}, f16[128,1152]{1,0:T(8,128)(2,1)S(1)}, u32[]{:S(2)}, u32[]{:S(2)}) collective-permute-start(f16[128,1152]{1,0:T(8,128)(2,1)S(1)} %multiply_convert_fusion.4), channel_id=1, source_target_pairs={{0,1},{1,0},{2,3},{3,2},{4,5},{5,4},{6,7},{7,6},{8,9},{9,8},{10,11... | collective-permute-start | bytes 884744 | tf_op jit(solution)/shard_map/ppermute | solution.py:206
  64.2 1.2 %collective-permute-done.17 = f16[128,1152]{1,0:T(8,128)(2,1)S(1)} collective-permute-done((f16[128,1152]{1,0:T(8,128)(2,1)S(1)}, f16[128,1152]{1,0:T(8,128)(2,1)S(1)}, u32[]{:S(2)}, u32[]{:S(2)}) %collective-permute-start.17) | collective-permute-done | bytes 294944 | tf_op jit(solution)/shard_map/ppermute | solution.py:206
  65.4 0.2 select_add_fusion
  65.6 2.0 %finish.1 = (f32[128,1152]{1,0:T(8,128)}, f32[128,1152]{1,0:T(8,128)}, f32[1]{0:T(128)}) custom-call(f32[2]{0:T(128)S(1)} %pad_maximum_fusion.scalar_ref, bf16[128,1152]{1,0:T(8,128)(2,1)S(1)} %copy-done, bf16[128,1152]{1,0:T(8,128)(2,1)S(1)} %copy-done.1, f32[128,1152]{1,0:T(8,128)S(1)} %get-tuple-element.91.image_hat, ...), custom_call_target="tpu_custom_call" | custom-call | flops 20000000000 | bytes 60000000 | tf_op jit(solution)/shard_map/finish/pallas_call | solution.py:21
  (11 shorter events, 0.1 us)
Async XLA Ops:
  0.6 20.1 %copy-start.1 = (bf16[128,1152]{1,0:T(8,128)(2,1)S(1)}, bf16[128,1152]{1,0:T(8,128)(2,1)}, u32[]{:S(2)}) copy-start(bf16[128,1152]{1,0:T(8,128)(2,1)} %text.1) | copy-start | bytes 884740
  0.6 20.1 %copy-start = (bf16[128,1152]{1,0:T(8,128)(2,1)S(1)}, bf16[128,1152]{1,0:T(8,128)(2,1)}, u32[]{:S(2)}) copy-start(bf16[128,1152]{1,0:T(8,128)(2,1)} %image.1) | copy-start | bytes 884740
  0.7 15.6 %collective-permute-start.4 = (bf16[128,1152]{1,0:T(8,128)(2,1)}, bf16[128,1152]{1,0:T(8,128)(2,1)S(1)}, u32[]{:S(2)}, u32[]{:S(2)}) collective-permute-start(bf16[128,1152]{1,0:T(8,128)(2,1)} %text.1), channel_id=1, source_target_pairs={{0,24},{1,25},{2,26},{3,27},{4,28},{5,29},{6,30},{7,31},{8,16},{9,... | collective-permute-start | bytes 884744 | tf_op jit(solution)/shard_map/ppermute | solution.py:202
  4.0 12.2 %collective-permute-start.3 = (bf16[128,1152]{1,0:T(8,128)(2,1)}, bf16[128,1152]{1,0:T(8,128)(2,1)S(1)}, u32[]{:S(2)}, u32[]{:S(2)}) collective-permute-start(bf16[128,1152]{1,0:T(8,128)(2,1)} %text.1), channel_id=1, source_target_pairs={{0,8},{1,9},{2,10},{3,11},{4,12},{5,13},{6,14},{7,15},{8,0},{9,1},... | collective-permute-start | bytes 884744 | tf_op jit(solution)/shard_map/ppermute | solution.py:202
  4.0 12.4 %collective-permute-start.1 = (bf16[128,1152]{1,0:T(8,128)(2,1)}, bf16[128,1152]{1,0:T(8,128)(2,1)S(1)}, u32[]{:S(2)}, u32[]{:S(2)}) collective-permute-start(bf16[128,1152]{1,0:T(8,128)(2,1)} %image.1), channel_id=1, source_target_pairs={{0,6},{1,7},{2,0},{3,1},{4,2},{5,3},{6,4},{7,5},{8,14},{9,15},{10,... | collective-permute-start | bytes 884744 | tf_op jit(solution)/shard_map/ppermute | solution.py:202
  6.8 9.6 %collective-permute-start = (bf16[128,1152]{1,0:T(8,128)(2,1)}, bf16[128,1152]{1,0:T(8,128)(2,1)S(1)}, u32[]{:S(2)}, u32[]{:S(2)}) collective-permute-start(bf16[128,1152]{1,0:T(8,128)(2,1)} %image.1), channel_id=1, source_target_pairs={{0,2},{1,3},{2,4},{3,5},{4,6},{5,7},{6,0},{7,1},{8,10},{9,11},{10,... | collective-permute-start | bytes 884744 | tf_op jit(solution)/shard_map/ppermute | solution.py:202
  6.8 9.7 %collective-permute-start.2 = (bf16[128,1152]{1,0:T(8,128)(2,1)}, bf16[128,1152]{1,0:T(8,128)(2,1)S(1)}, u32[]{:S(2)}, u32[]{:S(2)}) collective-permute-start(bf16[128,1152]{1,0:T(8,128)(2,1)} %text.1), channel_id=1, source_target_pairs={{0,1},{1,0},{2,3},{3,2},{4,5},{5,4},{6,7},{7,6},{8,9},{9,8},{10,11... | collective-permute-start | bytes 884744 | tf_op jit(solution)/shard_map/ppermute | solution.py:206
  16.3 7.3 %collective-permute-start.6 = (bf16[128,1152]{1,0:T(8,128)(2,1)S(1)}, bf16[128,1152]{1,0:T(8,128)(2,1)S(1)}, u32[]{:S(2)}, u32[]{:S(2)}) collective-permute-start(bf16[128,1152]{1,0:T(8,128)(2,1)S(1)} %broadcast_select_fusion), channel_id=1, source_target_pairs={{0,24},{1,9},{2,26},{3,11},{4,28},{5,13},{6,30},{7,15},{8,16},{9,1... | collective-permute-start | bytes 884744 | tf_op jit(solution)/shard_map/ppermute | solution.py:202
  16.4 4.3 %collective-permute-start.7 = (bf16[128,1152]{1,0:T(8,128)(2,1)S(1)}, bf16[128,1152]{1,0:T(8,128)(2,1)S(1)}, u32[]{:S(2)}, u32[]{:S(2)}) collective-permute-start(bf16[128,1152]{1,0:T(8,128)(2,1)S(1)} %collective-permute-done.3.t1), channel_id=1, source_target_pairs={{0,1},{1,0},{2,3},{3,2},{4,5},{5,4},{6,7},{7,6},{8,9},{9,8},{10,11... | collective-permute-start | bytes 884744 | tf_op jit(solution)/shard_map/ppermute | solution.py:206
  17.8 3.0 %collective-permute-start.8 = (bf16[128,1152]{1,0:T(8,128)(2,1)S(1)}, bf16[128,1152]{1,0:T(8,128)(2,1)S(1)}, u32[]{:S(2)}, u32[]{:S(2)}) collective-permute-start(bf16[128,1152]{1,0:T(8,128)(2,1)S(1)} %collective-permute-done.4.s0), channel_id=1, source_target_pairs={{0,1},{1,0},{2,3},{3,2},{4,5},{5,4},{6,7},{7,6},{8,9},{9,8},{10,11... | collective-permute-start | bytes 884744 | tf_op jit(solution)/shard_map/ppermute | solution.py:206
  17.9 11.3 %collective-permute-start.5 = (bf16[128,1152]{1,0:T(8,128)(2,1)S(1)}, bf16[128,1152]{1,0:T(8,128)(2,1)S(1)}, u32[]{:S(2)}, u32[]{:S(2)}) collective-permute-start(bf16[128,1152]{1,0:T(8,128)(2,1)S(1)} %broadcast_select_fusion.1), channel_id=1, source_target_pairs={{0,2},{1,7},{2,4},{3,1},{4,6},{5,3},{6,0},{7,5},{8,10},{9,15},{10,... | collective-permute-start | bytes 884744 | tf_op jit(solution)/shard_map/ppermute | solution.py:202
  23.7 5.5 %collective-permute-start.9 = (bf16[128,1152]{1,0:T(8,128)(2,1)S(1)}, bf16[128,1152]{1,0:T(8,128)(2,1)S(1)}, u32[]{:S(2)}, u32[]{:S(2)}) collective-permute-start(bf16[128,1152]{1,0:T(8,128)(2,1)S(1)} %collective-permute-done.6.s1), channel_id=1, source_target_pairs={{0,1},{1,0},{2,3},{3,2},{4,5},{5,4},{6,7},{7,6},{8,9},{9,8},{10,11... | collective-permute-start | bytes 884744 | tf_op jit(solution)/shard_map/ppermute | solution.py:206
  31.5 3.3 %collective-permute-start.10 = (f32[8,128]{1,0:T(8,128)S(1)}, f32[8,128]{1,0:T(8,128)S(1)}, u32[]{:S(2)}, u32[]{:S(2)}) collective-permute-start(f32[8,128]{1,0:T(8,128)S(1)} %get-tuple-element.71), channel_id=1, source_target_pairs={{0,2},{2,0},{4,6},{6,4},{1,3},{3,1},{5,7},{7,5},{8,10},{10,8},{12,... | collective-permute-start | bytes 12296 | tf_op jit(solution)/shard_map/ppermute | solution.py:252
  35.3 4.4 %collective-permute-start.11 = (f16[896,1152]{1,0:T(8,128)(2,1)S(1)}, f16[896,1152]{1,0:T(8,128)(2,1)S(1)}, u32[]{:S(2)}, u32[]{:S(2)}) collective-permute-start(f16[896,1152]{1,0:T(8,128)(2,1)S(1)} %multiply_convert_fusion), channel_id=1, source_target_pairs={{0,1},{1,0},{2,3},{3,2},{4,5},{5,4},{6,7},{7,6},{8,9},{9,8},{10,11... | collective-permute-start | bytes 6193160 | tf_op jit(solution)/shard_map/ppermute | solution.py:206
  36.0 2.5 %collective-permute-start.12 = (f32[8,128]{1,0:T(8,128)S(1)}, f32[8,128]{1,0:T(8,128)S(1)}, u32[]{:S(2)}, u32[]{:S(2)}) collective-permute-start(f32[8,128]{1,0:T(8,128)S(1)} %add.35), channel_id=1, source_target_pairs={{0,8},{1,9},{2,10},{3,11},{4,12},{5,13},{6,14},{7,15},{8,0},{9,1},... | collective-permute-start | bytes 12296 | tf_op jit(solution)/shard_map/ppermute | solution.py:202
  39.7 5.9 %collective-permute-start.16 = (f32[8,128]{1,0:T(8,128)S(1)}, f32[8,128]{1,0:T(8,128)S(1)}, u32[]{:S(2)}, u32[]{:S(2)}) collective-permute-start(f32[8,128]{1,0:T(8,128)S(1)} %add.36), channel_id=1, source_target_pairs={{0,4},{2,6},{4,0},{6,2},{1,5},{3,7},{5,1},{7,3},{8,12},{10,14},{12... | collective-permute-start | bytes 12296 | tf_op jit(solution)/shard_map/ppermute | solution.py:265
  43.4 19.8 %collective-permute-start.15 = (f16[256,1152]{1,0:T(8,128)(2,1)S(1)}, f16[256,1152]{1,0:T(8,128)(2,1)S(1)}, u32[]{:S(2)}, u32[]{:S(2)}) collective-permute-start(f16[256,1152]{1,0:T(8,128)(2,1)S(1)} %get-tuple-element.87), channel_id=1, source_target_pairs={{0,8},{1,7},{2,10},{3,1},{4,12},{5,3},{6,14},{7,5},{8,0},{9,15},{1... | collective-permute-start | bytes 1769480 | tf_op jit(solution)/shard_map/ppermute | solution.py:202
  44.2 18.9 %collective-permute-start.14 = (f16[256,1152]{1,0:T(8,128)(2,1)S(1)}, f16[256,1152]{1,0:T(8,128)(2,1)S(1)}, u32[]{:S(2)}, u32[]{:S(2)}) collective-permute-start(f16[256,1152]{1,0:T(8,128)(2,1)S(1)} %get-tuple-element.88), channel_id=1, source_target_pairs={{0,248},{1,3},{2,250},{3,5},{4,252},{5,7},{6,254},{7,1},{8,240},{9... | collective-permute-start | bytes 1769480 | tf_op jit(solution)/shard_map/ppermute | solution.py:202
  44.9 18.2 %collective-permute-start.13 = (f16[256,1152]{1,0:T(8,128)(2,1)S(1)}, f16[256,1152]{1,0:T(8,128)(2,1)S(1)}, u32[]{:S(2)}, u32[]{:S(2)}) collective-permute-start(f16[256,1152]{1,0:T(8,128)(2,1)S(1)} %get-tuple-element.89), channel_id=1, source_target_pairs={{0,240},{1,5},{2,242},{3,7},{4,244},{5,1},{6,246},{7,3},{8,248},{9... | collective-permute-start | bytes 1769480 | tf_op jit(solution)/shard_map/ppermute | solution.py:202
  63.5 1.9 %collective-permute-start.17 = (f16[128,1152]{1,0:T(8,128)(2,1)S(1)}, f16[128,1152]{1,0:T(8,128)(2,1)S(1)}, u32[]{:S(2)}, u32[]{:S(2)}) collective-permute-start(f16[128,1152]{1,0:T(8,128)(2,1)S(1)} %multiply_convert_fusion.4), channel_id=1, source_target_pairs={{0,1},{1,0},{2,3},{3,2},{4,5},{5,4},{6,7},{7,6},{8,9},{9,8},{10,11... | collective-permute-start | bytes 884744 | tf_op jit(solution)/shard_map/ppermute | solution.py:206

commit v8 on v7

--- a/solution.py
+++ b/solution.py
@@ -155,9 +155,9 @@
     out[...] = jnp.broadcast_to(jnp.sum(loss[...], axis=0, keepdims=True), out.shape)
 
 
-def finish(scalar_ref, image, text, image_hat, text_hat, parts, image_grad, text_grad, loss):
+def finish(scalar_ref, image, text, image_inverse, image_hat, text_hat, parts, image_grad, text_grad, loss):
     for raw, hat_ref, out in ((image, image_hat, image_grad), (text, text_hat, text_grad)):
-        inverse = inverse_norm(raw[...])
+        inverse = image_inverse[pl.ds(0, ROWS), 0:1] if raw is image else inverse_norm(raw[...])
         unit = raw[...].astype(F32) * inverse
         hat = scalar_ref[0] * hat_ref[...]
         out[...] = (hat - unit * jnp.sum(unit * hat, axis=1, keepdims=True)) * inverse
@@ -278,7 +278,7 @@
     text_hat = own_text + jnp.where(first, stay, swapped)
     image_hat = own_image + jnp.where(first, swapped, stay)
     image_grad, text_grad, loss = call(
-        finish, (block, block, ((1,), F32)), 20.0, 12, scalars, image_embed, text_embed, image_hat, text_hat, loss)
+        finish, (block, block, ((1,), F32)), 20.0, 12, scalars, image_embed, text_embed, image_inverse, image_hat, text_hat, loss)
     return loss, image_grad, text_grad
 
 

time: 67.9 us -> 67.9 us (level)
  no operation moved by 1% of the time
where the time goes in v8:
time: 67.9 us; the launch traced here: 67.8 us
  starting transfers between devices  24 us (35%)
  blocking collectives  17.5 us (26%)
  Pallas kernels  11.3 us (17%)
  waiting for transfers between devices  10.8 us (16%)
  between operations  2.31 us (3%)
  other arithmetic  1.86 us (3%)
    all_to_all x1, blocking collectives, body(): loss = lax.all_to_all(loss, ('z', 'xh', 'c'), 0, 0, tiled=True)  17.5 us
    pallas_call x7, Pallas kernels, call(): pl.pallas_call(kernel, out_shape=shapes, in_specs=[SMEM if a.ndim == 1 el...  11.3 us
    ppermute x10, starting transfers between devices, move(): return lax.ppermute(block, AXES, route)  11.3 us
    ppermute x10, waiting for transfers between devices, move(): return lax.ppermute(block, AXES, route)  8.28 us
    ppermute x6, starting transfers between devices, swap_cores(): return lax.ppermute(block, 'c', [(0, 1), (1, 0)])  8.26 us
    ppermute x1, starting transfers between devices, body(): loss = loss + lax.ppermute(loss, 'y', [(i, i ^ 2) for i in range(4)])  2.92 us
    ppermute x6, waiting for transfers between devices, swap_cores(): return lax.ppermute(block, 'c', [(0, 1), (1, 0)])  2.48 us
    ppermute x1, starting transfers between devices, body(): loss_y = lax.ppermute(loss, 'y', [(i, i ^ 1) for i in range(4)])  1.56 us
  transfers between devices with their start and end apart: 18, of which 4 were waited for; matrix products, arithmetic and copies ran while one was open for 1% of the time, Pallas kernels for 10%

profile of v8, /device:TPU:1, one launch (start us, length us, event | category | flops | bytes accessed | tf_op | source)
XLA Modules:
  0.0 67.8 jit_solution(16177192602566905867)
XLA Ops:
  0.7 3.4 %collective-permute-start.4 = (bf16[128,1152]{1,0:T(8,128)(2,1)}, bf16[128,1152]{1,0:T(8,128)(2,1)S(1)}, u32[]{:S(2)}, u32[]{:S(2)}) collective-permute-start(bf16[128,1152]{1,0:T(8,128)(2,1)} %text.1), channel_id=1, source_target_pairs={{0,24},{1,25},{2,26},{3,27},{4,28},{5,29},{6,30},{7,31},{8,16},{9,... | collective-permute-start | bytes 884744 | tf_op jit(solution)/shard_map/ppermute | solution.py:202
  4.0 0.0 collective-permute-start.3
  4.0 2.7 %collective-permute-start.1 = (bf16[128,1152]{1,0:T(8,128)(2,1)}, bf16[128,1152]{1,0:T(8,128)(2,1)S(1)}, u32[]{:S(2)}, u32[]{:S(2)}) collective-permute-start(bf16[128,1152]{1,0:T(8,128)(2,1)} %image.1), channel_id=1, source_target_pairs={{0,6},{1,7},{2,0},{3,1},{4,2},{5,3},{6,4},{7,5},{8,14},{9,15},{10,... | collective-permute-start | bytes 884744 | tf_op jit(solution)/shard_map/ppermute | solution.py:202
  6.8 0.0 collective-permute-start
  6.8 1.5 %collective-permute-start.2 = (bf16[128,1152]{1,0:T(8,128)(2,1)}, bf16[128,1152]{1,0:T(8,128)(2,1)S(1)}, u32[]{:S(2)}, u32[]{:S(2)}) collective-permute-start(bf16[128,1152]{1,0:T(8,128)(2,1)} %text.1), channel_id=1, source_target_pairs={{0,1},{1,0},{2,3},{3,2},{4,5},{5,4},{6,7},{7,6},{8,9},{9,8},{10,11... | collective-permute-start | bytes 884744 | tf_op jit(solution)/shard_map/ppermute | solution.py:206
  9.6 0.1 pad_maximum_fusion.scalar_ref
  9.7 6.6 %collective-permute-done.4.s0 = bf16[128,1152]{1,0:T(8,128)(2,1)S(1)} collective-permute-done((bf16[128,1152]{1,0:T(8,128)(2,1)}, bf16[128,1152]{1,0:T(8,128)(2,1)S(1)}, u32[]{:S(2)}, u32[]{:S(2)}) %collective-permute-start.4) | collective-permute-done | bytes 294944 | tf_op jit(solution)/shard_map/ppermute | solution.py:202
  16.3 0.0 collective-permute-done.3.t1
  16.3 0.1 collective-permute-start.8
  16.4 0.0 collective-permute-done.1.ib
  16.4 0.0 collective-permute-done.ia
  16.4 0.0 collective-permute-done.2.t0x
  16.4 1.3 %collective-permute-start.5 = (bf16[128,1152]{1,0:T(8,128)(2,1)S(1)}, bf16[128,1152]{1,0:T(8,128)(2,1)S(1)}, u32[]{:S(2)}, u32[]{:S(2)}) collective-permute-start(bf16[128,1152]{1,0:T(8,128)(2,1)S(1)} %collective-permute-done.3.t1), channel_id=1, source_target_pairs={{0,1},{1,0},{2,3},{3,2},{4,5},{5,4},{6,7},{7,6},{8,9},{9,8},{10,11... | collective-permute-start | bytes 884744 | tf_op jit(solution)/shard_map/ppermute | solution.py:206
  17.8 0.1 collective-permute-start.6
  17.9 2.8 %collective-permute-start.7 = (bf16[128,1152]{1,0:T(8,128)(2,1)S(1)}, bf16[128,1152]{1,0:T(8,128)(2,1)S(1)}, u32[]{:S(2)}, u32[]{:S(2)}) collective-permute-start(bf16[128,1152]{1,0:T(8,128)(2,1)S(1)} %broadcast_select_fusion.1), channel_id=1, source_target_pairs={{0,2},{1,7},{2,4},{3,1},{4,6},{5,3},{6,0},{7,5},{8,10},{9,15},{10,... | collective-permute-start | bytes 884744 | tf_op jit(solution)/shard_map/ppermute | solution.py:202
  20.7 0.0 collective-permute-done.5.t1x
  20.7 0.0 collective-permute-done.6.s0x
  20.7 2.9 %near.1 = (bf16[384,1152]{1,0:T(8,128)(2,1)S(1)}, bf16[768,1152]{1,0:T(8,128)(2,1)S(1)}, f32[384,128]{1,0:T(8,128)S(1)}, f32[8,768]{1,0:T(8,128)S(1)}, f32[8,128...) custom-call(f32[2]{0:T(128)S(1)} %pad_maximum_fusion.scalar_ref, ...), custom_call_target="tpu_custom_call" | custom-call | flops 8000000000 | bytes 24000000 | tf_op jit(solution)/shard_map/near/pallas_call | solution.py:21
  23.7 0.0 collective-permute-done.8.s1
  23.7 4.0 %collective-permute-start.9 = (bf16[128,1152]{1,0:T(8,128)(2,1)S(1)}, bf16[128,1152]{1,0:T(8,128)(2,1)S(1)}, u32[]{:S(2)}, u32[]{:S(2)}) collective-permute-start(bf16[128,1152]{1,0:T(8,128)(2,1)S(1)} %collective-permute-done.8.s1), channel_id=1, source_target_pairs={{0,1},{1,0},{2,3},{3,2},{4,5},{5,4},{6,7},{7,6},{8,9},{9,8},{10,11... | collective-permute-start | bytes 884744 | tf_op jit(solution)/shard_map/ppermute | solution.py:206
  27.7 1.5 %near_sums.1 = (f32[128,1152]{1,0:T(8,128)S(1)}, f32[128,1152]{1,0:T(8,128)S(1)}, f32[384,1152]{1,0:T(8,128)S(1)}, f32[256,1152]{1,0:T(8,128)S(1)}) custom-call(bf16[384,768]{1,0:T(8,128)(2,1)S(1)} %get-tuple-element.65.by_text.near_by_text, bf16[384,768]{1,0:T(8,128)(2,1)S(1)} %get-tuple-element.66.by_image.near_by_image, ...), custom_call_target="tpu_custom_call" | custom-call | flops 4000000000 | bytes 12000000 | tf_op jit(solution)/shard_map/near_sums/pallas_call | solution.py:21
  29.2 0.0 collective-permute-done.7.i2
  29.2 0.0 collective-permute-done.9.sx
  29.2 2.3 %far.1 = (f32[8,128]{1,0:T(8,128)S(1)}, bf16[128,768]{1,0:T(8,128)(2,1)S(1)}, bf16[128,768]{1,0:T(8,128)(2,1)S(1)}, bf16[512,256]{1,0:T(8,128)(2,1)S(1)}, bf16[5...) custom-call(f32[2]{0:T(128)S(1)} %pad_maximum_fusion.scalar_ref, ...), custom_call_target="tpu_custom_call" | custom-call | flops 2000000000 | bytes 6000000 | tf_op jit(solution)/shard_map/far/pallas_call | solution.py:21
  31.5 1.6 %collective-permute-start.10 = (f32[8,128]{1,0:T(8,128)S(1)}, f32[8,128]{1,0:T(8,128)S(1)}, u32[]{:S(2)}, u32[]{:S(2)}) collective-permute-start(f32[8,128]{1,0:T(8,128)S(1)} %get-tuple-element.71), channel_id=1, source_target_pairs={{0,2},{2,0},{4,6},{6,4},{1,3},{3,1},{5,7},{7,5},{8,10},{10,8},{12,... | collective-permute-start | bytes 12296 | tf_op jit(solution)/shard_map/ppermute | solution.py:252
  33.1 1.7 %sums.1 = f32[1664,1152]{1,0:T(8,128)S(1)} custom-call(s32[1]{0:T(128)} %bitcast.core_ref, bf16[128,768]{1,0:T(8,128)(2,1)S(1)} %get-tuple-element.59.by_near_text, bf16[128,768]{1,0:T(8,128)(2,1)S(1)} %get-tuple-element.60.by_near_image, bf16[512,256]{1,0:T(8,128)(2,1)S(1)} %get-tuple-element.61.by_far_text, ...), custom_call_target="tpu_custom_call" | custom-call | flops 4000000000 | bytes 12000000 | tf_op jit(solution)/shard_map/sums/pallas_call | solution.py:21
  34.8 0.0 collective-permute-done.10
  34.9 0.4 multiply_convert_fusion
  35.3 0.7 %collective-permute-start.11 = (f16[896,1152]{1,0:T(8,128)(2,1)S(1)}, f16[896,1152]{1,0:T(8,128)(2,1)S(1)}, u32[]{:S(2)}, u32[]{:S(2)}) collective-permute-start(f16[896,1152]{1,0:T(8,128)(2,1)S(1)} %multiply_convert_fusion), channel_id=1, source_target_pairs={{0,1},{1,0},{2,3},{3,2},{4,5},{5,4},{6,7},{7,6},{8,9},{9,8},{10,11... | collective-permute-start | bytes 6193160 | tf_op jit(solution)/shard_map/ppermute | solution.py:206
  36.0 0.0 collective-permute-start.12
  36.0 0.8 %own_sums.1 = (f32[128,1152]{1,0:T(8,128)S(1)}, f32[128,1152]{1,0:T(8,128)S(1)}) custom-call(bf16[384,768]{1,0:T(8,128)(2,1)S(1)} %get-tuple-element.65.by_text.near_by_text, bf16[384,768]{1,0:T(8,128)(2,1)S(1)} %get-tuple-element.66.by_image.near_by_image, bf16[128,768]{1,0:T(8,128)(2,1)S(1)} %get-tuple-element.60.by_near_image, ...), custom_call_target="tpu_custom_call" | custom-call | flops 2000000000 | bytes 6000000 | tf_op jit(solution)/shard_map/own_sums/pallas_call | solution.py:21
  36.8 1.6 %collective-permute-done.12 = f32[8,128]{1,0:T(8,128)S(1)} collective-permute-done((f32[8,128]{1,0:T(8,128)S(1)}, f32[8,128]{1,0:T(8,128)S(1)}, u32[]{:S(2)}, u32[]{:S(2)}) %collective-permute-start.12) | collective-permute-done | bytes 4128 | tf_op jit(solution)/shard_map/ppermute | solution.py:202
  38.5 1.3 %collective-permute-done.11 = f16[896,1152]{1,0:T(8,128)(2,1)S(1)} collective-permute-done((f16[896,1152]{1,0:T(8,128)(2,1)S(1)}, f16[896,1152]{1,0:T(8,128)(2,1)S(1)}, u32[]{:S(2)}, u32[]{:S(2)}) %collective-permute-start.11) | collective-permute-done | bytes 2064416 | tf_op jit(solution)/shard_map/ppermute | solution.py:206
  39.7 2.9 %collective-permute-start.16 = (f32[8,128]{1,0:T(8,128)S(1)}, f32[8,128]{1,0:T(8,128)S(1)}, u32[]{:S(2)}, u32[]{:S(2)}) collective-permute-start(f32[8,128]{1,0:T(8,128)S(1)} %add.36), channel_id=1, source_target_pairs={{0,4},{2,6},{4,0},{6,2},{1,5},{3,7},{5,1},{7,3},{8,12},{10,14},{12... | collective-permute-start | bytes 12296 | tf_op jit(solution)/shard_map/ppermute | solution.py:265
  42.6 0.7 %multiply_convert_fusion.1 = (f16[256,1152]{1,0:T(8,128)(2,1)S(1)}, f16[256,1152]{1,0:T(8,128)(2,1)S(1)}, f16[256,1152]{1,0:T(8,128)(2,1)S(1)}) fusion(f32[1664,1152]{1,0:T(8,128)S(1)} %sums.1, f16[896,1152]{1,0:T(8,128)(2,1)S(1)} %collective-permute-done.11), kind=kLoop, calls=%fused_computation.2 | loop fusion | flops 4423680 | bytes 7077888 | tf_op jit(solution)/shard_map/convert_element_type | solution.py:210
  43.4 0.8 %collective-permute-start.15 = (f16[256,1152]{1,0:T(8,128)(2,1)S(1)}, f16[256,1152]{1,0:T(8,128)(2,1)S(1)}, u32[]{:S(2)}, u32[]{:S(2)}) collective-permute-start(f16[256,1152]{1,0:T(8,128)(2,1)S(1)} %get-tuple-element.87), channel_id=1, source_target_pairs={{0,8},{1,7},{2,10},{3,1},{4,12},{5,3},{6,14},{7,5},{8,0},{9,15},{1... | collective-permute-start | bytes 1769480 | tf_op jit(solution)/shard_map/ppermute | solution.py:202
  44.2 0.7 %collective-permute-start.14 = (f16[256,1152]{1,0:T(8,128)(2,1)S(1)}, f16[256,1152]{1,0:T(8,128)(2,1)S(1)}, u32[]{:S(2)}, u32[]{:S(2)}) collective-permute-start(f16[256,1152]{1,0:T(8,128)(2,1)S(1)} %get-tuple-element.88), channel_id=1, source_target_pairs={{0,248},{1,3},{2,250},{3,5},{4,252},{5,7},{6,254},{7,1},{8,240},{9... | collective-permute-start | bytes 1769480 | tf_op jit(solution)/shard_map/ppermute | solution.py:202
  44.9 0.7 %collective-permute-start.13 = (f16[256,1152]{1,0:T(8,128)(2,1)S(1)}, f16[256,1152]{1,0:T(8,128)(2,1)S(1)}, u32[]{:S(2)}, u32[]{:S(2)}) collective-permute-start(f16[256,1152]{1,0:T(8,128)(2,1)S(1)} %get-tuple-element.89), channel_id=1, source_target_pairs={{0,240},{1,5},{2,242},{3,7},{4,244},{5,1},{6,246},{7,3},{8,248},{9... | collective-permute-start | bytes 1769480 | tf_op jit(solution)/shard_map/ppermute | solution.py:202
  45.7 0.0 collective-permute-done.16
  45.7 17.5 %all_to_all.12 = f32[32,1,128]{2,1,0:T(1,128)S(1)} all-to-all(f32[32,1,128]{2,1,0:T(1,128)S(1)} %bitcast.6), channel_id=1, replica_groups=mesh['z'=8,'xh'=2,'xl'=2,'y'=4,'c'=2] {'z','xh','c'}, dimensions={0} | all-to-all | bytes 32768 | tf_op jit(solution)/shard_map/all_to_all | solution.py:273
  63.2 0.0 collective-permute-done.15
  63.2 0.0 collective-permute-done.13
  63.2 0.2 add_multiply_fusion
  63.4 0.1 multiply_convert_fusion.4
  63.5 0.7 %collective-permute-start.17 = (f16[128,1152]{1,0:T(8,128)(2,1)S(1)}, f16[128,1152]{1,0:T(8,128)(2,1)S(1)}, u32[]{:S(2)}, u32[]{:S(2)}) collective-permute-start(f16[128,1152]{1,0:T(8,128)(2,1)S(1)} %multiply_convert_fusion.4), channel_id=1, source_target_pairs={{0,1},{1,0},{2,3},{3,2},{4,5},{5,4},{6,7},{7,6},{8,9},{9,8},{10,11... | collective-permute-start | bytes 884744 | tf_op jit(solution)/shard_map/ppermute | solution.py:206
  64.2 1.2 %collective-permute-done.17 = f16[128,1152]{1,0:T(8,128)(2,1)S(1)} collective-permute-done((f16[128,1152]{1,0:T(8,128)(2,1)S(1)}, f16[128,1152]{1,0:T(8,128)(2,1)S(1)}, u32[]{:S(2)}, u32[]{:S(2)}) %collective-permute-start.17) | collective-permute-done | bytes 294944 | tf_op jit(solution)/shard_map/ppermute | solution.py:206
  65.4 0.2 select_add_fusion
  65.6 2.0 %finish.1 = (f32[128,1152]{1,0:T(8,128)}, f32[128,1152]{1,0:T(8,128)}, f32[1]{0:T(128)}) custom-call(f32[2]{0:T(128)S(1)} %pad_maximum_fusion.scalar_ref, bf16[128,1152]{1,0:T(8,128)(2,1)S(1)} %copy-done, bf16[128,1152]{1,0:T(8,128)(2,1)S(1)} %copy-done.1, f32[384,128]{1,0:T(8,128)S(1)} %get-tuple-element.52.image_inverse, ...), custom_call_target="tpu_custom_call" | custom-call | flops 20000000000 | bytes 60000000 | tf_op jit(solution)/shard_map/finish/pallas_call | solution.py:21
  (11 shorter events, 0.1 us)
Async XLA Ops:
  0.6 20.1 %copy-start.1 = (bf16[128,1152]{1,0:T(8,128)(2,1)S(1)}, bf16[128,1152]{1,0:T(8,128)(2,1)}, u32[]{:S(2)}) copy-start(bf16[128,1152]{1,0:T(8,128)(2,1)} %text.1) | copy-start | bytes 884740
  0.6 20.1 %copy-start = (bf16[128,1152]{1,0:T(8,128)(2,1)S(1)}, bf16[128,1152]{1,0:T(8,128)(2,1)}, u32[]{:S(2)}) copy-start(bf16[128,1152]{1,0:T(8,128)(2,1)} %image.1) | copy-start | bytes 884740
  0.7 15.6 %collective-permute-start.4 = (bf16[128,1152]{1,0:T(8,128)(2,1)}, bf16[128,1152]{1,0:T(8,128)(2,1)S(1)}, u32[]{:S(2)}, u32[]{:S(2)}) collective-permute-start(bf16[128,1152]{1,0:T(8,128)(2,1)} %text.1), channel_id=1, source_target_pairs={{0,24},{1,25},{2,26},{3,27},{4,28},{5,29},{6,30},{7,31},{8,16},{9,... | collective-permute-start | bytes 884744 | tf_op jit(solution)/shard_map/ppermute | solution.py:202
  4.0 12.2 %collective-permute-start.3 = (bf16[128,1152]{1,0:T(8,128)(2,1)}, bf16[128,1152]{1,0:T(8,128)(2,1)S(1)}, u32[]{:S(2)}, u32[]{:S(2)}) collective-permute-start(bf16[128,1152]{1,0:T(8,128)(2,1)} %text.1), channel_id=1, source_target_pairs={{0,8},{1,9},{2,10},{3,11},{4,12},{5,13},{6,14},{7,15},{8,0},{9,1},... | collective-permute-start | bytes 884744 | tf_op jit(solution)/shard_map/ppermute | solution.py:202
  4.0 12.4 %collective-permute-start.1 = (bf16[128,1152]{1,0:T(8,128)(2,1)}, bf16[128,1152]{1,0:T(8,128)(2,1)S(1)}, u32[]{:S(2)}, u32[]{:S(2)}) collective-permute-start(bf16[128,1152]{1,0:T(8,128)(2,1)} %image.1), channel_id=1, source_target_pairs={{0,6},{1,7},{2,0},{3,1},{4,2},{5,3},{6,4},{7,5},{8,14},{9,15},{10,... | collective-permute-start | bytes 884744 | tf_op jit(solution)/shard_map/ppermute | solution.py:202
  6.8 9.6 %collective-permute-start = (bf16[128,1152]{1,0:T(8,128)(2,1)}, bf16[128,1152]{1,0:T(8,128)(2,1)S(1)}, u32[]{:S(2)}, u32[]{:S(2)}) collective-permute-start(bf16[128,1152]{1,0:T(8,128)(2,1)} %image.1), channel_id=1, source_target_pairs={{0,2},{1,3},{2,4},{3,5},{4,6},{5,7},{6,0},{7,1},{8,10},{9,11},{10,... | collective-permute-start | bytes 884744 | tf_op jit(solution)/shard_map/ppermute | solution.py:202
  6.8 9.7 %collective-permute-start.2 = (bf16[128,1152]{1,0:T(8,128)(2,1)}, bf16[128,1152]{1,0:T(8,128)(2,1)S(1)}, u32[]{:S(2)}, u32[]{:S(2)}) collective-permute-start(bf16[128,1152]{1,0:T(8,128)(2,1)} %text.1), channel_id=1, source_target_pairs={{0,1},{1,0},{2,3},{3,2},{4,5},{5,4},{6,7},{7,6},{8,9},{9,8},{10,11... | collective-permute-start | bytes 884744 | tf_op jit(solution)/shard_map/ppermute | solution.py:206
  16.3 7.3 %collective-permute-start.8 = (bf16[128,1152]{1,0:T(8,128)(2,1)S(1)}, bf16[128,1152]{1,0:T(8,128)(2,1)S(1)}, u32[]{:S(2)}, u32[]{:S(2)}) collective-permute-start(bf16[128,1152]{1,0:T(8,128)(2,1)S(1)} %broadcast_select_fusion), channel_id=1, source_target_pairs={{0,24},{1,9},{2,26},{3,11},{4,28},{5,13},{6,30},{7,15},{8,16},{9,1... | collective-permute-start | bytes 884744 | tf_op jit(solution)/shard_map/ppermute | solution.py:202
  16.4 4.3 %collective-permute-start.5 = (bf16[128,1152]{1,0:T(8,128)(2,1)S(1)}, bf16[128,1152]{1,0:T(8,128)(2,1)S(1)}, u32[]{:S(2)}, u32[]{:S(2)}) collective-permute-start(bf16[128,1152]{1,0:T(8,128)(2,1)S(1)} %collective-permute-done.3.t1), channel_id=1, source_target_pairs={{0,1},{1,0},{2,3},{3,2},{4,5},{5,4},{6,7},{7,6},{8,9},{9,8},{10,11... | collective-permute-start | bytes 884744 | tf_op jit(solution)/shard_map/ppermute | solution.py:206
  17.8 3.0 %collective-permute-start.6 = (bf16[128,1152]{1,0:T(8,128)(2,1)S(1)}, bf16[128,1152]{1,0:T(8,128)(2,1)S(1)}, u32[]{:S(2)}, u32[]{:S(2)}) collective-permute-start(bf16[128,1152]{1,0:T(8,128)(2,1)S(1)} %collective-permute-done.4.s0), channel_id=1, source_target_pairs={{0,1},{1,0},{2,3},{3,2},{4,5},{5,4},{6,7},{7,6},{8,9},{9,8},{10,11... | collective-permute-start | bytes 884744 | tf_op jit(solution)/shard_map/ppermute | solution.py:206
  17.9 11.3 %collective-permute-start.7 = (bf16[128,1152]{1,0:T(8,128)(2,1)S(1)}, bf16[128,1152]{1,0:T(8,128)(2,1)S(1)}, u32[]{:S(2)}, u32[]{:S(2)}) collective-permute-start(bf16[128,1152]{1,0:T(8,128)(2,1)S(1)} %broadcast_select_fusion.1), channel_id=1, source_target_pairs={{0,2},{1,7},{2,4},{3,1},{4,6},{5,3},{6,0},{7,5},{8,10},{9,15},{10,... | collective-permute-start | bytes 884744 | tf_op jit(solution)/shard_map/ppermute | solution.py:202
  23.7 5.5 %collective-permute-start.9 = (bf16[128,1152]{1,0:T(8,128)(2,1)S(1)}, bf16[128,1152]{1,0:T(8,128)(2,1)S(1)}, u32[]{:S(2)}, u32[]{:S(2)}) collective-permute-start(bf16[128,1152]{1,0:T(8,128)(2,1)S(1)} %collective-permute-done.8.s1), channel_id=1, source_target_pairs={{0,1},{1,0},{2,3},{3,2},{4,5},{5,4},{6,7},{7,6},{8,9},{9,8},{10,11... | collective-permute-start | bytes 884744 | tf_op jit(solution)/shard_map/ppermute | solution.py:206
  31.5 3.3 %collective-permute-start.10 = (f32[8,128]{1,0:T(8,128)S(1)}, f32[8,128]{1,0:T(8,128)S(1)}, u32[]{:S(2)}, u32[]{:S(2)}) collective-permute-start(f32[8,128]{1,0:T(8,128)S(1)} %get-tuple-element.71), channel_id=1, source_target_pairs={{0,2},{2,0},{4,6},{6,4},{1,3},{3,1},{5,7},{7,5},{8,10},{10,8},{12,... | collective-permute-start | bytes 12296 | tf_op jit(solution)/shard_map/ppermute | solution.py:252
  35.3 4.4 %collective-permute-start.11 = (f16[896,1152]{1,0:T(8,128)(2,1)S(1)}, f16[896,1152]{1,0:T(8,128)(2,1)S(1)}, u32[]{:S(2)}, u32[]{:S(2)}) collective-permute-start(f16[896,1152]{1,0:T(8,128)(2,1)S(1)} %multiply_convert_fusion), channel_id=1, source_target_pairs={{0,1},{1,0},{2,3},{3,2},{4,5},{5,4},{6,7},{7,6},{8,9},{9,8},{10,11... | collective-permute-start | bytes 6193160 | tf_op jit(solution)/shard_map/ppermute | solution.py:206
  36.0 2.5 %collective-permute-start.12 = (f32[8,128]{1,0:T(8,128)S(1)}, f32[8,128]{1,0:T(8,128)S(1)}, u32[]{:S(2)}, u32[]{:S(2)}) collective-permute-start(f32[8,128]{1,0:T(8,128)S(1)} %add.35), channel_id=1, source_target_pairs={{0,8},{1,9},{2,10},{3,11},{4,12},{5,13},{6,14},{7,15},{8,0},{9,1},... | collective-permute-start | bytes 12296 | tf_op jit(solution)/shard_map/ppermute | solution.py:202
  39.7 5.9 %collective-permute-start.16 = (f32[8,128]{1,0:T(8,128)S(1)}, f32[8,128]{1,0:T(8,128)S(1)}, u32[]{:S(2)}, u32[]{:S(2)}) collective-permute-start(f32[8,128]{1,0:T(8,128)S(1)} %add.36), channel_id=1, source_target_pairs={{0,4},{2,6},{4,0},{6,2},{1,5},{3,7},{5,1},{7,3},{8,12},{10,14},{12... | collective-permute-start | bytes 12296 | tf_op jit(solution)/shard_map/ppermute | solution.py:265
  43.4 19.8 %collective-permute-start.15 = (f16[256,1152]{1,0:T(8,128)(2,1)S(1)}, f16[256,1152]{1,0:T(8,128)(2,1)S(1)}, u32[]{:S(2)}, u32[]{:S(2)}) collective-permute-start(f16[256,1152]{1,0:T(8,128)(2,1)S(1)} %get-tuple-element.87), channel_id=1, source_target_pairs={{0,8},{1,7},{2,10},{3,1},{4,12},{5,3},{6,14},{7,5},{8,0},{9,15},{1... | collective-permute-start | bytes 1769480 | tf_op jit(solution)/shard_map/ppermute | solution.py:202
  44.2 18.9 %collective-permute-start.14 = (f16[256,1152]{1,0:T(8,128)(2,1)S(1)}, f16[256,1152]{1,0:T(8,128)(2,1)S(1)}, u32[]{:S(2)}, u32[]{:S(2)}) collective-permute-start(f16[256,1152]{1,0:T(8,128)(2,1)S(1)} %get-tuple-element.88), channel_id=1, source_target_pairs={{0,248},{1,3},{2,250},{3,5},{4,252},{5,7},{6,254},{7,1},{8,240},{9... | collective-permute-start | bytes 1769480 | tf_op jit(solution)/shard_map/ppermute | solution.py:202
  44.9 18.2 %collective-permute-start.13 = (f16[256,1152]{1,0:T(8,128)(2,1)S(1)}, f16[256,1152]{1,0:T(8,128)(2,1)S(1)}, u32[]{:S(2)}, u32[]{:S(2)}) collective-permute-start(f16[256,1152]{1,0:T(8,128)(2,1)S(1)} %get-tuple-element.89), channel_id=1, source_target_pairs={{0,240},{1,5},{2,242},{3,7},{4,244},{5,1},{6,246},{7,3},{8,248},{9... | collective-permute-start | bytes 1769480 | tf_op jit(solution)/shard_map/ppermute | solution.py:202
  63.5 1.9 %collective-permute-start.17 = (f16[128,1152]{1,0:T(8,128)(2,1)S(1)}, f16[128,1152]{1,0:T(8,128)(2,1)S(1)}, u32[]{:S(2)}, u32[]{:S(2)}) collective-permute-start(f16[128,1152]{1,0:T(8,128)(2,1)S(1)} %multiply_convert_fusion.4), channel_id=1, source_target_pairs={{0,1},{1,0},{2,3},{3,2},{4,5},{5,4},{6,7},{7,6},{8,9},{9,8},{10,11... | collective-permute-start | bytes 884744 | tf_op jit(solution)/shard_map/ppermute | solution.py:206
